TPU v7x, 256 devices: a whole 4x4x8 slice. The times are simulated.
256 devices in a mesh: fsdp: 32 (over y, z), rep: 8 (over x, core).
Axes of the slice: x: 4, y: 4, z: 8, core: 2. Of those that a mesh axis runs over, the one named last changes fastest.
Arguments:
- gradient: float32 [8, 4096, 6656], P('rep', 'fsdp')
- second_moment: float32 [4096, 6656], P('fsdp'), may hold values from 0.0001 to 0.1
- owner_cols: int32 [8, 1, 32], replicated, may hold values from -1 to 12, as said below
- stat_left: float32 [32, 1, 8, 512, 512], P('fsdp', None, None, 'rep'), as said below
- stat_right: float32 [32, 1, 8, 512, 512], P('fsdp', None, None, 'rep'), as said below
- root_left: float32 [32, 1, 8, 512, 512], P('fsdp', None, None, 'rep'), as said below
- root_right: float32 [32, 1, 8, 512, 512], P('fsdp', None, None, 'rep'), as said below
Outputs:
- direction: float32 [4096, 6656], P('fsdp')
- moment_new: float32 [4096, 6656], P('fsdp')
- left_new: float32 [32, 1, 8, 512, 512], P('fsdp', None, None, 'rep')
- right_new: float32 [32, 1, 8, 512, 512], P('fsdp', None, None, 'rep')
Inputs may be any that keep to these rules, and one draw needn't show every extreme that they name: owner_cols[b, k, o] is the column block of block row b kept in slot k of owner o, or -1 for an empty slot; every column block of every block row is kept in exactly one slot. `stat_left`: each block is symmetric. `stat_right`: each block is symmetric. `root_left`: each block is symmetric. `root_right`: each block is symmetric.
All inputs are finite; a program needn't handle non-finite values.
Results may differ from a plain program's by a relative error of at most 0.000071.
Values sent between devices are 32-bit elements; how exact they have to be, the bound alone decides.
No kernel may reach another device: no remote copies, remote signals or barrier semaphores. Data moves between devices by JAX's collectives and lax.ppermute only.
A program may use at most 128 MiB of HBM per device.

v0:
```python
import jax
import jax.numpy as jnp
from jax import lax
from jax.sharding import PartitionSpec as P

SHAMPOO_DECAY = 0.9
ADAM_DECAY = 0.95
ADAM_EPS = 1e-08
NORM_EPS = 1e-06
HIGHEST = lax.Precision.HIGHEST


def place_row(values, row_count, my_row):
    rows_here = jnp.arange(row_count, dtype=jnp.int32)[:, None] == my_row
    return jnp.where(rows_here, values[None, :], 0.0)


def pack_blocks(pieces, cols_here):
    chosen = jnp.take(pieces, jnp.maximum(cols_here, 0), axis=0)
    return jnp.where((cols_here >= 0)[:, :, None, None], chosen, 0.0)


def shards(gradient, second_moment, owner_cols, stat_left, stat_right, root_left, root_right):
    shard_rows = gradient.shape[1]
    full_width = gradient.shape[2]
    block_size = stat_left.shape[-1]
    block_rows = owner_cols.shape[0]
    slot_count = owner_cols.shape[1]
    owner_count = lax.axis_size("fsdp")
    replicas = lax.axis_size("rep")
    col_blocks = full_width // block_size
    rep_share = block_size // replicas
    my_block_row = lax.axis_index("fsdp") // (block_size // shard_rows)
    rep_start = lax.axis_index("rep") * rep_share
    summed = lax.psum(gradient[0], "rep")
    averaged = summed / replicas
    moment_new = ADAM_DECAY * second_moment + (1.0 - ADAM_DECAY) * averaged * averaged
    adam_step = averaged / (jnp.sqrt(moment_new) + ADAM_EPS)
    adam_squares = jnp.sum(
        jnp.square(adam_step).reshape(shard_rows, col_blocks, block_size), axis=(0, 2)
    )
    adam_total = lax.psum(place_row(adam_squares, block_rows, my_block_row), "fsdp")
    cols_here = lax.dynamic_index_in_dim(owner_cols, my_block_row, 0, keepdims=False)
    pieces = averaged.reshape(shard_rows, col_blocks, block_size).transpose(1, 0, 2)
    arrived = lax.all_to_all(
        pack_blocks(pieces, cols_here), "fsdp", split_axis=1, concat_axis=1, tiled=True
    )
    owned_blocks = arrived.reshape(slot_count, block_rows, block_size, block_size)
    grad_rows = lax.dynamic_slice_in_dim(owned_blocks, rep_start, rep_share, 2)
    grad_cols = lax.dynamic_slice_in_dim(owned_blocks, rep_start, rep_share, 3)
    left_gram = jnp.einsum("kbij,kblj->kbil", grad_rows, owned_blocks, precision=HIGHEST)
    right_gram = jnp.einsum("kbji,kbjl->kbil", grad_cols, owned_blocks, precision=HIGHEST)
    left_new = SHAMPOO_DECAY * stat_left[0] + (1.0 - SHAMPOO_DECAY) * left_gram
    right_new = SHAMPOO_DECAY * stat_right[0] + (1.0 - SHAMPOO_DECAY) * right_gram
    left_whole = lax.all_gather(root_left[0], "rep", axis=2, tiled=True)
    right_part = jnp.einsum("kbij,kblj->kbil", owned_blocks, root_right[0], precision=HIGHEST)
    applied = jnp.einsum("kbij,kbjl->kbil", left_whole, right_part, precision=HIGHEST)
    whole_applied = lax.all_gather(applied, "rep", axis=3, tiled=True)
    returned = lax.all_to_all(
        whole_applied.reshape(slot_count, owner_count, shard_rows, block_size),
        "fsdp",
        split_axis=1,
        concat_axis=1,
        tiled=True,
    )
    matches = cols_here[None, :, :] == jnp.arange(col_blocks, dtype=jnp.int32)[:, None, None]
    source = jnp.argmax(matches.reshape(col_blocks, slot_count * owner_count), axis=1)
    shampoo = jnp.take(
        returned.reshape(slot_count * owner_count, shard_rows, block_size), source, axis=0
    )
    shampoo_squares = jnp.sum(jnp.square(shampoo), axis=(1, 2))
    shampoo_total = lax.psum(place_row(shampoo_squares, block_rows, my_block_row), "fsdp")
    adam_here = lax.dynamic_index_in_dim(adam_total, my_block_row, 0, keepdims=False)
    shampoo_here = lax.dynamic_index_in_dim(shampoo_total, my_block_row, 0, keepdims=False)
    graft_scale = jnp.sqrt(adam_here) / (jnp.sqrt(shampoo_here) + NORM_EPS)
    direction = (
        (shampoo * graft_scale[:, None, None]).transpose(1, 0, 2).reshape(shard_rows, full_width)
    )
    return (direction, moment_new, left_new[None], right_new[None])


def solution(mesh):
    return jax.shard_map(
        shards,
        mesh=mesh,
        in_specs=(
            P("rep", "fsdp", None),
            P("fsdp", None),
            P(),
            P("fsdp", None, None, "rep", None),
            P("fsdp", None, None, "rep", None),
            P("fsdp", None, None, "rep", None),
            P("fsdp", None, None, "rep", None),
        ),
        out_specs=(
            P("fsdp", None),
            P("fsdp", None),
            P("fsdp", None, None, "rep", None),
            P("fsdp", None, None, "rep", None),
        ),
        check_vma=False,
    )
```

profile of v0, /device:TPU:1, one launch (start us, length us, event | category | flops | bytes accessed | tf_op | source)
XLA Modules:
  0.0 703.6 jit_solution(14004019180855692304)
XLA Ops:
  7.2 5.1 copy.30
  12.3 5.0 copy.35
  18.6 70.8 %all-reduce.3.cloned.1.call-done = f32[128,6656]{0,1:T(8,128)} async-done(((f32[128,6656]{0,1:T(8,128)}), f32[128,6656]{0,1:T(8,128)}) %all-reduce.3.cloned.1.call-update) | async-done | bytes 3407888 | tf_op jit(solution)/shard_map/psum | solution.py:35
  89.4 7.8 %multiply_add_fusion = (f32[128,6656]{0,1:T(8,128)}, f32[6656]{0:T(1024)S(1)}, f32[128,6656]{0,1:T(8,128)}) fusion(f32[128,6656]{0,1:T(8,128)} %all-reduce.3.cloned.1.call-done, f32[128,6656]{0,1:T(8,128)} %copy.35), kind=kLoop, calls=%fused_computation.10 | loop fusion | flops 7661056 | bytes 13658112 | tf_op jit(solution)/shard_map/add | solution.py:37
  97.2 4.7 copy.31
  101.9 6.3 gather_fusion
  108.2 8.5 %fusion.3 = f32[1,32,128,512]{3,2,0,1:T(8,128)} fusion(f32[32,128,512]{2,1,0:T(8,128)} %gather_fusion, pred[32]{0:T(512)(128)(4,1)S(1)} %maximum_compare_fusion, pred[32]{0:T(512)(128)(4,1)S(1)} %get-tuple-element.20), kind=kLoop, calls=%fused_computation.6 | loop fusion | flops 4194304 | bytes 16777280 | tf_op jit(solution)/shard_map/jit(_where)/select_n | solution.py:20
  116.7 9.7 %all-to-all-start = ((f32[1,32,128,512]{3,2,0,1:T(8,128)}), f32[1,32,128,512]{3,2,0,1:T(8,128)}, u32[]{:S(2)}, u32[]{:S(2)}) async-start(f32[1,32,128,512]{3,2,0,1:T(8,128)} %fusion.3), calls=%async_computation | async-start | bytes 16777216 | tf_op jit(solution)/shard_map/all_to_all | solution.py:45
  127.4 182.1 %all-to-all-done = f32[1,32,128,512]{3,2,0,1:T(8,128)} async-done(((f32[1,32,128,512]{3,2,0,1:T(8,128)}), f32[1,32,128,512]{3,2,0,1:T(8,128)}, u32[]{:S(2)}, u32[]{:S(2)}) %all-to-all-start) | async-done | bytes 8388640 | tf_op jit(solution)/shard_map/all_to_all | solution.py:45
  309.5 10.5 %fusion.22 = f32[8,512,64]{1,2,0:T(8,128)S(1)} fusion(f32[8,512,512]{2,1,0:T(8,128)} %bitcast.7, f32[1,1,8,64,512]{4,3,2,1,0:T(8,128)S(1)} %copy-done), kind=kOutput, calls=%fused_computation.23 | convolution fusion | flops 1610612736 | bytes 10485760 | tf_op jit(solution)/shard_map/kbij,kblj->kbil/dot_general | solution.py:56
  320.0 11.4 %fusion.10 = f32[8,512,64]{1,2,0:T(8,128)} fusion(f32[8,512,64]{1,2,0:T(8,128)S(1)} %fusion.22, f32[1,1,8,512,512]{4,3,2,1,0:T(8,128)} %all-gather.5.cloned.1.call-done), kind=kOutput, calls=%fused_computation.16 | convolution fusion | flops 1610612736 | bytes 10485760 | tf_op jit(solution)/shard_map/kbij,kbjl->kbil/dot_general | solution.py:57
  331.5 68.0 %all-gather.7.cloned.1.call-done = f32[8,512,512]{1,2,0:T(8,128)} async-done(((f32[8,512,64]{1,2,0:T(8,128)}), f32[8,512,512]{1,2,0:T(8,128)}) %all-gather.7.cloned.1.call-update) | async-done | bytes 8388624 | tf_op jit(solution)/shard_map/all_gather | solution.py:58
  399.4 9.1 %copy.33 = f32[8,512,512]{2,1,0:T(8,128)} copy(f32[8,512,512]{1,2,0:T(8,128)} %all-gather.7.cloned.1.call-done) | data formatting | bytes 16777216 | tf_op jit(solution)/shard_map/all_gather | solution.py:58
  408.6 9.7 %all-to-all-start.1 = ((f32[1,32,128,512]{3,2,0,1:T(8,128)}), f32[1,32,128,512]{3,2,0,1:T(8,128)}, u32[]{:S(2)}, u32[]{:S(2)}) async-start(f32[1,32,128,512]{3,2,0,1:T(8,128)} %bitcast.63), calls=%async_computation.1 | async-start | bytes 16777216 | tf_op jit(solution)/shard_map/all_to_all | solution.py:59
  419.0 5.1 copy.39
  424.2 10.2 %fusion.16 = f32[1,1,8,64,512]{4,3,2,1,0:T(8,128)} fusion(f32[8,512,512]{2,1,0:T(8,128)} %bitcast.7, f32[1,8,512,512]{3,2,1,0:T(8,128)} %bitcast.18, s32[]{:T(128)S(6)} %select_n.73, f32[1,1,8,64,512]{4,3,2,1,0:T(8,128)S(1)} %copy-done.2), kind=kOutput, calls=%fused_computation.18 | convolution fusion | flops 1611399168 | bytes 12582916 | tf_op jit(solution)/shard_map/kbji,kbjl->kbil/dot_general | solution.py:52
  434.4 12.8 %fusion.20 = f32[1,1,8,64,512]{4,3,2,1,0:T(8,128)} fusion(f32[8,512,512]{2,1,0:T(8,128)} %bitcast.7, f32[1,8,512,512]{3,2,1,0:T(8,128)} %bitcast.18, s32[]{:T(128)S(6)} %select_n.73, f32[1,1,8,64,512]{4,3,2,1,0:T(8,128)S(1)} %copy-done.3), kind=kOutput, calls=%fused_computation.21 | convolution fusion | flops 1611399168 | bytes 11534340 | tf_op jit(solution)/shard_map/kbij,kblj->kbil/dot_general | solution.py:51
  447.2 160.7 %all-to-all-done.1 = f32[1,32,128,512]{3,2,0,1:T(8,128)} async-done(((f32[1,32,128,512]{3,2,0,1:T(8,128)}), f32[1,32,128,512]{3,2,0,1:T(8,128)}, u32[]{:S(2)}, u32[]{:S(2)}) %all-to-all-start.1) | async-done | bytes 8388640 | tf_op jit(solution)/shard_map/all_to_all | solution.py:59
  607.8 5.9 gather_fusion.1
  613.7 2.5 multiply_reduce_fusion
  616.3 66.7 %all-reduce = (f32[8,13]{1,0:T(8,128)S(1)}, f32[8,13]{1,0:T(8,128)S(1)}) all-reduce(f32[8,13]{1,0:T(8,128)S(1)} %get-tuple-element.26, f32[8,13]{1,0:T(8,128)S(1)} %get-tuple-element.25), channel_id=1, replica_groups=mesh['fsdp'=32,'rep'=8] {'fsdp'}, use_global_device_ids=true, to_apply=%region_6.7 | all-reduce | flops 208 | bytes 1664 | tf_op jit(solution)/shard_map/psum | solution.py:72
  683.0 4.3 multiply_bitcast_fusion
  687.3 4.7 copy.36
  692.0 5.1 copy.38
  (28 shorter events, 3.3 us)
Async XLA Ops:
  7.2 302.4 %copy-start = (f32[1,1,8,64,512]{4,3,2,1,0:T(8,128)S(1)}, f32[1,1,8,64,512]{4,3,2,1,0:T(8,128)}, u32[]{:S(2)}) copy-start(f32[1,1,8,64,512]{4,3,2,1,0:T(8,128)} %param.13) | copy-start | bytes 3145732
  7.2 82.2 %all-reduce.3.cloned.1.call-start = ((), (), s32[]{:S(2)}) async-start(), calls=%async_computation.2 | async-start | bytes 6815744 | tf_op jit(solution)/shard_map/psum | solution.py:35
  116.7 192.8 %all-to-all-start = ((f32[1,32,128,512]{3,2,0,1:T(8,128)}), f32[1,32,128,512]{3,2,0,1:T(8,128)}, u32[]{:S(2)}, u32[]{:S(2)}) async-start(f32[1,32,128,512]{3,2,0,1:T(8,128)} %fusion.3), calls=%async_computation | async-start | bytes 16777216 | tf_op jit(solution)/shard_map/all_to_all | solution.py:45
  126.4 193.6 %all-gather.5.cloned.1.call-start = ((), (), s32[]{:S(2)}) async-start(), calls=%async_computation.3 | async-start | bytes 9437184 | tf_op jit(solution)/shard_map/all_gather | solution.py:55
  127.2 272.3 %all-gather.7.cloned.1.call-start = ((), (), s32[]{:S(2)}) async-start(), calls=%async_computation.4 | async-start | bytes 9437184 | tf_op jit(solution)/shard_map/all_gather | solution.py:58
  408.6 199.3 %all-to-all-start.1 = ((f32[1,32,128,512]{3,2,0,1:T(8,128)}), f32[1,32,128,512]{3,2,0,1:T(8,128)}, u32[]{:S(2)}, u32[]{:S(2)}) async-start(f32[1,32,128,512]{3,2,0,1:T(8,128)} %bitcast.63), calls=%async_computation.1 | async-start | bytes 16777216 | tf_op jit(solution)/shard_map/all_to_all | solution.py:59
  419.0 5.2 copy-start.2
  424.2 10.2 %copy-start.3 = (f32[1,1,8,64,512]{4,3,2,1,0:T(8,128)S(1)}, f32[1,1,8,64,512]{4,3,2,1,0:T(8,128)}, u32[]{:S(2)}) copy-start(f32[1,1,8,64,512]{4,3,2,1,0:T(8,128)} %param.10) | copy-start | bytes 3145732
  692.0 5.1 copy-start.1
Sparse Core Ops, SparseCore 0:
  12.4 76.9 all-reduce.2
  129.1 53.9 all-gather.4
  331.6 67.8 all-gather.6
where the time goes:
time: 717 us; the launch traced here: 704 us
  waiting for transfers between devices  482 us (67%)
  blocking collectives  66.7 us (9%)
  local copies, waits for them, and re-layouts  51 us (7%)
  matrix products  44.9 us (6%)
  other arithmetic  25.2 us (4%)
  starting transfers between devices  19.7 us (3%)
  between operations  13.9 us (2%)
    all_to_all x1, waiting for transfers between devices, shards(): lax.all_to_all(pack_blocks(pieces, cols_here), 'fsdp', split_axis=1, conc...  182 us
    all_to_all x1, waiting for transfers between devices, shards(): lax.all_to_all(whole_applied.reshape(slot_count, owner_count, shard_rows,...  161 us
    psum x1, waiting for transfers between devices, shards(): summed = lax.psum(gradient[0], 'rep')  70.8 us
    all_gather x1, waiting for transfers between devices, shards(): whole_applied = lax.all_gather(applied, 'rep', axis=3, tiled=True)  68 us
    psum x1, blocking collectives, shards(): lax.psum(place_row(shampoo_squares, block_rows, my_block_row), 'fsdp')  66.7 us
    unnamed x12, local copies, waits for them, and re-layouts  20.2 us
  transfers between devices with their start and end apart: 5, of which 4 were waited for; matrix products, arithmetic and copies ran while one was open for 6% of the time, Pallas kernels for 0%

commit v1 on v0

v1 whole, which is shorter than its diff:
```python
import functools

import jax
import jax.numpy as jnp
from jax import lax
from jax.experimental import pallas as pl
from jax.experimental.pallas import tpu as pltpu
from jax.sharding import PartitionSpec as P

SHAMPOO_DECAY = 0.9
ADAM_DECAY = 0.95
ADAM_EPS = 1e-08
NORM_EPS = 1e-06
PARAMS = pltpu.CompilerParams(vmem_limit_bytes=32 * 1024 * 1024)
F32 = jnp.float32
BF16 = jnp.bfloat16


def rep_shift(value, step, count):
    return lax.ppermute(value, "rep", [(i, (i + step) % count) for i in range(count)])


def pick(array, index, axis=0):
    return lax.dynamic_index_in_dim(array, index, axis, keepdims=False)


def split(value):
    high = value.astype(BF16)
    return high, (value - high.astype(F32)).astype(BF16)


def dot3(a, b, dims):
    dot = functools.partial(
        lax.dot_general, dimension_numbers=(dims, ((), ())), preferred_element_type=F32
    )
    return dot(a[0], b[0]) + (dot(a[0], b[1]) + dot(a[1], b[0]))


def moment_kernel(cols, replicas, ids, owner_cols, *refs):
    parts, second = refs[:4], refs[4]
    moment, squares, packed, averaged = refs[5:]
    row = ids[1]
    width = packed.shape[-1]
    squares[...] = jnp.zeros_like(squares)
    for c in range(cols):
        here = slice(c * width, (c + 1) * width)
        summed = (parts[0][:, here] + parts[1][:, here]) + (parts[2][:, here] + parts[3][:, here])
        mean = summed / replicas
        averaged[:, here] = mean
        new = ADAM_DECAY * second[:, here] + (1.0 - ADAM_DECAY) * mean * mean
        moment[:, here] = new
        step = mean / (jnp.sqrt(new) + ADAM_EPS)
        square = jnp.sum(step * step, axis=0, keepdims=True)
        lanes = square[:, 0:128]
        for k in range(1, width // 128):
            lanes = lanes + square[:, k * 128 : (k + 1) * 128]
        lane = (c // 8) * 128
        squares[c % 8 : c % 8 + 1, lane : lane + 128] = lanes
    for o in range(packed.shape[0]):
        col = owner_cols[row, o]
        start = pl.multiple_of(jnp.maximum(col, 0) * width, width)
        piece = averaged[:, pl.ds(start, width)]
        packed[o] = jnp.where(col >= 0, piece, 0.0)


def load_block(blocks, high, low):
    pieces, quarters, rows, _ = blocks.shape
    for i in range(quarters):
        for r in range(pieces):
            at = (i * pieces + r) * rows
            high[at : at + rows, :], low[at : at + rows, :] = split(blocks[r, i])


def apply_kernel(ids, blocks, *refs):
    roots = refs[:8]
    applied, gh, gl, lh, ll, rh, rl, whole = refs[8:]
    count, side = 8, whole.shape[0]
    share = side // count
    load_block(blocks, gh, gl)
    for k in range(count):
        start = pl.multiple_of(lax.rem(ids[0] - k + count, count) * share, share)
        lh[pl.ds(start, share), :], ll[pl.ds(start, share), :] = split(roots[k][0])
        rh[pl.ds(start, share), :], rl[pl.ds(start, share), :] = split(roots[k][1])
    right = dot3((gh[...], gl[...]), (rh[...], rl[...]), ((1,), (0,)))
    value = dot3((lh[...], ll[...]), split(right), ((1,), (0,)))
    whole[...] = value
    norm = jnp.sqrt(jnp.sum(value * value, keepdims=True))
    scale = 1.0 / (norm + NORM_EPS)
    pieces, quarters, rows, _ = applied.shape
    for i in range(quarters):
        for r in range(pieces):
            at = (i * pieces + r) * rows
            applied[r, i] = whole[at : at + rows, :] * scale


def gram_kernel(ids, blocks, squares, *refs):
    outs = refs[:8]
    gh, gl, left, right = refs[8:]
    count, side = 8, left.shape[0]
    share = side // count
    load_block(blocks, gh, gl)
    g = (gh[...], gl[...])
    left[...] = dot3(g, g, ((1,), (1,)))
    right[...] = dot3(g, g, ((0,), (0,)))
    for k in range(count):
        start = pl.multiple_of(lax.rem(ids[0] + k, count) * share, share)
        outs[k][0:share, :] = left[pl.ds(start, share), :]
        outs[k][share : 2 * share, :] = right[pl.ds(start, share), :]
        outs[k][2 * share :, :] = squares[...]


def stat_kernel(ids, moment, stat_left, stat_right, *refs):
    grams = refs[:8]
    moment_new, left, right = refs[8:]
    moment_new[...] = moment[...]
    share = left.shape[1]
    for k in range(8):
        b = lax.rem(ids[0] - k + 8, 8)
        left[b] = SHAMPOO_DECAY * stat_left[b] + (1.0 - SHAMPOO_DECAY) * grams[k][0:share, :]
        right[b] = (
            SHAMPOO_DECAY * stat_right[b] + (1.0 - SHAMPOO_DECAY) * grams[k][share : 2 * share, :]
        )


def direction_kernel(ids, owner_cols, returned, *refs):
    grams = refs[:8]
    direction, norms = refs[8:]
    tail = grams[0].shape[0] - 8
    row = ids[1]
    width = returned.shape[-1]
    total = grams[0][tail:, :]
    for k in range(1, 8):
        total = total + grams[k][tail:, :]
    for c in range(direction.shape[-1] // width):
        lane = (c // 8) * 128
        lanes = total[c % 8 : c % 8 + 1, lane : lane + 128]
        norm = jnp.sqrt(jnp.sum(lanes, axis=1, keepdims=True))
        norms[c : c + 1, :] = jnp.broadcast_to(norm, (1, 128))
    for o in range(returned.shape[0]):
        col = owner_cols[row, o]

        @pl.when(col >= 0)
        def _():
            norm = norms[pl.ds(col, 1), :][:, 0:1]
            start = pl.multiple_of(col * width, width)
            direction[:, pl.ds(start, width)] = returned[o] * norm


def root_kernel(ids, root_left, root_right, *outs):
    for k in range(8):
        to = lax.rem(ids[0] + k, 8)
        outs[k][0] = root_left[to]
        outs[k][1] = root_right[to]


def staged(kernel, n_small, n_in, n_out, *refs):
    cut = [n_small, n_in, n_out, n_in, n_out]
    groups, at = [], 0
    for size in cut:
        groups.append(refs[at : at + size])
        at += size
    small, sources, targets, ins, outs = groups
    in_sems, out_sems = refs[at : at + 2]
    loads = [
        pltpu.make_async_copy(src, dst, in_sems.at[i])
        for i, (src, dst) in enumerate(zip(sources, ins))
    ]
    for load in loads:
        load.start()
    for load in loads:
        load.wait()
    kernel(*small, *ins, *outs, *refs[at + 2 :])
    stores = [
        pltpu.make_async_copy(src, dst, out_sems.at[i])
        for i, (src, dst) in enumerate(zip(outs, targets))
    ]
    for store in stores:
        store.start()
    for store in stores:
        store.wait()


def call(kernel, outs, small, ins, scratch):
    hbm = pl.BlockSpec(memory_space=pltpu.HBM)
    smem = pl.BlockSpec(memory_space=pltpu.SMEM)
    held = [pltpu.VMEM(x.shape, F32) for x in ins] + [pltpu.VMEM(s, F32) for s in outs]
    sems = [pltpu.SemaphoreType.DMA((len(ins),)), pltpu.SemaphoreType.DMA((len(outs),))]
    return pl.pallas_call(
        functools.partial(staged, kernel, len(small), len(ins), len(outs)),
        out_shape=[pltpu.HBM(shape, F32) for shape in outs],
        in_specs=[smem] * len(small) + [hbm] * len(ins),
        out_specs=[hbm] * len(outs),
        scratch_shapes=held + sems + scratch,
        compiler_params=PARAMS,
    )(*small, *[pltpu.with_memory_space_constraint(x, pltpu.HBM) for x in ins])


def shards(gradient, second_moment, owner_cols, stat_left, stat_right, root_left, root_right):
    shard_rows, full_width = gradient.shape[1:]
    side = stat_left.shape[-1]
    owners = lax.axis_size("fsdp")
    reps = lax.axis_size("rep")
    chips = reps // 2
    cols = full_width // side
    rows = shard_rows // reps
    share = side // reps
    quarters = side // shard_rows
    block_rows = owner_cols.shape[0]
    rep = lax.axis_index("rep")
    chip, core = rep // 2, rep % 2
    my_row = lax.axis_index("fsdp") // quarters
    ids = jnp.stack([rep, my_row]).astype(jnp.int32)
    oc = owner_cols[:, 0, :]
    barrier = lax.optimization_barrier

    grad = gradient[0].reshape(chips, 2, rows, full_width)
    swap = [(i, i ^ 1) for i in range(reps)]
    pieces = {}
    for k in (2, 1, 3, 0):
        here = pick(grad, (chip + k) % chips)
        other = lax.ppermute(pick(here, 1 - core), "rep", swap)
        pieces[k] = pick(here, core) + other
    parts = [pieces[0]] + [rep_shift(pieces[k], 2 * k, reps) for k in (1, 2, 3)]
    second = lax.dynamic_slice_in_dim(second_moment, rep * rows, rows, 0)
    later_ids, _ = barrier((ids, pieces[0]))
    stats = (block_rows, share, side)
    pair = (2, share, side)
    roots = call(root_kernel, [pair] * reps, [later_ids], [root_left[0, 0], root_right[0, 0]], [])

    strip = (rows, full_width)
    tail = (8, side)
    moment, squares, packed = call(
        functools.partial(moment_kernel, cols, reps),
        [strip, tail, (owners, rows, side)],
        [ids, oc],
        [*parts, second],
        [pltpu.VMEM(strip, F32)],
    )
    packed, *roots = barrier((packed, *roots))
    arrived = lax.all_to_all(packed, "fsdp", 0, 0, tiled=True)
    moment_all = lax.all_gather(moment, "rep", axis=0, tiled=True)
    roots = [r if k == 0 else rep_shift(r, k, reps) for k, r in enumerate(roots)]
    arrived, squares, *roots = barrier((arrived, squares, *roots))

    square_sum = squares
    for bits in (1, 2, 3):
        square_sum = square_sum + lax.ppermute(
            squares, "fsdp", [(i, i ^ bits) for i in range(owners)]
        )
    blocks = lax.all_to_all(
        arrived.reshape(block_rows, quarters, rows, side), "rep", 0, 0, tiled=True
    )
    half = pltpu.VMEM((side, side), BF16)
    full = pltpu.VMEM((side, side), F32)
    (applied,) = call(
        apply_kernel, [blocks.shape], [ids], [blocks, *roots], [half] * 6 + [full]
    )
    spread = lax.all_to_all(applied, "rep", 0, 0, tiled=True)
    grams = call(
        gram_kernel,
        [(2 * share + 8, side)] * reps,
        [ids],
        [blocks, square_sum],
        [half] * 2 + [full] * 2,
    )
    spread, *grams = barrier((spread, *grams))
    returned = lax.all_to_all(spread.reshape(owners, rows, side), "fsdp", 0, 0, tiled=True)
    grams = [g if k == 0 else rep_shift(g, k, reps) for k, g in enumerate(grams)]
    returned, *grams = barrier((returned, *grams))
    (part,) = call(
        direction_kernel,
        [strip],
        [ids, oc],
        [returned, *grams],
        [pltpu.VMEM((16, 128), F32)],
    )
    direction = lax.all_gather(part, "rep", axis=0, tiled=True)
    moment_new, left_new, right_new = call(
        stat_kernel,
        [(shard_rows, full_width), stats, stats],
        [ids],
        [moment_all, stat_left[0, 0], stat_right[0, 0], *grams],
        [],
    )
    return (direction, moment_new, left_new[None, None], right_new[None, None])


def solution(mesh):
    return jax.shard_map(
        shards,
        mesh=mesh,
        in_specs=(
            P("rep", "fsdp", None),
            P("fsdp", None),
            P(),
            P("fsdp", None, None, "rep", None),
            P("fsdp", None, None, "rep", None),
            P("fsdp", None, None, "rep", None),
            P("fsdp", None, None, "rep", None),
        ),
        out_specs=(
            P("fsdp", None),
            P("fsdp", None),
            P("fsdp", None, None, "rep", None),
            P("fsdp", None, None, "rep", None),
        ),
        check_vma=False,
    )
```

time: 717 us -> 232 us (0.32); the launches traced: 704 us -> 232 us
  waiting for transfers between devices: 482 us -> 103 us
  blocking collectives: 66.7 us -> 17.9 us
  matrix products: 44.9 us -> 0 us
  local copies, waits for them, and re-layouts: 51 us -> 7.56 us
  starting transfers between devices: 19.7 us -> 56.4 us
  Pallas kernels: 0 us -> 29 us
  other arithmetic: 25.2 us -> 3.81 us
    all_to_all x2 -> x3, waiting for transfers between devices: 343 us -> 2.78 us  [the longest x1 2.78 us: shards(): spread = lax.all_to_all(applied, 'rep', 0, 0, tiled=True)]
    ppermute x0 -> x24, waiting for transfers between devices: none -> 74.4 us  [the longest x17 68.2 us: rep_shift(): lax.ppermute(value, 'rep', [(i, (i + step) % count) for i in range(count)])]
    psum x1 -> x0, waiting for transfers between devices: 70.8 us -> none  [shards(): summed = lax.psum(gradient[0], 'rep')]
    psum x1 -> x0, blocking collectives: 66.7 us -> none  [shards(): lax.psum(place_row(shampoo_squares, block_rows, my_block_row), 'fsdp')]
    dot_general x4 -> x0, matrix products: 44.9 us -> none  [the longest x1 12.8 us: shards(): jnp.einsum('kbij,kblj->kbil', grad_rows, owned_blocks, precision=HIGHEST)]
    all_gather x2, waiting for transfers between devices: 68 us -> 25.4 us  [the longest x1 25.4 us: shards(): direction = lax.all_gather(part, 'rep', axis=0, tiled=True)]
    ppermute x0 -> x24, starting transfers between devices: none -> 30.1 us  [the longest x17 22.6 us: rep_shift(): lax.ppermute(value, 'rep', [(i, (i + step) % count) for i in range(count)])]
    pallas_call x0 -> x6, Pallas kernels: none -> 29 us  [call(): pl.pallas_call(functools.partial(staged, kernel, len(small), len(ins), le...]
  transfers between devices with their start and end apart: 5 -> 29, of which waited for: 4 -> 20; matrix products, arithmetic and copies ran while one was open for 6% -> 1% of each run, Pallas kernels for 0% -> 11%
where the time goes in v1:
time: 232 us
  waiting for transfers between devices  103 us (44%)
  starting transfers between devices  56.4 us (24%)
  Pallas kernels  29 us (12%)
  blocking collectives  17.9 us (8%)
  between operations  14.3 us (6%)
  local copies, waits for them, and re-layouts  7.56 us (3%)
  other arithmetic  3.81 us (2%)
    ppermute x17, waiting for transfers between devices, rep_shift(): lax.ppermute(value, 'rep', [(i, (i + step) % count) for i in range(count)])  68.2 us
    pallas_call x6, Pallas kernels, call(): pl.pallas_call(functools.partial(staged, kernel, len(small), len(ins), le...  29 us
    all_gather x1, waiting for transfers between devices, shards(): direction = lax.all_gather(part, 'rep', axis=0, tiled=True)  25.4 us
    ppermute x17, starting transfers between devices, rep_shift(): lax.ppermute(value, 'rep', [(i, (i + step) % count) for i in range(count)])  22.6 us
    all_to_all x1, blocking collectives, shards(): lax.all_to_all(arrived.reshape(block_rows, quarters, rows, side), 'rep',...  17.9 us
    all_to_all x1, starting transfers between devices, shards(): arrived = lax.all_to_all(packed, 'fsdp', 0, 0, tiled=True)  11.3 us
    all_to_all x1, starting transfers between devices, shards(): lax.all_to_all(spread.reshape(owners, rows, side), 'fsdp', 0, 0, tiled=True)  9.7 us
    all_to_all x1, starting transfers between devices, shards(): spread = lax.all_to_all(applied, 'rep', 0, 0, tiled=True)  5.17 us
  transfers between devices with their start and end apart: 29, of which 20 were waited for; matrix products, arithmetic and copies ran while one was open for 1% of the time, Pallas kernels for 11%

profile of v1, /device:TPU:1, one launch (start us, length us, event | category | flops | bytes accessed | tf_op | source)
XLA Modules:
  0.0 231.6 jit_solution(11627933139410585674)
XLA Ops:
  10.1 3.2 %collective-permute-start.5 = (f32[16,6656]{1,0:T(8,128)}, f32[16,6656]{1,0:T(8,128)}, u32[]{:S(2)}, u32[]{:S(2)}) collective-permute-start(f32[16,6656]{1,0:T(8,128)} %get-tuple-element.128), channel_id=1, source_target_pairs={{0,1},{1,0},{2,3},{3,2},{4,5},{5,4},{6,7},{7,6},{8,9},{9,8},{10,11... | collective-permute-start | bytes 1277960 | tf_op jit(solution)/shard_map/ppermute | solution.py:221
  16.9 3.1 %bitcast_add_fusion = (f32[16,6656]{1,0:T(8,128)}, f32[16,6656]{1,0:T(8,128)}, f32[16,6656]{1,0:T(8,128)}, f32[16,6656]{1,0:T(8,128)}) fusion(f32[16,6656]{1,0:T(8,128)} %collective-permute-done.5, f32[4,2,16,6656]{3,2,1,0:T(8,128)} %bitcast.31, s32[]{:T(128)S(6)} %select_n.89, s32[]{:T(128)S(6)} %select_n.78, f32[16,6656]{1,0:T(8,128)} %collective-permute-done.3, ...), kind=kLoop, calls=%fused_computation | loop fusion | flops 425984 | bytes 5111828 | tf_op jit(solution)/shard_map/add | solution.py:222
  22.8 8.6 %collective-permute-done.6.refs_5_ = f32[16,6656]{1,0:T(8,128)} collective-permute-done((f32[16,6656]{1,0:T(8,128)}, f32[16,6656]{1,0:T(8,128)}, u32[]{:S(2)}, u32[]{:S(2)}) %collective-permute-start.6) | collective-permute-done | bytes 426016 | tf_op jit(solution)/shard_map/ppermute | solution.py:20
  33.4 10.1 %collective-permute-done.2.refs_3_ = f32[16,6656]{1,0:T(8,128)} collective-permute-done((f32[16,6656]{1,0:T(8,128)}, f32[16,6656]{1,0:T(8,128)}, u32[]{:S(2)}, u32[]{:S(2)}) %collective-permute-start.2) | collective-permute-done | bytes 426016 | tf_op jit(solution)/shard_map/ppermute | solution.py:20
  43.5 3.7 %shard_map.102 = (f32[16,6656]{1,0:T(8,128)}, f32[8,512]{1,0:T(8,128)}, f32[32,16,512]{2,1,0:T(8,128)}) custom-call(s32[2]{0:T(128)S(1)} %pad_add_fusion.refs_0_, s32[8,32]{1,0:T(8,128)S(1)} %bitcast.28, f32[16,6656]{1,0:T(8,128)} %get-tuple-element.127.refs_2_, f32[16,6656]{1,0:T(8,128)} %collective-permute-done.2.refs_3_, ...), custom_call_target="tpu_custom_call" | custom-call | tf_op jit(solution)/shard_map/pallas_call | solution.py:188
  47.2 3.5 %shard_map.103 = (f32[2,64,512]{2,1,0:T(8,128)}, f32[2,64,512]{2,1,0:T(8,128)}, f32[2,64,512]{2,1,0:T(8,128)}, f32[2,64,512]{2,1,0:T(8,128)}, f32[2,64,512]{2,1,...) custom-call(s32[2]{0:T(128)S(1)} %pad_add_fusion.refs_0_, ...), custom_call_target="tpu_custom_call" | custom-call | tf_op jit(solution)/shard_map/pallas_call | solution.py:188
  50.7 11.3 %all-to-all-start = ((f32[32,16,512]{2,1,0:T(8,128)}), f32[32,16,512]{2,1,0:T(8,128)}, u32[]{:S(2)}, u32[]{:S(2)}) async-start(f32[32,16,512]{2,1,0:T(8,128)} %get-tuple-element.74), calls=%async_computation | async-start | bytes 2097152 | tf_op jit(solution)/shard_map/all_to_all | solution.py:240
  69.2 4.3 %collective-permute-done.7.refs_3_ = f32[2,64,512]{2,1,0:T(8,128)} collective-permute-done((f32[2,64,512]{2,1,0:T(8,128)}, f32[2,64,512]{2,1,0:T(8,128)}, u32[]{:S(2)}, u32[]{:S(2)}) %collective-permute-start.7) | collective-permute-done | bytes 262176 | tf_op jit(solution)/shard_map/ppermute | solution.py:20
  73.5 3.7 %collective-permute-start.12 = (f32[2,64,512]{2,1,0:T(8,128)}, f32[2,64,512]{2,1,0:T(8,128)}, u32[]{:S(2)}, u32[]{:S(2)}) collective-permute-start(f32[2,64,512]{2,1,0:T(8,128)} %get-tuple-element.82), channel_id=1, source_target_pairs={{0,6},{1,7},{2,0},{3,1},{4,2},{5,3},{6,4},{7,5},{8,14},{9,15},{10,... | collective-permute-start | bytes 786440 | tf_op jit(solution)/shard_map/ppermute | solution.py:20
  77.2 12.5 %collective-permute-done.8.refs_4_ = f32[2,64,512]{2,1,0:T(8,128)} collective-permute-done((f32[2,64,512]{2,1,0:T(8,128)}, f32[2,64,512]{2,1,0:T(8,128)}, u32[]{:S(2)}, u32[]{:S(2)}) %collective-permute-start.8) | collective-permute-done | bytes 262176 | tf_op jit(solution)/shard_map/ppermute | solution.py:20
  91.1 9.1 %collective-permute-done.10.refs_6_ = f32[2,64,512]{2,1,0:T(8,128)} collective-permute-done((f32[2,64,512]{2,1,0:T(8,128)}, f32[2,64,512]{2,1,0:T(8,128)}, u32[]{:S(2)}, u32[]{:S(2)}) %collective-permute-start.10) | collective-permute-done | bytes 262176 | tf_op jit(solution)/shard_map/ppermute | solution.py:20
  100.5 17.9 %all_to_all.20.refs_1_ = f32[8,4,16,512]{3,2,1,0:T(8,128)} all-to-all(f32[8,4,16,512]{3,2,1,0:T(8,128)} %bitcast.14), channel_id=1, replica_groups=mesh['fsdp'=32,'rep'=8] {'rep'}, dimensions={0} | all-to-all | bytes 2097152 | tf_op jit(solution)/shard_map/all_to_all | solution.py:250
  118.5 5.9 %shard_map.104 = f32[8,4,16,512]{3,2,1,0:T(8,128)} custom-call(s32[2]{0:T(128)S(1)} %pad_add_fusion.refs_0_, f32[8,4,16,512]{3,2,1,0:T(8,128)} %all_to_all.20.refs_1_, f32[2,64,512]{2,1,0:T(8,128)} %get-tuple-element.85.refs_2_, f32[2,64,512]{2,1,0:T(8,128)} %collective-permute-done.7.refs_3_, f32[2,64,512]{2,1,0:T(8,128)} %collective-permute-done.8.refs_4_, ...), custom_call_target="tpu_custom_call" | custom-call | tf_op jit(solution)/shard_map/pallas_call | solution.py:188
  124.4 5.2 %all-to-all-start.2 = ((f32[8,4,16,512]{3,2,1,0:T(8,128)}), f32[8,4,16,512]{3,2,1,0:T(8,128)}, u32[]{:S(2)}, u32[]{:S(2)}) async-start(f32[8,4,16,512]{3,2,1,0:T(8,128)} %shard_map.104), calls=%async_computation.2 | async-start | bytes 2097152 | tf_op jit(solution)/shard_map/all_to_all | solution.py:258
  129.5 3.3 %collective-permute-start.16 = (f32[8,512]{1,0:T(8,128)S(1)}, f32[8,512]{1,0:T(8,128)S(1)}, u32[]{:S(2)}, u32[]{:S(2)}) collective-permute-start(f32[8,512]{1,0:T(8,128)S(1)} %copy-done.2), channel_id=1, source_target_pairs={{0,24},{8,16},{16,8},{24,0},{32,56},{40,48},{48,40},{56,32},{64,88... | collective-permute-start | bytes 49160 | tf_op jit(solution)/shard_map/ppermute | solution.py:247
  136.9 5.0 %shard_map.105 = (f32[136,512]{1,0:T(8,128)}, f32[136,512]{1,0:T(8,128)}, f32[136,512]{1,0:T(8,128)}, f32[136,512]{1,0:T(8,128)}, f32[136,512]{1,0:T(8,128)}, /*...) custom-call(s32[2]{0:T(128)S(1)} %pad_add_fusion.refs_0_, f32[8,4,16,512]{3,2,1,0:T(8,128)} %all_to_all.20.refs_1_, ...), custom_call_target="tpu_custom_call" | custom-call | tf_op jit(solution)/shard_map/pallas_call | solution.py:188
  142.0 2.8 %all-to-all-done.2 = f32[8,4,16,512]{3,2,1,0:T(8,128)} async-done(((f32[8,4,16,512]{3,2,1,0:T(8,128)}), f32[8,4,16,512]{3,2,1,0:T(8,128)}, u32[]{:S(2)}, u32[]{:S(2)}) %all-to-all-start.2) | async-done | bytes 1048608 | tf_op jit(solution)/shard_map/all_to_all | solution.py:258
  144.8 9.7 %all-to-all-start.3 = ((f32[32,16,512]{2,1,0:T(8,128)}), f32[32,16,512]{2,1,0:T(8,128)}, u32[]{:S(2)}, u32[]{:S(2)}) async-start(f32[32,16,512]{2,1,0:T(8,128)} %bitcast.15), calls=%async_computation.3 | async-start | bytes 2097152 | tf_op jit(solution)/shard_map/all_to_all | solution.py:267
  164.4 7.3 %collective-permute-done.18.refs_5_.refs_6_ = f32[136,512]{1,0:T(8,128)} collective-permute-done((f32[136,512]{1,0:T(8,128)}, f32[136,512]{1,0:T(8,128)}, u32[]{:S(2)}, u32[]{:S(2)}) %collective-permute-start.18) | collective-permute-done | bytes 278560 | tf_op jit(solution)/shard_map/ppermute | solution.py:20
  171.7 11.9 %collective-permute-done.19.refs_6_.refs_7_ = f32[136,512]{1,0:T(8,128)} collective-permute-done((f32[136,512]{1,0:T(8,128)}, f32[136,512]{1,0:T(8,128)}, u32[]{:S(2)}, u32[]{:S(2)}) %collective-permute-start.19) | collective-permute-done | bytes 278560 | tf_op jit(solution)/shard_map/ppermute | solution.py:20
  184.4 4.1 %shard_map.106 = f32[16,6656]{1,0:T(8,128)} custom-call(s32[2]{0:T(128)S(1)} %pad_add_fusion.refs_0_, s32[8,32]{1,0:T(8,128)S(1)} %bitcast.29, f32[32,16,512]{2,1,0:T(8,128)} %all-to-all-done.3.refs_2_, f32[136,512]{1,0:T(8,128)} %get-tuple-element.112.refs_3_.refs_4_, f32[136,512]{1,0:T(8,128)} %collective-permute-done.17.refs_4_.refs_5_, ...), custom_call_target="tpu_custom_call" | custom-call | tf_op jit(solution)/shard_map/pallas_call | solution.py:188
  188.6 6.8 %shard_map.107 = (f32[128,6656]{1,0:T(8,128)}, f32[8,64,512]{2,1,0:T(8,128)}, f32[8,64,512]{2,1,0:T(8,128)}) custom-call(s32[2]{0:T(128)S(1)} %pad_add_fusion.refs_0_, f32[128,6656]{1,0:T(8,128)} %all-gather.5.cloned.1.call-done.refs_1_, f32[8,64,512]{2,1,0:T(8,128)} %bitcast.34, f32[8,64,512]{2,1,0:T(8,128)} %bitcast.35, ...), custom_call_target="tpu_custom_call" | custom-call | tf_op jit(solution)/shard_map/pallas_call | solution.py:188
  195.3 25.4 %all-gather.3.cloned.1.call-done = f32[128,6656]{1,0:T(8,128)} async-done(((f32[16,6656]{1,0:T(8,128)}), f32[128,6656]{1,0:T(8,128)}) %all-gather.3.cloned.1.call-update) | async-done | bytes 3407888 | tf_op jit(solution)/shard_map/all_gather | solution.py:277
  220.8 4.0 %copy.12 = f32[128,6656]{1,0:T(8,128)} copy(f32[128,6656]{1,0:T(8,128)} %all-gather.3.cloned.1.call-done) | data formatting | bytes 6815744
  (55 shorter events, 34.7 us)
Async XLA Ops:
  7.2 181.4 %all-gather.5.cloned.1.call-start = ((), (), s32[]{:S(2)}) async-start(), calls=%async_computation.5 | async-start | bytes 3833856 | tf_op jit(solution)/shard_map/all_gather | solution.py:241
  10.1 5.0 %collective-permute-start.5 = (f32[16,6656]{1,0:T(8,128)}, f32[16,6656]{1,0:T(8,128)}, u32[]{:S(2)}, u32[]{:S(2)}) collective-permute-start(f32[16,6656]{1,0:T(8,128)} %get-tuple-element.128), channel_id=1, source_target_pairs={{0,1},{1,0},{2,3},{3,2},{4,5},{5,4},{6,7},{7,6},{8,9},{9,8},{10,11... | collective-permute-start | bytes 1277960 | tf_op jit(solution)/shard_map/ppermute | solution.py:221
  20.0 11.3 %collective-permute-start.6 = (f32[16,6656]{1,0:T(8,128)}, f32[16,6656]{1,0:T(8,128)}, u32[]{:S(2)}, u32[]{:S(2)}) collective-permute-start(f32[16,6656]{1,0:T(8,128)} %get-tuple-element.124), channel_id=1, source_target_pairs={{0,6},{1,7},{2,0},{3,1},{4,2},{5,3},{6,4},{7,5},{8,14},{9,15},{10,... | collective-permute-start | bytes 1277960 | tf_op jit(solution)/shard_map/ppermute | solution.py:20
  20.8 12.6 %collective-permute-start.4 = (f32[16,6656]{1,0:T(8,128)}, f32[16,6656]{1,0:T(8,128)}, u32[]{:S(2)}, u32[]{:S(2)}) collective-permute-start(f32[16,6656]{1,0:T(8,128)} %get-tuple-element.125), channel_id=1, source_target_pairs={{0,4},{1,5},{2,6},{3,7},{4,0},{5,1},{6,2},{7,3},{8,12},{9,13},{10,... | collective-permute-start | bytes 1277960 | tf_op jit(solution)/shard_map/ppermute | solution.py:20
  21.3 22.2 %collective-permute-start.2 = (f32[16,6656]{1,0:T(8,128)}, f32[16,6656]{1,0:T(8,128)}, u32[]{:S(2)}, u32[]{:S(2)}) collective-permute-start(f32[16,6656]{1,0:T(8,128)} %get-tuple-element.126), channel_id=1, source_target_pairs={{0,2},{1,3},{2,4},{3,5},{4,6},{5,7},{6,0},{7,1},{8,10},{9,11},{10,... | collective-permute-start | bytes 1277960 | tf_op jit(solution)/shard_map/ppermute | solution.py:20
  50.7 49.8 %all-to-all-start = ((f32[32,16,512]{2,1,0:T(8,128)}), f32[32,16,512]{2,1,0:T(8,128)}, u32[]{:S(2)}, u32[]{:S(2)}) async-start(f32[32,16,512]{2,1,0:T(8,128)} %get-tuple-element.74), calls=%async_computation | async-start | bytes 2097152 | tf_op jit(solution)/shard_map/all_to_all | solution.py:240
  62.1 11.5 %collective-permute-start.7 = (f32[2,64,512]{2,1,0:T(8,128)}, f32[2,64,512]{2,1,0:T(8,128)}, u32[]{:S(2)}, u32[]{:S(2)}) collective-permute-start(f32[2,64,512]{2,1,0:T(8,128)} %get-tuple-element.77), channel_id=1, source_target_pairs={{0,1},{1,2},{2,3},{3,4},{4,5},{5,6},{6,7},{7,0},{8,9},{9,10},{10,1... | collective-permute-start | bytes 786440 | tf_op jit(solution)/shard_map/ppermute | solution.py:20
  62.1 27.7 %collective-permute-start.8 = (f32[2,64,512]{2,1,0:T(8,128)}, f32[2,64,512]{2,1,0:T(8,128)}, u32[]{:S(2)}, u32[]{:S(2)}) collective-permute-start(f32[2,64,512]{2,1,0:T(8,128)} %get-tuple-element.78), channel_id=1, source_target_pairs={{0,2},{1,3},{2,4},{3,5},{4,6},{5,7},{6,0},{7,1},{8,10},{9,11},{10,... | collective-permute-start | bytes 786440 | tf_op jit(solution)/shard_map/ppermute | solution.py:20
  62.9 28.2 %collective-permute-start.9 = (f32[2,64,512]{2,1,0:T(8,128)}, f32[2,64,512]{2,1,0:T(8,128)}, u32[]{:S(2)}, u32[]{:S(2)}) collective-permute-start(f32[2,64,512]{2,1,0:T(8,128)} %get-tuple-element.79), channel_id=1, source_target_pairs={{0,3},{1,4},{2,5},{3,6},{4,7},{5,0},{6,1},{7,2},{8,11},{9,12},{10,... | collective-permute-start | bytes 786440 | tf_op jit(solution)/shard_map/ppermute | solution.py:20
  64.6 35.6 %collective-permute-start.10 = (f32[2,64,512]{2,1,0:T(8,128)}, f32[2,64,512]{2,1,0:T(8,128)}, u32[]{:S(2)}, u32[]{:S(2)}) collective-permute-start(f32[2,64,512]{2,1,0:T(8,128)} %get-tuple-element.80), channel_id=1, source_target_pairs={{0,4},{1,5},{2,6},{3,7},{4,0},{5,1},{6,2},{7,3},{8,12},{9,13},{10,... | collective-permute-start | bytes 786440 | tf_op jit(solution)/shard_map/ppermute | solution.py:20
  66.6 33.9 %collective-permute-start.11 = (f32[2,64,512]{2,1,0:T(8,128)}, f32[2,64,512]{2,1,0:T(8,128)}, u32[]{:S(2)}, u32[]{:S(2)}) collective-permute-start(f32[2,64,512]{2,1,0:T(8,128)} %get-tuple-element.81), channel_id=1, source_target_pairs={{0,5},{1,6},{2,7},{3,0},{4,1},{5,2},{6,3},{7,4},{8,13},{9,14},{10,... | collective-permute-start | bytes 786440 | tf_op jit(solution)/shard_map/ppermute | solution.py:20
  73.5 27.0 %collective-permute-start.12 = (f32[2,64,512]{2,1,0:T(8,128)}, f32[2,64,512]{2,1,0:T(8,128)}, u32[]{:S(2)}, u32[]{:S(2)}) collective-permute-start(f32[2,64,512]{2,1,0:T(8,128)} %get-tuple-element.82), channel_id=1, source_target_pairs={{0,6},{1,7},{2,0},{3,1},{4,2},{5,3},{6,4},{7,5},{8,14},{9,15},{10,... | collective-permute-start | bytes 786440 | tf_op jit(solution)/shard_map/ppermute | solution.py:20
  89.8 10.8 %collective-permute-start.13 = (f32[2,64,512]{2,1,0:T(8,128)}, f32[2,64,512]{2,1,0:T(8,128)}, u32[]{:S(2)}, u32[]{:S(2)}) collective-permute-start(f32[2,64,512]{2,1,0:T(8,128)} %get-tuple-element.83), channel_id=1, source_target_pairs={{0,7},{1,0},{2,1},{3,2},{4,3},{5,4},{6,5},{7,6},{8,15},{9,8},{10,9... | collective-permute-start | bytes 786440 | tf_op jit(solution)/shard_map/ppermute | solution.py:20
  124.4 20.4 %all-to-all-start.2 = ((f32[8,4,16,512]{3,2,1,0:T(8,128)}), f32[8,4,16,512]{3,2,1,0:T(8,128)}, u32[]{:S(2)}, u32[]{:S(2)}) async-start(f32[8,4,16,512]{3,2,1,0:T(8,128)} %shard_map.104), calls=%async_computation.2 | async-start | bytes 2097152 | tf_op jit(solution)/shard_map/all_to_all | solution.py:258
  129.5 4.8 %collective-permute-start.16 = (f32[8,512]{1,0:T(8,128)S(1)}, f32[8,512]{1,0:T(8,128)S(1)}, u32[]{:S(2)}, u32[]{:S(2)}) collective-permute-start(f32[8,512]{1,0:T(8,128)S(1)} %copy-done.2), channel_id=1, source_target_pairs={{0,24},{8,16},{16,8},{24,0},{32,56},{40,48},{48,40},{56,32},{64,88... | collective-permute-start | bytes 49160 | tf_op jit(solution)/shard_map/ppermute | solution.py:247
  144.8 39.6 %all-to-all-start.3 = ((f32[32,16,512]{2,1,0:T(8,128)}), f32[32,16,512]{2,1,0:T(8,128)}, u32[]{:S(2)}, u32[]{:S(2)}) async-start(f32[32,16,512]{2,1,0:T(8,128)} %bitcast.15), calls=%async_computation.3 | async-start | bytes 2097152 | tf_op jit(solution)/shard_map/all_to_all | solution.py:267
  154.5 66.3 %all-gather.3.cloned.1.call-start = ((), (), s32[]{:S(2)}) async-start(), calls=%async_computation.4 | async-start | bytes 3833856 | tf_op jit(solution)/shard_map/all_gather | solution.py:277
  154.5 7.5 %collective-permute-start.17 = (f32[136,512]{1,0:T(8,128)}, f32[136,512]{1,0:T(8,128)}, u32[]{:S(2)}, u32[]{:S(2)}) collective-permute-start(f32[136,512]{1,0:T(8,128)} %get-tuple-element.104), channel_id=1, source_target_pairs={{0,1},{1,2},{2,3},{3,4},{4,5},{5,6},{6,7},{7,0},{8,9},{9,10},{10,1... | collective-permute-start | bytes 835592 | tf_op jit(solution)/shard_map/ppermute | solution.py:20
  155.9 15.9 %collective-permute-start.18 = (f32[136,512]{1,0:T(8,128)}, f32[136,512]{1,0:T(8,128)}, u32[]{:S(2)}, u32[]{:S(2)}) collective-permute-start(f32[136,512]{1,0:T(8,128)} %get-tuple-element.105), channel_id=1, source_target_pairs={{0,2},{1,3},{2,4},{3,5},{4,6},{5,7},{6,0},{7,1},{8,10},{9,11},{10,... | collective-permute-start | bytes 835592 | tf_op jit(solution)/shard_map/ppermute | solution.py:20
  155.9 27.8 %collective-permute-start.19 = (f32[136,512]{1,0:T(8,128)}, f32[136,512]{1,0:T(8,128)}, u32[]{:S(2)}, u32[]{:S(2)}) collective-permute-start(f32[136,512]{1,0:T(8,128)} %get-tuple-element.106), channel_id=1, source_target_pairs={{0,3},{1,4},{2,5},{3,6},{4,7},{5,0},{6,1},{7,2},{8,11},{9,12},{10,... | collective-permute-start | bytes 835592 | tf_op jit(solution)/shard_map/ppermute | solution.py:20
  158.0 25.7 %collective-permute-start.20 = (f32[136,512]{1,0:T(8,128)}, f32[136,512]{1,0:T(8,128)}, u32[]{:S(2)}, u32[]{:S(2)}) collective-permute-start(f32[136,512]{1,0:T(8,128)} %get-tuple-element.107), channel_id=1, source_target_pairs={{0,4},{1,5},{2,6},{3,7},{4,0},{5,1},{6,2},{7,3},{8,12},{9,13},{10,... | collective-permute-start | bytes 835592 | tf_op jit(solution)/shard_map/ppermute | solution.py:20
  159.4 24.3 %collective-permute-start.21 = (f32[136,512]{1,0:T(8,128)}, f32[136,512]{1,0:T(8,128)}, u32[]{:S(2)}, u32[]{:S(2)}) collective-permute-start(f32[136,512]{1,0:T(8,128)} %get-tuple-element.108), channel_id=1, source_target_pairs={{0,5},{1,6},{2,7},{3,0},{4,1},{5,2},{6,3},{7,4},{8,13},{9,14},{10,... | collective-permute-start | bytes 835592 | tf_op jit(solution)/shard_map/ppermute | solution.py:20
  162.1 21.7 %collective-permute-start.22 = (f32[136,512]{1,0:T(8,128)}, f32[136,512]{1,0:T(8,128)}, u32[]{:S(2)}, u32[]{:S(2)}) collective-permute-start(f32[136,512]{1,0:T(8,128)} %get-tuple-element.109), channel_id=1, source_target_pairs={{0,6},{1,7},{2,0},{3,1},{4,2},{5,3},{6,4},{7,5},{8,14},{9,15},{10,... | collective-permute-start | bytes 835592 | tf_op jit(solution)/shard_map/ppermute | solution.py:20
  171.7 12.6 %collective-permute-start.23 = (f32[136,512]{1,0:T(8,128)}, f32[136,512]{1,0:T(8,128)}, u32[]{:S(2)}, u32[]{:S(2)}) collective-permute-start(f32[136,512]{1,0:T(8,128)} %get-tuple-element.110), channel_id=1, source_target_pairs={{0,7},{1,0},{2,1},{3,2},{4,3},{5,4},{6,5},{7,6},{8,15},{9,8},{10,9... | collective-permute-start | bytes 835592 | tf_op jit(solution)/shard_map/ppermute | solution.py:20
  (8 other events, 74.5 us)
Sparse Core Ops, SparseCore 0:
  47.3 44.2 all-gather.4
  188.6 32.0 all-gather.2

commit v2 on v1

--- a/solution.py
+++ b/solution.py
@@ -73,16 +73,26 @@
 
 def apply_kernel(ids, blocks, *refs):
     roots = refs[:8]
-    applied, gh, gl, lh, ll, rh, rl, whole = refs[8:]
+    applied, gh, gl, left, right, whole = refs[8:]
     count, side = 8, whole.shape[0]
     share = side // count
+    part = side // 4
     load_block(blocks, gh, gl)
     for k in range(count):
-        start = pl.multiple_of(lax.rem(ids[0] - k + count, count) * share, share)
-        lh[pl.ds(start, share), :], ll[pl.ds(start, share), :] = split(roots[k][0])
-        rh[pl.ds(start, share), :], rl[pl.ds(start, share), :] = split(roots[k][1])
-    right = dot3((gh[...], gl[...]), (rh[...], rl[...]), ((1,), (0,)))
-    value = dot3((lh[...], ll[...]), split(right), ((1,), (0,)))
+        other = lax.rem(ids[0] - k + count, count)
+        start = pl.multiple_of(other * share, share)
+        for j in range(3):
+            lane = pl.multiple_of(lax.rem(other // 2 + j, 4) * part, part)
+            here = slice(j * part, (j + 1) * part)
+            left[pl.ds(start, share), pl.ds(lane, part)] = roots[k][0, :, here]
+            right[pl.ds(start, share), pl.ds(lane, part)] = roots[k][1, :, here]
+    for x in range(4):
+        before = (x + 3) % 4
+        at, to = slice(x * part, (x + 1) * part), slice(before * part, (before + 1) * part)
+        left[at, to] = left[to, at].T
+        right[at, to] = right[to, at].T
+    product = dot3((gh[...], gl[...]), split(right[...]), ((1,), (0,)))
+    value = dot3(split(left[...]), split(product), ((1,), (0,)))
     whole[...] = value
     norm = jnp.sqrt(jnp.sum(value * value, keepdims=True))
     scale = 1.0 / (norm + NORM_EPS)
@@ -109,10 +119,17 @@
         outs[k][2 * share :, :] = squares[...]
 
 
-def stat_kernel(ids, moment, stat_left, stat_right, *refs):
+def stat_kernel(ids, own, swapped, stat_left, stat_right, *refs):
     grams = refs[:8]
     moment_new, left, right = refs[8:]
-    moment_new[...] = moment[...]
+    core = lax.rem(ids[0], 2)
+    rows = own.shape[0] // 4
+    for x in range(4):
+        here = slice(x * rows, (x + 1) * rows)
+        at = pl.multiple_of((2 * x + core) * rows, rows)
+        moment_new[pl.ds(at, rows), :] = own[here, :]
+        at = pl.multiple_of((2 * x + 1 - core) * rows, rows)
+        moment_new[pl.ds(at, rows), :] = swapped[here, :]
     share = left.shape[1]
     for k in range(8):
         b = lax.rem(ids[0] - k + 8, 8)
@@ -124,7 +141,7 @@
 
 def direction_kernel(ids, owner_cols, returned, *refs):
     grams = refs[:8]
-    direction, norms = refs[8:]
+    low, high, direction, norms = refs[8:]
     tail = grams[0].shape[0] - 8
     row = ids[1]
     width = returned.shape[-1]
@@ -145,12 +162,9 @@
             start = pl.multiple_of(col * width, width)
             direction[:, pl.ds(start, width)] = returned[o] * norm
 
-
-def root_kernel(ids, root_left, root_right, *outs):
-    for k in range(8):
-        to = lax.rem(ids[0] + k, 8)
-        outs[k][0] = root_left[to]
-        outs[k][1] = root_right[to]
+    middle = low.shape[1]
+    low[...] = direction[:, :middle]
+    high[...] = direction[:, middle:]
 
 
 def staged(kernel, n_small, n_in, n_out, *refs):
@@ -195,6 +209,63 @@
     )(*small, *[pltpu.with_memory_space_constraint(x, pltpu.HBM) for x in ins])
 
 
+def root_plan(ids, ins, outs):
+    chip = ids[0] // 2
+    for k, out in enumerate(outs):
+        to = lax.rem(ids[0] + k, 8)
+        for side in range(2):
+            for j in range(3):
+                lane = pl.multiple_of(lax.rem(chip + j, 4) * 128, 128)
+                yield (
+                    ins[side].at[to, :, pl.ds(lane, 128)],
+                    out.at[side, :, slice(j * 128, (j + 1) * 128)],
+                )
+
+
+def place_plan(ids, ins, outs):
+    chip, core = ids[0] // 2, ids[0] % 2
+    rows, middle = ins[0].shape
+    for j, piece in enumerate(ins):
+        owner = core if j < 8 else 1 - core
+        from_chip = lax.rem(chip + (0, 3, 1, 2)[j % 8 // 2], 4)
+        start = pl.multiple_of((from_chip * 2 + owner) * rows, rows)
+        columns = slice(j % 2 * middle, (j % 2 + 1) * middle)
+        yield piece, outs[0].at[pl.ds(start, rows), columns]
+
+
+def copying(plan, n_small, n_in, n_out, *refs):
+    small, ins = refs[:n_small], refs[n_small : n_small + n_in]
+    outs = refs[n_small + n_in : n_small + n_in + n_out]
+    held, (sems, out_sems) = refs[n_small + n_in + n_out : -2], refs[-2:]
+    loads = [
+        pltpu.make_async_copy(src, dst, sems.at[i])
+        for i, (src, dst) in enumerate(plan(*small, ins, held))
+    ]
+    stores = [
+        pltpu.make_async_copy(src, dst, out_sems.at[i])
+        for i, (src, dst) in enumerate(zip(held, outs))
+    ]
+    for copies in (loads, stores):
+        for copy in copies:
+            copy.start()
+        for copy in copies:
+            copy.wait()
+
+
+def shuffle(plan, outs, small, ins, count):
+    hbm = pl.BlockSpec(memory_space=pltpu.HBM)
+    smem = pl.BlockSpec(memory_space=pltpu.SMEM)
+    return pl.pallas_call(
+        functools.partial(copying, plan, len(small), len(ins), len(outs)),
+        out_shape=[pltpu.HBM(shape, F32) for shape in outs],
+        in_specs=[smem] * len(small) + [hbm] * len(ins),
+        out_specs=[hbm] * len(outs),
+        scratch_shapes=[pltpu.VMEM(shape, F32) for shape in outs]
+        + [pltpu.SemaphoreType.DMA((count,)), pltpu.SemaphoreType.DMA((len(outs),))],
+        compiler_params=PARAMS,
+    )(*small, *[pltpu.with_memory_space_constraint(x, pltpu.HBM) for x in ins])
+
+
 def shards(gradient, second_moment, owner_cols, stat_left, stat_right, root_left, root_right):
     shard_rows, full_width = gradient.shape[1:]
     side = stat_left.shape[-1]
@@ -215,17 +286,26 @@
 
     grad = gradient[0].reshape(chips, 2, rows, full_width)
     swap = [(i, i ^ 1) for i in range(reps)]
-    pieces = {}
-    for k in (2, 1, 3, 0):
-        here = pick(grad, (chip + k) % chips)
-        other = lax.ppermute(pick(here, 1 - core), "rep", swap)
-        pieces[k] = pick(here, core) + other
-    parts = [pieces[0]] + [rep_shift(pieces[k], 2 * k, reps) for k in (1, 2, 3)]
+    other = lax.ppermute(pick(grad, 1 - core, 1), "rep", swap)
+    mine = pick(grad, core, 1)
+    parts = []
+    for k in range(chips):
+        to = (chip + k) % chips
+        piece = pick(mine, to) + pick(other, to)
+        parts.append(piece if k == 0 else rep_shift(piece, 2 * k, reps))
     second = lax.dynamic_slice_in_dim(second_moment, rep * rows, rows, 0)
-    later_ids, _ = barrier((ids, pieces[0]))
+    later_ids, _ = barrier((ids, parts[0]))
     stats = (block_rows, share, side)
     pair = (2, share, side)
-    roots = call(root_kernel, [pair] * reps, [later_ids], [root_left[0, 0], root_right[0, 0]], [])
+    root_pair = (2, share, 3 * side // 4)
+    roots = shuffle(
+        root_plan,
+        [root_pair] * reps,
+        [later_ids],
+        [root_left[0, 0], root_right[0, 0]],
+        6 * reps,
+    )
+    ids, *roots = barrier((ids, *roots))
 
     strip = (rows, full_width)
     tail = (8, side)
@@ -236,9 +316,10 @@
         [*parts, second],
         [pltpu.VMEM(strip, F32)],
     )
+    lines = [[2 * x + c for x in range(chips)] for c in range(2)]
+    moment_line = lax.all_gather(moment, "rep", axis=0, tiled=True, axis_index_groups=lines)
     packed, *roots = barrier((packed, *roots))
     arrived = lax.all_to_all(packed, "fsdp", 0, 0, tiled=True)
-    moment_all = lax.all_gather(moment, "rep", axis=0, tiled=True)
     roots = [r if k == 0 else rep_shift(r, k, reps) for k, r in enumerate(roots)]
     arrived, squares, *roots = barrier((arrived, squares, *roots))
 
@@ -253,7 +334,7 @@
     half = pltpu.VMEM((side, side), BF16)
     full = pltpu.VMEM((side, side), F32)
     (applied,) = call(
-        apply_kernel, [blocks.shape], [ids], [blocks, *roots], [half] * 6 + [full]
+        apply_kernel, [blocks.shape], [ids], [blocks, *roots], [half] * 2 + [full] * 3
     )
     spread = lax.all_to_all(applied, "rep", 0, 0, tiled=True)
     grams = call(
@@ -263,24 +344,44 @@
         [blocks, square_sum],
         [half] * 2 + [full] * 2,
     )
-    spread, *grams = barrier((spread, *grams))
+    spread, moment_line, *grams = barrier((spread, moment_line, *grams))
+    moment_swap = lax.ppermute(moment_line, "rep", swap)
     returned = lax.all_to_all(spread.reshape(owners, rows, side), "fsdp", 0, 0, tiled=True)
     grams = [g if k == 0 else rep_shift(g, k, reps) for k, g in enumerate(grams)]
     returned, *grams = barrier((returned, *grams))
-    (part,) = call(
+    middle = full_width // 2
+    low, high = call(
         direction_kernel,
-        [strip],
+        [(rows, middle)] * 2,
         [ids, oc],
         [returned, *grams],
-        [pltpu.VMEM((16, 128), F32)],
-    )
-    direction = lax.all_gather(part, "rep", axis=0, tiled=True)
+        [pltpu.VMEM(strip, F32), pltpu.VMEM((16, 128), F32)],
+    )
+    left_low = rep_shift(low, 2, reps)
+    right_high = rep_shift(high, reps - 2, reps)
+    left_high = rep_shift(high, 2, reps)
+    right_low = rep_shift(low, reps - 2, reps)
+    last_ids, left_low, right_high = barrier((ids, left_low, right_high))
     moment_new, left_new, right_new = call(
         stat_kernel,
         [(shard_rows, full_width), stats, stats],
+        [last_ids],
+        [moment_line, moment_swap, stat_left[0, 0], stat_right[0, 0], *grams],
+        [],
+    )
+    far_low = rep_shift(left_low, 2, reps)
+    far_high = rep_shift(right_high, reps - 2, reps)
+    found = [low, high, left_low, left_high, right_low, right_high]
+    swapped = [lax.ppermute(x, "rep", swap) for x in found]
+    far_low, far_high, left_new = barrier((far_low, far_high, left_new))
+    far = [far_low, far_high]
+    far_swapped = [lax.ppermute(x, "rep", swap) for x in far]
+    (direction,) = shuffle(
+        place_plan,
+        [(shard_rows, full_width)],
         [ids],
-        [moment_all, stat_left[0, 0], stat_right[0, 0], *grams],
-        [],
+        [*found, *far, *swapped, *far_swapped],
+        16,
     )
     return (direction, moment_new, left_new[None, None], right_new[None, None])
 

time: 232 us -> 221 us (0.953)
  waiting for transfers between devices: 103 us -> 75.4 us
  starting transfers between devices: 56.4 us -> 67.9 us
  Pallas kernels: 29 us -> 33.3 us
  local copies, waits for them, and re-layouts: 7.56 us -> 4.8 us
  blocking collectives: 17.9 us -> 20.5 us
    all_gather x2 -> x1, waiting for transfers between devices: 25.4 us -> 0.02 us  [shards(): lax.all_gather(moment, 'rep', axis=0, tiled=True, axis_index_groups=lines)]
    pallas_call x0 -> x2, Pallas kernels: none -> 8.03 us  [shuffle(): pl.pallas_call(functools.partial(copying, plan, len(small), len(ins), len...]
    ppermute x4 -> x10, starting transfers between devices: 3.84 us -> 11.2 us  [the longest x6 6.1 us: shards(): swapped = [lax.ppermute(x, 'rep', swap) for x in found]]
    ppermute x17 -> x23, starting transfers between devices: 22.6 us -> 28.3 us  [rep_shift(): lax.ppermute(value, 'rep', [(i, (i + step) % count) for i in range(count)])]
    ppermute x17 -> x23, waiting for transfers between devices: 68.2 us -> 63.8 us  [rep_shift(): lax.ppermute(value, 'rep', [(i, (i + step) % count) for i in range(count)])]
    pallas_call x6 -> x5, Pallas kernels: 29 us -> 25.3 us  [call(): pl.pallas_call(functools.partial(staged, kernel, len(small), len(ins), le...]
    unnamed x7 -> x34, local copies, waits for them, and re-layouts: 3.98 us -> 1.09 us
    all_to_all x1, blocking collectives: 17.9 us -> 20.5 us  [shards(): lax.all_to_all(arrived.reshape(block_rows, quarters, rows, side), 'rep',...]
  transfers between devices with their start and end apart: 29 -> 40, of which waited for: 20 -> 23; matrix products, arithmetic and copies ran while one was open for 1% -> 1% of each run, Pallas kernels for 11% -> 11%
where the time goes in v2:
time: 221 us; the launch traced here: 220 us
  waiting for transfers between devices  75.4 us (34%)
  starting transfers between devices  67.9 us (31%)
  Pallas kernels  33.3 us (15%)
  blocking collectives  20.5 us (9%)
  between operations  14.3 us (6%)
  local copies, waits for them, and re-layouts  4.8 us (2%)
  other arithmetic  3.81 us (2%)
    ppermute x23, waiting for transfers between devices, rep_shift(): lax.ppermute(value, 'rep', [(i, (i + step) % count) for i in range(count)])  63.8 us
    ppermute x23, starting transfers between devices, rep_shift(): lax.ppermute(value, 'rep', [(i, (i + step) % count) for i in range(count)])  28.3 us
    pallas_call x5, Pallas kernels, call(): pl.pallas_call(functools.partial(staged, kernel, len(small), len(ins), le...  25.3 us
    all_to_all x1, blocking collectives, shards(): lax.all_to_all(arrived.reshape(block_rows, quarters, rows, side), 'rep',...  20.5 us
    all_to_all x1, starting transfers between devices, shards(): arrived = lax.all_to_all(packed, 'fsdp', 0, 0, tiled=True)  10.3 us
    all_to_all x1, starting transfers between devices, shards(): lax.all_to_all(spread.reshape(owners, rows, side), 'fsdp', 0, 0, tiled=True)  9.28 us
    pallas_call x2, Pallas kernels, shuffle(): pl.pallas_call(functools.partial(copying, plan, len(small), len(ins), len...  8.03 us
    ppermute x6, starting transfers between devices, shards(): swapped = [lax.ppermute(x, 'rep', swap) for x in found]  6.1 us
  transfers between devices with their start and end apart: 40, of which 23 were waited for; matrix products, arithmetic and copies ran while one was open for 1% of the time, Pallas kernels for 11%

profile of v2, /device:TPU:1, one launch (start us, length us, event | category | flops | bytes accessed | tf_op | source)
XLA Modules:
  0.0 219.9 jit_solution(5125191356897314834)
XLA Ops:
  7.2 2.9 %dynamic-slice_bitcast_fusion = f32[4,16,6656]{2,1,0:T(8,128)} fusion(f32[4,2,16,6656]{3,2,1,0:T(8,128)} %bitcast.32, s32[]{:T(128)S(6)} %select_n.75), kind=kLoop, calls=%fused_computation | loop fusion | bytes 3407876 | tf_op jit(solution)/shard_map/jit(dynamic_index_in_dim)/squeeze | solution.py:24
  10.1 3.2 %collective-permute-start = (f32[4,16,6656]{2,1,0:T(8,128)}, f32[4,16,6656]{2,1,0:T(8,128)}, u32[]{:S(2)}, u32[]{:S(2)}) collective-permute-start(f32[4,16,6656]{2,1,0:T(8,128)} %dynamic-slice_bitcast_fusion), channel_id=1, source_target_pairs={{0,1},{1,0},{2,3},{3,2},{4,5},{5,4},{6,7},{7,6},{8,9},{9,8},{10,11... | collective-permute-start | bytes 5111816 | tf_op jit(solution)/shard_map/ppermute | solution.py:289
  13.4 3.6 %collective-permute-done = f32[4,16,6656]{2,1,0:T(8,128)} collective-permute-done((f32[4,16,6656]{2,1,0:T(8,128)}, f32[4,16,6656]{2,1,0:T(8,128)}, u32[]{:S(2)}, u32[]{:S(2)}) %collective-permute-start) | collective-permute-done | bytes 1703968 | tf_op jit(solution)/shard_map/ppermute | solution.py:289
  16.9 3.1 %bitcast_add_fusion = (f32[16,6656]{1,0:T(8,128)}, f32[16,6656]{1,0:T(8,128)}, f32[16,6656]{1,0:T(8,128)}, f32[16,6656]{1,0:T(8,128)}) fusion(f32[4,16,6656]{2,1,0:T(8,128)} %collective-permute-done, s32[]{:T(128)S(6)} %select_n.83, f32[4,2,16,6656]{3,2,1,0:T(8,128)} %bitcast.33, s32[]{:T(128)S(6)} %select_n.84, s32[]{:T(128)S(6)} %select_n.74, ...), kind=kLoop, calls=%fused_computation.1 | loop fusion | flops 425984 | bytes 5111844 | tf_op jit(solution)/shard_map/add | solution.py:294
  24.0 3.6 %shard_map.102 = (f32[2,64,384]{2,1,0:T(8,128)}, f32[2,64,384]{2,1,0:T(8,128)}, f32[2,64,384]{2,1,0:T(8,128)}, f32[2,64,384]{2,1,0:T(8,128)}, f32[2,64,384]{2,1,...) custom-call(s32[2]{0:T(128)S(1)} %pad_add_fusion.refs_0_, ...), custom_call_target="tpu_custom_call" | custom-call | tf_op jit(solution)/shard_map/pallas_call | solution.py:258
  27.6 5.8 %collective-permute-done.1.refs_3_ = f32[16,6656]{1,0:T(8,128)} collective-permute-done((f32[16,6656]{1,0:T(8,128)}, f32[16,6656]{1,0:T(8,128)}, u32[]{:S(2)}, u32[]{:S(2)}) %collective-permute-start.1) | collective-permute-done | bytes 426016 | tf_op jit(solution)/shard_map/ppermute | solution.py:20
  33.4 7.7 %collective-permute-done.2.refs_4_ = f32[16,6656]{1,0:T(8,128)} collective-permute-done((f32[16,6656]{1,0:T(8,128)}, f32[16,6656]{1,0:T(8,128)}, u32[]{:S(2)}, u32[]{:S(2)}) %collective-permute-start.2) | collective-permute-done | bytes 426016 | tf_op jit(solution)/shard_map/ppermute | solution.py:20
  42.0 3.7 %shard_map.103 = (f32[16,6656]{1,0:T(8,128)}, f32[8,512]{1,0:T(8,128)}, f32[32,16,512]{2,1,0:T(8,128)}) custom-call(s32[2]{0:T(128)S(1)} %pad_add_fusion.refs_0_, s32[8,32]{1,0:T(8,128)S(1)} %bitcast.30, f32[16,6656]{1,0:T(8,128)} %get-tuple-element.163.refs_2_, f32[16,6656]{1,0:T(8,128)} %collective-permute-done.1.refs_3_, ...), custom_call_target="tpu_custom_call" | custom-call | tf_op jit(solution)/shard_map/pallas_call | solution.py:202
  45.7 10.3 %all-to-all-start = ((f32[32,16,512]{2,1,0:T(8,128)}), f32[32,16,512]{2,1,0:T(8,128)}, u32[]{:S(2)}, u32[]{:S(2)}) async-start(f32[32,16,512]{2,1,0:T(8,128)} %get-tuple-element.101), calls=%async_computation | async-start | bytes 2097152 | tf_op jit(solution)/shard_map/all_to_all | solution.py:322
  66.9 12.4 %collective-permute-done.5.refs_4_ = f32[2,64,384]{2,1,0:T(8,128)} collective-permute-done((f32[2,64,384]{2,1,0:T(8,128)}, f32[2,64,384]{2,1,0:T(8,128)}, u32[]{:S(2)}, u32[]{:S(2)}) %collective-permute-start.5) | collective-permute-done | bytes 196640 | tf_op jit(solution)/shard_map/ppermute | solution.py:20
  84.7 20.5 %all_to_all.20.refs_1_ = f32[8,4,16,512]{3,2,1,0:T(8,128)} all-to-all(f32[8,4,16,512]{3,2,1,0:T(8,128)} %bitcast.15), channel_id=1, replica_groups=mesh['fsdp'=32,'rep'=8] {'rep'}, dimensions={0} | all-to-all | bytes 2097152 | tf_op jit(solution)/shard_map/all_to_all | solution.py:331
  105.1 5.7 %shard_map.104 = f32[8,4,16,512]{3,2,1,0:T(8,128)} custom-call(s32[2]{0:T(128)S(1)} %pad_add_fusion.refs_0_, f32[8,4,16,512]{3,2,1,0:T(8,128)} %all_to_all.20.refs_1_, f32[2,64,384]{2,1,0:T(8,128)} %get-tuple-element.112.refs_2_, f32[2,64,384]{2,1,0:T(8,128)} %collective-permute-done.4.refs_3_, f32[2,64,384]{2,1,0:T(8,128)} %collective-permute-done.5.refs_4_, ...), custom_call_target="tpu_custom_call" | custom-call | tf_op jit(solution)/shard_map/pallas_call | solution.py:202
  110.8 5.2 %all-to-all-start.2 = ((f32[8,4,16,512]{3,2,1,0:T(8,128)}), f32[8,4,16,512]{3,2,1,0:T(8,128)}, u32[]{:S(2)}, u32[]{:S(2)}) async-start(f32[8,4,16,512]{3,2,1,0:T(8,128)} %shard_map.104), calls=%async_computation.2 | async-start | bytes 2097152 | tf_op jit(solution)/shard_map/all_to_all | solution.py:339
  124.2 5.1 %shard_map.105 = (f32[136,512]{1,0:T(8,128)}, f32[136,512]{1,0:T(8,128)}, f32[136,512]{1,0:T(8,128)}, f32[136,512]{1,0:T(8,128)}, f32[136,512]{1,0:T(8,128)}, /*...) custom-call(s32[2]{0:T(128)S(1)} %pad_add_fusion.refs_0_, f32[8,4,16,512]{3,2,1,0:T(8,128)} %all_to_all.20.refs_1_, ...), custom_call_target="tpu_custom_call" | custom-call | tf_op jit(solution)/shard_map/pallas_call | solution.py:202
  131.2 9.3 %all-to-all-start.3 = ((f32[32,16,512]{2,1,0:T(8,128)}), f32[32,16,512]{2,1,0:T(8,128)}, u32[]{:S(2)}, u32[]{:S(2)}) async-start(f32[32,16,512]{2,1,0:T(8,128)} %bitcast.16), calls=%async_computation.3 | async-start | bytes 2097152 | tf_op jit(solution)/shard_map/all_to_all | solution.py:349
  147.7 3.1 %collective-permute-start.18 = (f32[136,512]{1,0:T(8,128)}, f32[136,512]{1,0:T(8,128)}, u32[]{:S(2)}, u32[]{:S(2)}) collective-permute-start(f32[136,512]{1,0:T(8,128)} %get-tuple-element.136), channel_id=1, source_target_pairs={{0,5},{1,6},{2,7},{3,0},{4,1},{5,2},{6,3},{7,4},{8,13},{9,14},{10,... | collective-permute-start | bytes 835592 | tf_op jit(solution)/shard_map/ppermute | solution.py:20
  150.7 6.6 %collective-permute-done.15.refs_5_.refs_7_ = f32[136,512]{1,0:T(8,128)} collective-permute-done((f32[136,512]{1,0:T(8,128)}, f32[136,512]{1,0:T(8,128)}, u32[]{:S(2)}, u32[]{:S(2)}) %collective-permute-start.15) | collective-permute-done | bytes 278560 | tf_op jit(solution)/shard_map/ppermute | solution.py:20
  157.4 12.4 %collective-permute-done.16.refs_6_.refs_8_ = f32[136,512]{1,0:T(8,128)} collective-permute-done((f32[136,512]{1,0:T(8,128)}, f32[136,512]{1,0:T(8,128)}, u32[]{:S(2)}, u32[]{:S(2)}) %collective-permute-start.16) | collective-permute-done | bytes 278560 | tf_op jit(solution)/shard_map/ppermute | solution.py:20
  170.0 6.1 %collective-permute-done.20.refs_10_.refs_12_ = f32[136,512]{1,0:T(8,128)} collective-permute-done((f32[136,512]{1,0:T(8,128)}, f32[136,512]{1,0:T(8,128)}, u32[]{:S(2)}, u32[]{:S(2)}) %collective-permute-start.20) | collective-permute-done | bytes 278560 | tf_op jit(solution)/shard_map/ppermute | solution.py:20
  176.1 4.2 %shard_map.106 = (f32[16,3328]{1,0:T(8,128)}, f32[16,3328]{1,0:T(8,128)}) custom-call(s32[2]{0:T(128)S(1)} %pad_add_fusion.refs_0_, s32[8,32]{1,0:T(8,128)S(1)} %bitcast.31, f32[32,16,512]{2,1,0:T(8,128)} %all-to-all-done.3.refs_2_, f32[136,512]{1,0:T(8,128)} %get-tuple-element.140.refs_3_.refs_5_, f32[136,512]{1,0:T(8,128)} %collective-permute-done.14.refs_4_.refs_6_, ...), custom_call_target="tpu_custom_call" | custom-call | tf_op jit(solution)/shard_map/pallas_call | solution.py:202
  183.0 3.4 %collective-permute-done.21.refs_3_ = f32[16,3328]{1,0:T(8,128)S(1)} collective-permute-done((f32[16,3328]{1,0:T(8,128)}, f32[16,3328]{1,0:T(8,128)S(1)}, u32[]{:S(2)}, u32[]{:S(2)}) %collective-permute-start.21) | collective-permute-done | bytes 213024 | tf_op jit(solution)/shard_map/ppermute | solution.py:20
  194.8 2.9 %collective-permute-start.29 = (f32[16,3328]{1,0:T(8,128)}, f32[16,3328]{1,0:T(8,128)S(1)}, u32[]{:S(2)}, u32[]{:S(2)}) collective-permute-start(f32[16,3328]{1,0:T(8,128)} %get-tuple-element.149.refs_2_), channel_id=1, source_target_pairs={{0,1},{1,0},{2,3},{3,2},{4,5},{5,4},{6,7},{7,6},{8,9},{9,8},{10,11... | collective-permute-start | bytes 638984 | tf_op jit(solution)/shard_map/ppermute | solution.py:375
  198.0 6.7 %shard_map.107 = (f32[128,6656]{1,0:T(8,128)}, f32[8,64,512]{2,1,0:T(8,128)}, f32[8,64,512]{2,1,0:T(8,128)}) custom-call(s32[2]{0:T(128)S(1)} %pad_add_fusion.refs_0_, f32[64,6656]{1,0:T(8,128)} %all-gather.2.cloned.1.call-done.refs_1_, f32[64,6656]{1,0:T(8,128)} %collective-permute-done.27.refs_2_, f32[8,64,512]{2,1,0:T(8,128)} %bitcast.36, ...), custom_call_target="tpu_custom_call" | custom-call | tf_op jit(solution)/shard_map/pallas_call | solution.py:202
  208.6 4.5 %shard_map.108 = f32[128,6656]{1,0:T(8,128)} custom-call(s32[2]{0:T(128)S(1)} %pad_add_fusion.refs_0_, f32[16,3328]{1,0:T(8,128)} %get-tuple-element.148.refs_1_, f32[16,3328]{1,0:T(8,128)} %get-tuple-element.149.refs_2_, f32[16,3328]{1,0:T(8,128)} %copy-done.2, f32[16,3328]{1,0:T(8,128)} %copy-done.6, f32[16,3328]{1,0:T(8,128)} %copy-done.7, ...), custom_call_target="tpu_custom_call" | custom-call | tf_op jit(solution)/shard_map/pallas_call | solution.py:258
  (104 shorter events, 53.9 us)
Async XLA Ops:
  20.1 13.3 %collective-permute-start.1 = (f32[16,6656]{1,0:T(8,128)}, f32[16,6656]{1,0:T(8,128)}, u32[]{:S(2)}, u32[]{:S(2)}) collective-permute-start(f32[16,6656]{1,0:T(8,128)} %get-tuple-element.162), channel_id=1, source_target_pairs={{0,2},{1,3},{2,4},{3,5},{4,6},{5,7},{6,0},{7,1},{8,10},{9,11},{10,... | collective-permute-start | bytes 1277960 | tf_op jit(solution)/shard_map/ppermute | solution.py:20
  20.1 21.0 %collective-permute-start.2 = (f32[16,6656]{1,0:T(8,128)}, f32[16,6656]{1,0:T(8,128)}, u32[]{:S(2)}, u32[]{:S(2)}) collective-permute-start(f32[16,6656]{1,0:T(8,128)} %get-tuple-element.161), channel_id=1, source_target_pairs={{0,4},{1,5},{2,6},{3,7},{4,0},{5,1},{6,2},{7,3},{8,12},{9,13},{10,... | collective-permute-start | bytes 1277960 | tf_op jit(solution)/shard_map/ppermute | solution.py:20
  22.0 20.1 %collective-permute-start.3 = (f32[16,6656]{1,0:T(8,128)}, f32[16,6656]{1,0:T(8,128)}, u32[]{:S(2)}, u32[]{:S(2)}) collective-permute-start(f32[16,6656]{1,0:T(8,128)} %get-tuple-element.160), channel_id=1, source_target_pairs={{0,6},{1,7},{2,0},{3,1},{4,2},{5,3},{6,4},{7,5},{8,14},{9,15},{10,... | collective-permute-start | bytes 1277960 | tf_op jit(solution)/shard_map/ppermute | solution.py:20
  45.7 38.9 %all-to-all-start = ((f32[32,16,512]{2,1,0:T(8,128)}), f32[32,16,512]{2,1,0:T(8,128)}, u32[]{:S(2)}, u32[]{:S(2)}) async-start(f32[32,16,512]{2,1,0:T(8,128)} %get-tuple-element.101), calls=%async_computation | async-start | bytes 2097152 | tf_op jit(solution)/shard_map/all_to_all | solution.py:322
  56.1 73.3 %all-gather.2.cloned.1.call-start = ((), (), s32[]{:S(2)}) async-start(), calls=%async_computation.4 | async-start | bytes 2129920 | tf_op jit(solution)/shard_map/all_gather | solution.py:320
  59.3 20.1 %collective-permute-start.5 = (f32[2,64,384]{2,1,0:T(8,128)}, f32[2,64,384]{2,1,0:T(8,128)}, u32[]{:S(2)}, u32[]{:S(2)}) collective-permute-start(f32[2,64,384]{2,1,0:T(8,128)} %get-tuple-element.105), channel_id=1, source_target_pairs={{0,2},{1,3},{2,4},{3,5},{4,6},{5,7},{6,0},{7,1},{8,10},{9,11},{10,... | collective-permute-start | bytes 589832 | tf_op jit(solution)/shard_map/ppermute | solution.py:20
  60.3 21.7 %collective-permute-start.6 = (f32[2,64,384]{2,1,0:T(8,128)}, f32[2,64,384]{2,1,0:T(8,128)}, u32[]{:S(2)}, u32[]{:S(2)}) collective-permute-start(f32[2,64,384]{2,1,0:T(8,128)} %get-tuple-element.106), channel_id=1, source_target_pairs={{0,3},{1,4},{2,5},{3,6},{4,7},{5,0},{6,1},{7,2},{8,11},{9,12},{10,... | collective-permute-start | bytes 589832 | tf_op jit(solution)/shard_map/ppermute | solution.py:20
  62.1 19.8 %collective-permute-start.7 = (f32[2,64,384]{2,1,0:T(8,128)}, f32[2,64,384]{2,1,0:T(8,128)}, u32[]{:S(2)}, u32[]{:S(2)}) collective-permute-start(f32[2,64,384]{2,1,0:T(8,128)} %get-tuple-element.107), channel_id=1, source_target_pairs={{0,4},{1,5},{2,6},{3,7},{4,0},{5,1},{6,2},{7,3},{8,12},{9,13},{10,... | collective-permute-start | bytes 589832 | tf_op jit(solution)/shard_map/ppermute | solution.py:20
  63.6 19.2 %collective-permute-start.8 = (f32[2,64,384]{2,1,0:T(8,128)}, f32[2,64,384]{2,1,0:T(8,128)}, u32[]{:S(2)}, u32[]{:S(2)}) collective-permute-start(f32[2,64,384]{2,1,0:T(8,128)} %get-tuple-element.108), channel_id=1, source_target_pairs={{0,5},{1,6},{2,7},{3,0},{4,1},{5,2},{6,3},{7,4},{8,13},{9,14},{10,... | collective-permute-start | bytes 589832 | tf_op jit(solution)/shard_map/ppermute | solution.py:20
  66.3 18.4 %collective-permute-start.9 = (f32[2,64,384]{2,1,0:T(8,128)}, f32[2,64,384]{2,1,0:T(8,128)}, u32[]{:S(2)}, u32[]{:S(2)}) collective-permute-start(f32[2,64,384]{2,1,0:T(8,128)} %get-tuple-element.109), channel_id=1, source_target_pairs={{0,6},{1,7},{2,0},{3,1},{4,2},{5,3},{6,4},{7,5},{8,14},{9,15},{10,... | collective-permute-start | bytes 589832 | tf_op jit(solution)/shard_map/ppermute | solution.py:20
  110.8 20.4 %all-to-all-start.2 = ((f32[8,4,16,512]{3,2,1,0:T(8,128)}), f32[8,4,16,512]{3,2,1,0:T(8,128)}, u32[]{:S(2)}, u32[]{:S(2)}) async-start(f32[8,4,16,512]{3,2,1,0:T(8,128)} %shard_map.104), calls=%async_computation.2 | async-start | bytes 2097152 | tf_op jit(solution)/shard_map/all_to_all | solution.py:339
  131.2 44.8 %all-to-all-start.3 = ((f32[32,16,512]{2,1,0:T(8,128)}), f32[32,16,512]{2,1,0:T(8,128)}, u32[]{:S(2)}, u32[]{:S(2)}) async-start(f32[32,16,512]{2,1,0:T(8,128)} %bitcast.16), calls=%async_computation.3 | async-start | bytes 2097152 | tf_op jit(solution)/shard_map/all_to_all | solution.py:349
  140.5 52.2 %collective-permute-start.27 = (f32[64,6656]{1,0:T(8,128)}, f32[64,6656]{1,0:T(8,128)}, u32[]{:S(2)}, u32[]{:S(2)}) collective-permute-start(f32[64,6656]{1,0:T(8,128)} %all-gather.2.cloned.1.call-done.refs_1_), channel_id=1, source_target_pairs={{0,1},{1,0},{2,3},{3,2},{4,5},{5,4},{6,7},{7,6},{8,9},{9,8},{10,11... | collective-permute-start | bytes 5111816 | tf_op jit(solution)/shard_map/ppermute | solution.py:348
  142.0 15.4 %collective-permute-start.15 = (f32[136,512]{1,0:T(8,128)}, f32[136,512]{1,0:T(8,128)}, u32[]{:S(2)}, u32[]{:S(2)}) collective-permute-start(f32[136,512]{1,0:T(8,128)} %get-tuple-element.133), channel_id=1, source_target_pairs={{0,2},{1,3},{2,4},{3,5},{4,6},{5,7},{6,0},{7,1},{8,10},{9,11},{10,... | collective-permute-start | bytes 835592 | tf_op jit(solution)/shard_map/ppermute | solution.py:20
  142.0 27.7 %collective-permute-start.16 = (f32[136,512]{1,0:T(8,128)}, f32[136,512]{1,0:T(8,128)}, u32[]{:S(2)}, u32[]{:S(2)}) collective-permute-start(f32[136,512]{1,0:T(8,128)} %get-tuple-element.134), channel_id=1, source_target_pairs={{0,3},{1,4},{2,5},{3,6},{4,7},{5,0},{6,1},{7,2},{8,11},{9,12},{10,... | collective-permute-start | bytes 835592 | tf_op jit(solution)/shard_map/ppermute | solution.py:20
  144.5 25.3 %collective-permute-start.17 = (f32[136,512]{1,0:T(8,128)}, f32[136,512]{1,0:T(8,128)}, u32[]{:S(2)}, u32[]{:S(2)}) collective-permute-start(f32[136,512]{1,0:T(8,128)} %get-tuple-element.135), channel_id=1, source_target_pairs={{0,4},{1,5},{2,6},{3,7},{4,0},{5,1},{6,2},{7,3},{8,12},{9,13},{10,... | collective-permute-start | bytes 835592 | tf_op jit(solution)/shard_map/ppermute | solution.py:20
  147.7 22.1 %collective-permute-start.18 = (f32[136,512]{1,0:T(8,128)}, f32[136,512]{1,0:T(8,128)}, u32[]{:S(2)}, u32[]{:S(2)}) collective-permute-start(f32[136,512]{1,0:T(8,128)} %get-tuple-element.136), channel_id=1, source_target_pairs={{0,5},{1,6},{2,7},{3,0},{4,1},{5,2},{6,3},{7,4},{8,13},{9,14},{10,... | collective-permute-start | bytes 835592 | tf_op jit(solution)/shard_map/ppermute | solution.py:20
  157.4 12.6 %collective-permute-start.19 = (f32[136,512]{1,0:T(8,128)}, f32[136,512]{1,0:T(8,128)}, u32[]{:S(2)}, u32[]{:S(2)}) collective-permute-start(f32[136,512]{1,0:T(8,128)} %get-tuple-element.137), channel_id=1, source_target_pairs={{0,6},{1,7},{2,0},{3,1},{4,2},{5,3},{6,4},{7,5},{8,14},{9,15},{10,... | collective-permute-start | bytes 835592 | tf_op jit(solution)/shard_map/ppermute | solution.py:20
  187.5 10.1 %collective-permute-start.26 = (f32[16,3328]{1,0:T(8,128)S(1)}, f32[16,3328]{1,0:T(8,128)S(1)}, u32[]{:S(2)}, u32[]{:S(2)}) collective-permute-start(f32[16,3328]{1,0:T(8,128)S(1)} %collective-permute-done.22.refs_6_), channel_id=1, source_target_pairs={{0,6},{1,7},{2,0},{3,1},{4,2},{5,3},{6,4},{7,5},{8,14},{9,15},{10,... | collective-permute-start | bytes 638984 | tf_op jit(solution)/shard_map/ppermute | solution.py:20
  190.0 14.7 %collective-permute-start.23 = (f32[16,3328]{1,0:T(8,128)}, f32[16,3328]{1,0:T(8,128)S(1)}, u32[]{:S(2)}, u32[]{:S(2)}) collective-permute-start(f32[16,3328]{1,0:T(8,128)} %get-tuple-element.149.refs_2_), channel_id=1, source_target_pairs={{0,2},{1,3},{2,4},{3,5},{4,6},{5,7},{6,0},{7,1},{8,10},{9,11},{10,... | collective-permute-start | bytes 638984 | tf_op jit(solution)/shard_map/ppermute | solution.py:20
  190.0 15.1 %collective-permute-start.24 = (f32[16,3328]{1,0:T(8,128)}, f32[16,3328]{1,0:T(8,128)S(1)}, u32[]{:S(2)}, u32[]{:S(2)}) collective-permute-start(f32[16,3328]{1,0:T(8,128)} %get-tuple-element.148.refs_1_), channel_id=1, source_target_pairs={{0,6},{1,7},{2,0},{3,1},{4,2},{5,3},{6,4},{7,5},{8,14},{9,15},{10,... | collective-permute-start | bytes 638984 | tf_op jit(solution)/shard_map/ppermute | solution.py:20
  192.7 12.7 %collective-permute-start.28 = (f32[16,3328]{1,0:T(8,128)}, f32[16,3328]{1,0:T(8,128)S(1)}, u32[]{:S(2)}, u32[]{:S(2)}) collective-permute-start(f32[16,3328]{1,0:T(8,128)} %get-tuple-element.148.refs_1_), channel_id=1, source_target_pairs={{0,1},{1,0},{2,3},{3,2},{4,5},{5,4},{6,7},{7,6},{8,9},{9,8},{10,11... | collective-permute-start | bytes 638984 | tf_op jit(solution)/shard_map/ppermute | solution.py:375
  194.8 10.8 %collective-permute-start.29 = (f32[16,3328]{1,0:T(8,128)}, f32[16,3328]{1,0:T(8,128)S(1)}, u32[]{:S(2)}, u32[]{:S(2)}) collective-permute-start(f32[16,3328]{1,0:T(8,128)} %get-tuple-element.149.refs_2_), channel_id=1, source_target_pairs={{0,1},{1,0},{2,3},{3,2},{4,5},{5,4},{6,7},{7,6},{8,9},{9,8},{10,11... | collective-permute-start | bytes 638984 | tf_op jit(solution)/shard_map/ppermute | solution.py:375
  197.7 8.3 %collective-permute-start.30 = (f32[16,3328]{1,0:T(8,128)S(1)}, f32[16,3328]{1,0:T(8,128)S(1)}, u32[]{:S(2)}, u32[]{:S(2)}) collective-permute-start(f32[16,3328]{1,0:T(8,128)S(1)} %collective-permute-done.21.refs_3_), channel_id=1, source_target_pairs={{0,1},{1,0},{2,3},{3,2},{4,5},{5,4},{6,7},{7,6},{8,9},{9,8},{10,11... | collective-permute-start | bytes 638984 | tf_op jit(solution)/shard_map/ppermute | solution.py:375
  (33 other events, 199.9 us)
Sparse Core Ops, SparseCore 0:
  59.3 36.1 all-gather.1

commit v3 on v2

--- a/solution.py
+++ b/solution.py
@@ -71,13 +71,12 @@
             high[at : at + rows, :], low[at : at + rows, :] = split(blocks[r, i])
 
 
-def apply_kernel(ids, blocks, *refs):
+def root_kernel(ids, *refs):
     roots = refs[:8]
-    applied, gh, gl, left, right, whole = refs[8:]
-    count, side = 8, whole.shape[0]
+    lh, ll, rh, rl, left, right = refs[8:]
+    count, side = 8, left.shape[0]
     share = side // count
     part = side // 4
-    load_block(blocks, gh, gl)
     for k in range(count):
         other = lax.rem(ids[0] - k + count, count)
         start = pl.multiple_of(other * share, share)
@@ -91,8 +90,14 @@
         at, to = slice(x * part, (x + 1) * part), slice(before * part, (before + 1) * part)
         left[at, to] = left[to, at].T
         right[at, to] = right[to, at].T
-    product = dot3((gh[...], gl[...]), split(right[...]), ((1,), (0,)))
-    value = dot3(split(left[...]), split(product), ((1,), (0,)))
+    lh[...], ll[...] = split(left[...])
+    rh[...], rl[...] = split(right[...])
+
+
+def apply_kernel(blocks, lh, ll, rh, rl, applied, gh, gl, whole):
+    load_block(blocks, gh, gl)
+    product = dot3((gh[...], gl[...]), (rh[...], rl[...]), ((1,), (0,)))
+    value = dot3((lh[...], ll[...]), split(product), ((1,), (0,)))
     whole[...] = value
     norm = jnp.sqrt(jnp.sum(value * value, keepdims=True))
     scale = 1.0 / (norm + NORM_EPS)
@@ -141,13 +146,12 @@
 
 def direction_kernel(ids, owner_cols, returned, *refs):
     grams = refs[:8]
-    low, high, direction, norms = refs[8:]
-    tail = grams[0].shape[0] - 8
+    direction, norms = refs[8:]
     row = ids[1]
     width = returned.shape[-1]
-    total = grams[0][tail:, :]
+    total = grams[0][...]
     for k in range(1, 8):
-        total = total + grams[k][tail:, :]
+        total = total + grams[k][...]
     for c in range(direction.shape[-1] // width):
         lane = (c // 8) * 128
         lanes = total[c % 8 : c % 8 + 1, lane : lane + 128]
@@ -162,18 +166,17 @@
             start = pl.multiple_of(col * width, width)
             direction[:, pl.ds(start, width)] = returned[o] * norm
 
-    middle = low.shape[1]
-    low[...] = direction[:, :middle]
-    high[...] = direction[:, middle:]
-
-
-def staged(kernel, n_small, n_in, n_out, *refs):
+
+def staged(kernel, cuts, n_small, n_in, n_out, *refs):
     cut = [n_small, n_in, n_out, n_in, n_out]
     groups, at = [], 0
     for size in cut:
         groups.append(refs[at : at + size])
         at += size
     small, sources, targets, ins, outs = groups
+    sources = [
+        src if cut is None else src.at[pl.ds(*cut), :] for src, cut in zip(sources, cuts)
+    ]
     in_sems, out_sems = refs[at : at + 2]
     loads = [
         pltpu.make_async_copy(src, dst, in_sems.at[i])
@@ -194,14 +197,19 @@
         store.wait()
 
 
-def call(kernel, outs, small, ins, scratch):
+def call(kernel, outs, small, ins, scratch, cuts=None, dtype=F32):
     hbm = pl.BlockSpec(memory_space=pltpu.HBM)
     smem = pl.BlockSpec(memory_space=pltpu.SMEM)
-    held = [pltpu.VMEM(x.shape, F32) for x in ins] + [pltpu.VMEM(s, F32) for s in outs]
+    cuts = cuts or [None] * len(ins)
+    held = [
+        pltpu.VMEM(x.shape if cut is None else (cut[1], *x.shape[1:]), x.dtype)
+        for x, cut in zip(ins, cuts)
+    ]
+    held = held + [pltpu.VMEM(s, dtype) for s in outs]
     sems = [pltpu.SemaphoreType.DMA((len(ins),)), pltpu.SemaphoreType.DMA((len(outs),))]
     return pl.pallas_call(
-        functools.partial(staged, kernel, len(small), len(ins), len(outs)),
-        out_shape=[pltpu.HBM(shape, F32) for shape in outs],
+        functools.partial(staged, kernel, cuts, len(small), len(ins), len(outs)),
+        out_shape=[pltpu.HBM(shape, dtype) for shape in outs],
         in_specs=[smem] * len(small) + [hbm] * len(ins),
         out_specs=[hbm] * len(outs),
         scratch_shapes=held + sems + scratch,
@@ -223,17 +231,15 @@
 
 
 def place_plan(ids, ins, outs):
-    chip, core = ids[0] // 2, ids[0] % 2
-    rows, middle = ins[0].shape
-    for j, piece in enumerate(ins):
-        owner = core if j < 8 else 1 - core
-        from_chip = lax.rem(chip + (0, 3, 1, 2)[j % 8 // 2], 4)
-        start = pl.multiple_of((from_chip * 2 + owner) * rows, rows)
-        columns = slice(j % 2 * middle, (j % 2 + 1) * middle)
-        yield piece, outs[0].at[pl.ds(start, rows), columns]
-
-
-def copying(plan, n_small, n_in, n_out, *refs):
+    core = ids[0] % 2
+    rows = ins[0].shape[0] // 4
+    for x in range(4):
+        for piece, owner in zip(ins, (core, 1 - core)):
+            start = pl.multiple_of((x * 2 + owner) * rows, rows)
+            yield piece.at[pl.ds(x * rows, rows), :], outs[0].at[pl.ds(start, rows), :]
+
+
+def copying(plan, split_stores, n_small, n_in, n_out, *refs):
     small, ins = refs[:n_small], refs[n_small : n_small + n_in]
     outs = refs[n_small + n_in : n_small + n_in + n_out]
     held, (sems, out_sems) = refs[n_small + n_in + n_out : -2], refs[-2:]
@@ -241,27 +247,36 @@
         pltpu.make_async_copy(src, dst, sems.at[i])
         for i, (src, dst) in enumerate(plan(*small, ins, held))
     ]
+    pairs = zip(held, outs)
+    if split_stores:
+        landed = [dst for _, dst in plan(*small, ins, held)]
+        pairs = zip(landed, [dst for _, dst in plan(*small, ins, outs)])
     stores = [
-        pltpu.make_async_copy(src, dst, out_sems.at[i])
-        for i, (src, dst) in enumerate(zip(held, outs))
-    ]
-    for copies in (loads, stores):
-        for copy in copies:
-            copy.start()
-        for copy in copies:
-            copy.wait()
-
-
-def shuffle(plan, outs, small, ins, count):
+        pltpu.make_async_copy(src, dst, out_sems.at[i]) for i, (src, dst) in enumerate(pairs)
+    ]
+    for load in loads:
+        load.start()
+    for i, load in enumerate(loads):
+        load.wait()
+        if split_stores:
+            stores[i].start()
+    if not split_stores:
+        for store in stores:
+            store.start()
+    for store in stores:
+        store.wait()
+
+
+def shuffle(plan, outs, small, ins, count, split_stores=False):
     hbm = pl.BlockSpec(memory_space=pltpu.HBM)
     smem = pl.BlockSpec(memory_space=pltpu.SMEM)
     return pl.pallas_call(
-        functools.partial(copying, plan, len(small), len(ins), len(outs)),
+        functools.partial(copying, plan, split_stores, len(small), len(ins), len(outs)),
         out_shape=[pltpu.HBM(shape, F32) for shape in outs],
         in_specs=[smem] * len(small) + [hbm] * len(ins),
         out_specs=[hbm] * len(outs),
         scratch_shapes=[pltpu.VMEM(shape, F32) for shape in outs]
-        + [pltpu.SemaphoreType.DMA((count,)), pltpu.SemaphoreType.DMA((len(outs),))],
+        + [pltpu.SemaphoreType.DMA((count,))] * 2,
         compiler_params=PARAMS,
     )(*small, *[pltpu.with_memory_space_constraint(x, pltpu.HBM) for x in ins])
 
@@ -333,8 +348,11 @@
     )
     half = pltpu.VMEM((side, side), BF16)
     full = pltpu.VMEM((side, side), F32)
+    halves = call(
+        root_kernel, [(side, side)] * 4, [ids], roots, [full] * 2, dtype=BF16
+    )
     (applied,) = call(
-        apply_kernel, [blocks.shape], [ids], [blocks, *roots], [half] * 2 + [full] * 3
+        apply_kernel, [blocks.shape], [], [blocks, *halves], [half] * 2 + [full]
     )
     spread = lax.all_to_all(applied, "rep", 0, 0, tiled=True)
     grams = call(
@@ -349,19 +367,17 @@
     returned = lax.all_to_all(spread.reshape(owners, rows, side), "fsdp", 0, 0, tiled=True)
     grams = [g if k == 0 else rep_shift(g, k, reps) for k, g in enumerate(grams)]
     returned, *grams = barrier((returned, *grams))
-    middle = full_width // 2
-    low, high = call(
+    tails = (2 * share, 8)
+    (part,) = call(
         direction_kernel,
-        [(rows, middle)] * 2,
+        [strip],
         [ids, oc],
         [returned, *grams],
-        [pltpu.VMEM(strip, F32), pltpu.VMEM((16, 128), F32)],
-    )
-    left_low = rep_shift(low, 2, reps)
-    right_high = rep_shift(high, reps - 2, reps)
-    left_high = rep_shift(high, 2, reps)
-    right_low = rep_shift(low, reps - 2, reps)
-    last_ids, left_low, right_high = barrier((ids, left_low, right_high))
+        [pltpu.VMEM((16, 128), F32)],
+        [None] + [tails] * reps,
+    )
+    line = lax.all_gather(part, "rep", axis=0, tiled=True, axis_index_groups=lines)
+    last_ids, part = barrier((ids, part))
     moment_new, left_new, right_new = call(
         stat_kernel,
         [(shard_rows, full_width), stats, stats],
@@ -369,19 +385,14 @@
         [moment_line, moment_swap, stat_left[0, 0], stat_right[0, 0], *grams],
         [],
     )
-    far_low = rep_shift(left_low, 2, reps)
-    far_high = rep_shift(right_high, reps - 2, reps)
-    found = [low, high, left_low, left_high, right_low, right_high]
-    swapped = [lax.ppermute(x, "rep", swap) for x in found]
-    far_low, far_high, left_new = barrier((far_low, far_high, left_new))
-    far = [far_low, far_high]
-    far_swapped = [lax.ppermute(x, "rep", swap) for x in far]
+    line, left_new = barrier((line, left_new))
     (direction,) = shuffle(
         place_plan,
         [(shard_rows, full_width)],
         [ids],
-        [*found, *far, *swapped, *far_swapped],
-        16,
+        [line, lax.ppermute(line, "rep", swap)],
+        2 * chips,
+        True,
     )
     return (direction, moment_new, left_new[None, None], right_new[None, None])
 

time: 221 us -> 220 us (level)
  waiting for transfers between devices: 75.4 us -> 99.8 us
  blocking collectives: 20.5 us -> 0 us
  starting transfers between devices: 67.9 us -> 60.3 us
    all_to_all x1 -> x0, blocking collectives: 20.5 us -> none  [shards(): lax.all_to_all(arrived.reshape(block_rows, quarters, rows, side), 'rep',...]
    all_gather x0 -> x1, waiting for transfers between devices: none -> 18.8 us  [shards(): lax.all_gather(part, 'rep', axis=0, tiled=True, axis_index_groups=lines)]
    ppermute x23 -> x17, waiting for transfers between devices: 63.8 us -> 52.2 us  [rep_shift(): lax.ppermute(value, 'rep', [(i, (i + step) % count) for i in range(count)])]
    all_to_all x0 -> x1, waiting for transfers between devices: none -> 11.3 us  [shards(): lax.all_to_all(arrived.reshape(block_rows, quarters, rows, side), 'rep',...]
    ppermute x8 -> x1, starting transfers between devices: 6.77 us -> 0.67 us  [shards(): lax.ppermute(line, 'rep', swap)]
    ppermute x23 -> x17, starting transfers between devices: 28.3 us -> 23.1 us  [rep_shift(): lax.ppermute(value, 'rep', [(i, (i + step) % count) for i in range(count)])]
    all_to_all x0 -> x1, starting transfers between devices: none -> 5.08 us  [shards(): lax.all_to_all(arrived.reshape(block_rows, quarters, rows, side), 'rep',...]
    ppermute x1, waiting for transfers between devices: 0.01 us -> 3.8 us  [shards(): moment_swap = lax.ppermute(moment_line, 'rep', swap)]
  transfers between devices with their start and end apart: 40 -> 29, of which waited for: 23 -> 19; matrix products, arithmetic and copies ran while one was open for 1% -> 1% of each run, Pallas kernels for 11% -> 11%
where the time goes in v3:
time: 220 us
  waiting for transfers between devices  99.8 us (45%)
  starting transfers between devices  60.3 us (27%)
  Pallas kernels  35.3 us (16%)
  between operations  14.2 us (6%)
  local copies, waits for them, and re-layouts  6.14 us (3%)
  other arithmetic  3.81 us (2%)
    ppermute x17, waiting for transfers between devices, rep_shift(): lax.ppermute(value, 'rep', [(i, (i + step) % count) for i in range(count)])  52.2 us
    pallas_call x6, Pallas kernels, call(): pl.pallas_call(functools.partial(staged, kernel, cuts, len(small), len(in...  27.9 us
    ppermute x17, starting transfers between devices, rep_shift(): lax.ppermute(value, 'rep', [(i, (i + step) % count) for i in range(count)])  23.1 us
    all_gather x1, waiting for transfers between devices, shards(): lax.all_gather(part, 'rep', axis=0, tiled=True, axis_index_groups=lines)  18.8 us
    all_to_all x1, waiting for transfers between devices, shards(): lax.all_to_all(arrived.reshape(block_rows, quarters, rows, side), 'rep',...  11.3 us
    all_to_all x1, starting transfers between devices, shards(): arrived = lax.all_to_all(packed, 'fsdp', 0, 0, tiled=True)  10.3 us
    all_to_all x1, starting transfers between devices, shards(): lax.all_to_all(spread.reshape(owners, rows, side), 'fsdp', 0, 0, tiled=True)  9.22 us
    pallas_call x2, Pallas kernels, shuffle(): pl.pallas_call(functools.partial(copying, plan, split_stores, len(small),...  7.35 us
  transfers between devices with their start and end apart: 29, of which 19 were waited for; matrix products, arithmetic and copies ran while one was open for 1% of the time, Pallas kernels for 11%

profile of v3, /device:TPU:1, one launch (start us, length us, event | category | flops | bytes accessed | tf_op | source)
XLA Modules:
  0.0 219.5 jit_solution(11677917208825795326)
XLA Ops:
  10.1 3.2 %collective-permute-start = (f32[4,16,6656]{2,1,0:T(8,128)}, f32[4,16,6656]{2,1,0:T(8,128)}, u32[]{:S(2)}, u32[]{:S(2)}) collective-permute-start(f32[4,16,6656]{2,1,0:T(8,128)} %dynamic-slice_bitcast_fusion), channel_id=1, source_target_pairs={{0,1},{1,0},{2,3},{3,2},{4,5},{5,4},{6,7},{7,6},{8,9},{9,8},{10,11... | collective-permute-start | bytes 5111816 | tf_op jit(solution)/shard_map/ppermute | solution.py:304
  13.4 3.6 %collective-permute-done = f32[4,16,6656]{2,1,0:T(8,128)} collective-permute-done((f32[4,16,6656]{2,1,0:T(8,128)}, f32[4,16,6656]{2,1,0:T(8,128)}, u32[]{:S(2)}, u32[]{:S(2)}) %collective-permute-start) | collective-permute-done | bytes 1703968 | tf_op jit(solution)/shard_map/ppermute | solution.py:304
  16.9 3.1 %bitcast_add_fusion = (f32[16,6656]{1,0:T(8,128)}, f32[16,6656]{1,0:T(8,128)}, f32[16,6656]{1,0:T(8,128)}, f32[16,6656]{1,0:T(8,128)}) fusion(f32[4,16,6656]{2,1,0:T(8,128)} %collective-permute-done, s32[]{:T(128)S(6)} %select_n.83, f32[4,2,16,6656]{3,2,1,0:T(8,128)} %bitcast.33, s32[]{:T(128)S(6)} %select_n.84, s32[]{:T(128)S(6)} %select_n.74, ...), kind=kLoop, calls=%fused_computation.1 | loop fusion | flops 425984 | bytes 5111844 | tf_op jit(solution)/shard_map/add | solution.py:309
  24.0 3.9 %shard_map.102 = (f32[2,64,384]{2,1,0:T(8,128)}, f32[2,64,384]{2,1,0:T(8,128)}, f32[2,64,384]{2,1,0:T(8,128)}, f32[2,64,384]{2,1,0:T(8,128)}, f32[2,64,384]{2,1,...) custom-call(s32[2]{0:T(128)S(1)} %pad_add_fusion.refs_0_, ...), custom_call_target="tpu_custom_call" | custom-call | tf_op jit(solution)/shard_map/pallas_call | solution.py:273
  27.9 5.4 %collective-permute-done.1.refs_3_ = f32[16,6656]{1,0:T(8,128)} collective-permute-done((f32[16,6656]{1,0:T(8,128)}, f32[16,6656]{1,0:T(8,128)}, u32[]{:S(2)}, u32[]{:S(2)}) %collective-permute-start.1) | collective-permute-done | bytes 426016 | tf_op jit(solution)/shard_map/ppermute | solution.py:20
  33.4 7.7 %collective-permute-done.2.refs_4_ = f32[16,6656]{1,0:T(8,128)} collective-permute-done((f32[16,6656]{1,0:T(8,128)}, f32[16,6656]{1,0:T(8,128)}, u32[]{:S(2)}, u32[]{:S(2)}) %collective-permute-start.2) | collective-permute-done | bytes 426016 | tf_op jit(solution)/shard_map/ppermute | solution.py:20
  42.0 3.7 %shard_map.103 = (f32[16,6656]{1,0:T(8,128)}, f32[8,512]{1,0:T(8,128)}, f32[32,16,512]{2,1,0:T(8,128)}) custom-call(s32[2]{0:T(128)S(1)} %pad_add_fusion.refs_0_, s32[8,32]{1,0:T(8,128)S(1)} %bitcast.30, f32[16,6656]{1,0:T(8,128)} %get-tuple-element.161.refs_2_, f32[16,6656]{1,0:T(8,128)} %collective-permute-done.1.refs_3_, ...), custom_call_target="tpu_custom_call" | custom-call | tf_op jit(solution)/shard_map/pallas_call | solution.py:210
  45.7 10.3 %all-to-all-start = ((f32[32,16,512]{2,1,0:T(8,128)}), f32[32,16,512]{2,1,0:T(8,128)}, u32[]{:S(2)}, u32[]{:S(2)}) async-start(f32[32,16,512]{2,1,0:T(8,128)} %get-tuple-element.100), calls=%async_computation | async-start | bytes 2097152 | tf_op jit(solution)/shard_map/all_to_all | solution.py:337
  66.9 11.9 %collective-permute-done.5.refs_3_ = f32[2,64,384]{2,1,0:T(8,128)} collective-permute-done((f32[2,64,384]{2,1,0:T(8,128)}, f32[2,64,384]{2,1,0:T(8,128)}, u32[]{:S(2)}, u32[]{:S(2)}) %collective-permute-start.5) | collective-permute-done | bytes 196640 | tf_op jit(solution)/shard_map/ppermute | solution.py:20
  85.1 5.1 %all-to-all-start.1 = ((f32[8,4,16,512]{3,2,1,0:T(8,128)}), f32[8,4,16,512]{3,2,1,0:T(8,128)}, u32[]{:S(2)}, u32[]{:S(2)}) async-start(f32[8,4,16,512]{3,2,1,0:T(8,128)} %bitcast.15), calls=%async_computation.1 | async-start | bytes 2097152 | tf_op jit(solution)/shard_map/all_to_all | solution.py:346
  90.2 3.9 %shard_map.104 = (bf16[512,512]{1,0:T(8,128)(2,1)}, bf16[512,512]{1,0:T(8,128)(2,1)}, bf16[512,512]{1,0:T(8,128)(2,1)}, bf16[512,512]{1,0:T(8,128)(2,1)}) custom-call(s32[2]{0:T(128)S(1)} %pad_add_fusion.refs_0_, f32[2,64,384]{2,1,0:T(8,128)} %get-tuple-element.111.refs_1_, f32[2,64,384]{2,1,0:T(8,128)} %collective-permute-done.4.refs_2_, ...), custom_call_target="tpu_custom_call" | custom-call | tf_op jit(solution)/shard_map/pallas_call | solution.py:210
  94.1 11.3 %all-to-all-done.1.refs_0_.refs_1_ = f32[8,4,16,512]{3,2,1,0:T(8,128)} async-done(((f32[8,4,16,512]{3,2,1,0:T(8,128)}), f32[8,4,16,512]{3,2,1,0:T(8,128)}, u32[]{:S(2)}, u32[]{:S(2)}) %all-to-all-start.1) | async-done | bytes 1048608 | tf_op jit(solution)/shard_map/all_to_all | solution.py:346
  105.4 5.0 %shard_map.105 = f32[8,4,16,512]{3,2,1,0:T(8,128)} custom-call(f32[8,4,16,512]{3,2,1,0:T(8,128)} %all-to-all-done.1.refs_0_.refs_1_, bf16[512,512]{1,0:T(8,128)(2,1)} %get-tuple-element.119.refs_1_, bf16[512,512]{1,0:T(8,128)(2,1)} %get-tuple-element.120.refs_2_, bf16[512,512]{1,0:T(8,128)(2,1)} %get-tuple-element.121.refs_3_, ...), custom_call_target="tpu_custom_call" | custom-call | tf_op jit(solution)/shard_map/pallas_call | solution.py:210
  110.4 5.0 %all-to-all-start.2 = ((f32[8,4,16,512]{3,2,1,0:T(8,128)}), f32[8,4,16,512]{3,2,1,0:T(8,128)}, u32[]{:S(2)}, u32[]{:S(2)}) async-start(f32[8,4,16,512]{3,2,1,0:T(8,128)} %shard_map.105), calls=%async_computation.2 | async-start | bytes 2097152 | tf_op jit(solution)/shard_map/all_to_all | solution.py:357
  123.6 5.0 %shard_map.106 = (f32[136,512]{1,0:T(8,128)}, f32[136,512]{1,0:T(8,128)}, f32[136,512]{1,0:T(8,128)}, f32[136,512]{1,0:T(8,128)}, f32[136,512]{1,0:T(8,128)}, /*...) custom-call(s32[2]{0:T(128)S(1)} %pad_add_fusion.refs_0_, ...), custom_call_target="tpu_custom_call" | custom-call | tf_op jit(solution)/shard_map/pallas_call | solution.py:210
  130.7 9.2 %all-to-all-start.3 = ((f32[32,16,512]{2,1,0:T(8,128)}), f32[32,16,512]{2,1,0:T(8,128)}, u32[]{:S(2)}, u32[]{:S(2)}) async-start(f32[32,16,512]{2,1,0:T(8,128)} %bitcast.16), calls=%async_computation.3 | async-start | bytes 2097152 | tf_op jit(solution)/shard_map/all_to_all | solution.py:367
  149.8 7.3 %collective-permute-done.15.refs_5_.refs_7_ = f32[136,512]{1,0:T(8,128)} collective-permute-done((f32[136,512]{1,0:T(8,128)}, f32[136,512]{1,0:T(8,128)}, u32[]{:S(2)}, u32[]{:S(2)}) %collective-permute-start.15) | collective-permute-done | bytes 278560 | tf_op jit(solution)/shard_map/ppermute | solution.py:20
  157.2 11.9 %collective-permute-done.16.refs_6_.refs_8_ = f32[136,512]{1,0:T(8,128)} collective-permute-done((f32[136,512]{1,0:T(8,128)}, f32[136,512]{1,0:T(8,128)}, u32[]{:S(2)}, u32[]{:S(2)}) %collective-permute-start.16) | collective-permute-done | bytes 278560 | tf_op jit(solution)/shard_map/ppermute | solution.py:20
  169.8 3.5 %shard_map.107 = f32[16,6656]{1,0:T(8,128)} custom-call(s32[2]{0:T(128)S(1)} %pad_add_fusion.refs_0_, s32[8,32]{1,0:T(8,128)S(1)} %bitcast.31, f32[32,16,512]{2,1,0:T(8,128)} %all-to-all-done.3.refs_2_, f32[136,512]{1,0:T(8,128)} %get-tuple-element.143.refs_3_.refs_5_, f32[136,512]{1,0:T(8,128)} %collective-permute-done.14.refs_4_.refs_6_, ...), custom_call_target="tpu_custom_call" | custom-call | tf_op jit(solution)/shard_map/pallas_call | solution.py:210
  173.5 3.8 %collective-permute-done.21.refs_2_ = f32[64,6656]{1,0:T(8,128)S(1)} collective-permute-done((f32[64,6656]{1,0:T(8,128)}, f32[64,6656]{1,0:T(8,128)S(1)}, u32[]{:S(2)}, u32[]{:S(2)}) %collective-permute-start.21) | collective-permute-done | bytes 1703968 | tf_op jit(solution)/shard_map/ppermute | solution.py:366
  178.4 6.7 %shard_map.108 = (f32[128,6656]{1,0:T(8,128)}, f32[8,64,512]{2,1,0:T(8,128)}, f32[8,64,512]{2,1,0:T(8,128)}) custom-call(s32[2]{0:T(128)S(1)} %pad_add_fusion.refs_0_, f32[64,6656]{1,0:T(8,128)} %all-gather.3.cloned.1.call-done.refs_1_, f32[64,6656]{1,0:T(8,128)} %copy-done.3, f32[8,64,512]{2,1,0:T(8,128)} %bitcast.36, f32[8,64,512]{2,1,0:T(8,128)} %bitcast.37, ...), custom_call_target="tpu_custom_call" | custom-call | tf_op jit(solution)/shard_map/pallas_call | solution.py:210
  185.2 18.8 %all-gather.5.cloned.1.call-done.refs_1_ = f32[64,6656]{1,0:T(8,128)} async-done(((f32[16,6656]{1,0:T(8,128)}), f32[64,6656]{1,0:T(8,128)}) %all-gather.5.cloned.1.call-update) | async-done | bytes 1703952 | tf_op jit(solution)/shard_map/all_gather | solution.py:379
  204.6 3.4 %collective-permute-done.22.refs_2_ = f32[64,6656]{1,0:T(8,128)S(1)} collective-permute-done((f32[64,6656]{1,0:T(8,128)}, f32[64,6656]{1,0:T(8,128)S(1)}, u32[]{:S(2)}, u32[]{:S(2)}) %collective-permute-start.22) | collective-permute-done | bytes 1703968 | tf_op jit(solution)/shard_map/ppermute | solution.py:393
  209.3 3.4 %shard_map.109 = f32[128,6656]{1,0:T(8,128)} custom-call(s32[2]{0:T(128)S(1)} %pad_add_fusion.refs_0_, f32[64,6656]{1,0:T(8,128)} %all-gather.5.cloned.1.call-done.refs_1_, f32[64,6656]{1,0:T(8,128)} %copy-done.2), custom_call_target="tpu_custom_call" | custom-call | tf_op jit(solution)/shard_map/pallas_call | solution.py:273
  (59 shorter events, 49.0 us)
Async XLA Ops:
  10.1 6.8 %collective-permute-start = (f32[4,16,6656]{2,1,0:T(8,128)}, f32[4,16,6656]{2,1,0:T(8,128)}, u32[]{:S(2)}, u32[]{:S(2)}) collective-permute-start(f32[4,16,6656]{2,1,0:T(8,128)} %dynamic-slice_bitcast_fusion), channel_id=1, source_target_pairs={{0,1},{1,0},{2,3},{3,2},{4,5},{5,4},{6,7},{7,6},{8,9},{9,8},{10,11... | collective-permute-start | bytes 5111816 | tf_op jit(solution)/shard_map/ppermute | solution.py:304
  20.1 13.3 %collective-permute-start.1 = (f32[16,6656]{1,0:T(8,128)}, f32[16,6656]{1,0:T(8,128)}, u32[]{:S(2)}, u32[]{:S(2)}) collective-permute-start(f32[16,6656]{1,0:T(8,128)} %get-tuple-element.160), channel_id=1, source_target_pairs={{0,2},{1,3},{2,4},{3,5},{4,6},{5,7},{6,0},{7,1},{8,10},{9,11},{10,... | collective-permute-start | bytes 1277960 | tf_op jit(solution)/shard_map/ppermute | solution.py:20
  20.1 21.0 %collective-permute-start.2 = (f32[16,6656]{1,0:T(8,128)}, f32[16,6656]{1,0:T(8,128)}, u32[]{:S(2)}, u32[]{:S(2)}) collective-permute-start(f32[16,6656]{1,0:T(8,128)} %get-tuple-element.159), channel_id=1, source_target_pairs={{0,4},{1,5},{2,6},{3,7},{4,0},{5,1},{6,2},{7,3},{8,12},{9,13},{10,... | collective-permute-start | bytes 1277960 | tf_op jit(solution)/shard_map/ppermute | solution.py:20
  22.0 20.1 %collective-permute-start.3 = (f32[16,6656]{1,0:T(8,128)}, f32[16,6656]{1,0:T(8,128)}, u32[]{:S(2)}, u32[]{:S(2)}) collective-permute-start(f32[16,6656]{1,0:T(8,128)} %get-tuple-element.158), channel_id=1, source_target_pairs={{0,6},{1,7},{2,0},{3,1},{4,2},{5,3},{6,4},{7,5},{8,14},{9,15},{10,... | collective-permute-start | bytes 1277960 | tf_op jit(solution)/shard_map/ppermute | solution.py:20
  45.7 39.3 %all-to-all-start = ((f32[32,16,512]{2,1,0:T(8,128)}), f32[32,16,512]{2,1,0:T(8,128)}, u32[]{:S(2)}, u32[]{:S(2)}) async-start(f32[32,16,512]{2,1,0:T(8,128)} %get-tuple-element.100), calls=%async_computation | async-start | bytes 2097152 | tf_op jit(solution)/shard_map/all_to_all | solution.py:337
  56.1 72.6 %all-gather.3.cloned.1.call-start = ((), (), s32[]{:S(2)}) async-start(), calls=%async_computation.4 | async-start | bytes 2129920 | tf_op jit(solution)/shard_map/all_gather | solution.py:335
  56.8 6.8 %collective-permute-start.10 = (f32[2,64,384]{2,1,0:T(8,128)}, f32[2,64,384]{2,1,0:T(8,128)}, u32[]{:S(2)}, u32[]{:S(2)}) collective-permute-start(f32[2,64,384]{2,1,0:T(8,128)} %get-tuple-element.109), channel_id=1, source_target_pairs={{0,7},{1,0},{2,1},{3,2},{4,3},{5,4},{6,5},{7,6},{8,15},{9,8},{10,9... | collective-permute-start | bytes 589832 | tf_op jit(solution)/shard_map/ppermute | solution.py:20
  58.3 8.0 %collective-permute-start.4 = (f32[2,64,384]{2,1,0:T(8,128)}, f32[2,64,384]{2,1,0:T(8,128)}, u32[]{:S(2)}, u32[]{:S(2)}) collective-permute-start(f32[2,64,384]{2,1,0:T(8,128)} %get-tuple-element.103), channel_id=1, source_target_pairs={{0,1},{1,2},{2,3},{3,4},{4,5},{5,6},{6,7},{7,0},{8,9},{9,10},{10,1... | collective-permute-start | bytes 589832 | tf_op jit(solution)/shard_map/ppermute | solution.py:20
  59.3 19.5 %collective-permute-start.5 = (f32[2,64,384]{2,1,0:T(8,128)}, f32[2,64,384]{2,1,0:T(8,128)}, u32[]{:S(2)}, u32[]{:S(2)}) collective-permute-start(f32[2,64,384]{2,1,0:T(8,128)} %get-tuple-element.104), channel_id=1, source_target_pairs={{0,2},{1,3},{2,4},{3,5},{4,6},{5,7},{6,0},{7,1},{8,10},{9,11},{10,... | collective-permute-start | bytes 589832 | tf_op jit(solution)/shard_map/ppermute | solution.py:20
  60.3 21.4 %collective-permute-start.6 = (f32[2,64,384]{2,1,0:T(8,128)}, f32[2,64,384]{2,1,0:T(8,128)}, u32[]{:S(2)}, u32[]{:S(2)}) collective-permute-start(f32[2,64,384]{2,1,0:T(8,128)} %get-tuple-element.105), channel_id=1, source_target_pairs={{0,3},{1,4},{2,5},{3,6},{4,7},{5,0},{6,1},{7,2},{8,11},{9,12},{10,... | collective-permute-start | bytes 589832 | tf_op jit(solution)/shard_map/ppermute | solution.py:20
  62.1 19.5 %collective-permute-start.7 = (f32[2,64,384]{2,1,0:T(8,128)}, f32[2,64,384]{2,1,0:T(8,128)}, u32[]{:S(2)}, u32[]{:S(2)}) collective-permute-start(f32[2,64,384]{2,1,0:T(8,128)} %get-tuple-element.106), channel_id=1, source_target_pairs={{0,4},{1,5},{2,6},{3,7},{4,0},{5,1},{6,2},{7,3},{8,12},{9,13},{10,... | collective-permute-start | bytes 589832 | tf_op jit(solution)/shard_map/ppermute | solution.py:20
  63.6 19.6 %collective-permute-start.8 = (f32[2,64,384]{2,1,0:T(8,128)}, f32[2,64,384]{2,1,0:T(8,128)}, u32[]{:S(2)}, u32[]{:S(2)}) collective-permute-start(f32[2,64,384]{2,1,0:T(8,128)} %get-tuple-element.107), channel_id=1, source_target_pairs={{0,5},{1,6},{2,7},{3,0},{4,1},{5,2},{6,3},{7,4},{8,13},{9,14},{10,... | collective-permute-start | bytes 589832 | tf_op jit(solution)/shard_map/ppermute | solution.py:20
  66.3 18.8 %collective-permute-start.9 = (f32[2,64,384]{2,1,0:T(8,128)}, f32[2,64,384]{2,1,0:T(8,128)}, u32[]{:S(2)}, u32[]{:S(2)}) collective-permute-start(f32[2,64,384]{2,1,0:T(8,128)} %get-tuple-element.108), channel_id=1, source_target_pairs={{0,6},{1,7},{2,0},{3,1},{4,2},{5,3},{6,4},{7,5},{8,14},{9,15},{10,... | collective-permute-start | bytes 589832 | tf_op jit(solution)/shard_map/ppermute | solution.py:20
  85.1 20.3 %all-to-all-start.1 = ((f32[8,4,16,512]{3,2,1,0:T(8,128)}), f32[8,4,16,512]{3,2,1,0:T(8,128)}, u32[]{:S(2)}, u32[]{:S(2)}) async-start(f32[8,4,16,512]{3,2,1,0:T(8,128)} %bitcast.15), calls=%async_computation.1 | async-start | bytes 2097152 | tf_op jit(solution)/shard_map/all_to_all | solution.py:346
  110.4 20.2 %all-to-all-start.2 = ((f32[8,4,16,512]{3,2,1,0:T(8,128)}), f32[8,4,16,512]{3,2,1,0:T(8,128)}, u32[]{:S(2)}, u32[]{:S(2)}) async-start(f32[8,4,16,512]{3,2,1,0:T(8,128)} %shard_map.105), calls=%async_computation.2 | async-start | bytes 2097152 | tf_op jit(solution)/shard_map/all_to_all | solution.py:357
  130.7 39.1 %all-to-all-start.3 = ((f32[32,16,512]{2,1,0:T(8,128)}), f32[32,16,512]{2,1,0:T(8,128)}, u32[]{:S(2)}, u32[]{:S(2)}) async-start(f32[32,16,512]{2,1,0:T(8,128)} %bitcast.16), calls=%async_computation.3 | async-start | bytes 2097152 | tf_op jit(solution)/shard_map/all_to_all | solution.py:367
  139.9 64.0 %all-gather.5.cloned.1.call-start = ((), (), s32[]{:S(2)}) async-start(), calls=%async_computation.5 | async-start | bytes 2129920 | tf_op jit(solution)/shard_map/all_gather | solution.py:379
  139.9 7.5 %collective-permute-start.14 = (f32[136,512]{1,0:T(8,128)}, f32[136,512]{1,0:T(8,128)}, u32[]{:S(2)}, u32[]{:S(2)}) collective-permute-start(f32[136,512]{1,0:T(8,128)} %get-tuple-element.135), channel_id=1, source_target_pairs={{0,1},{1,2},{2,3},{3,4},{4,5},{5,6},{6,7},{7,0},{8,9},{9,10},{10,1... | collective-permute-start | bytes 835592 | tf_op jit(solution)/shard_map/ppermute | solution.py:20
  141.3 15.9 %collective-permute-start.15 = (f32[136,512]{1,0:T(8,128)}, f32[136,512]{1,0:T(8,128)}, u32[]{:S(2)}, u32[]{:S(2)}) collective-permute-start(f32[136,512]{1,0:T(8,128)} %get-tuple-element.136), channel_id=1, source_target_pairs={{0,2},{1,3},{2,4},{3,5},{4,6},{5,7},{6,0},{7,1},{8,10},{9,11},{10,... | collective-permute-start | bytes 835592 | tf_op jit(solution)/shard_map/ppermute | solution.py:20
  141.3 27.8 %collective-permute-start.16 = (f32[136,512]{1,0:T(8,128)}, f32[136,512]{1,0:T(8,128)}, u32[]{:S(2)}, u32[]{:S(2)}) collective-permute-start(f32[136,512]{1,0:T(8,128)} %get-tuple-element.137), channel_id=1, source_target_pairs={{0,3},{1,4},{2,5},{3,6},{4,7},{5,0},{6,1},{7,2},{8,11},{9,12},{10,... | collective-permute-start | bytes 835592 | tf_op jit(solution)/shard_map/ppermute | solution.py:20
  143.4 25.7 %collective-permute-start.17 = (f32[136,512]{1,0:T(8,128)}, f32[136,512]{1,0:T(8,128)}, u32[]{:S(2)}, u32[]{:S(2)}) collective-permute-start(f32[136,512]{1,0:T(8,128)} %get-tuple-element.138), channel_id=1, source_target_pairs={{0,4},{1,5},{2,6},{3,7},{4,0},{5,1},{6,2},{7,3},{8,12},{9,13},{10,... | collective-permute-start | bytes 835592 | tf_op jit(solution)/shard_map/ppermute | solution.py:20
  144.9 24.3 %collective-permute-start.18 = (f32[136,512]{1,0:T(8,128)}, f32[136,512]{1,0:T(8,128)}, u32[]{:S(2)}, u32[]{:S(2)}) collective-permute-start(f32[136,512]{1,0:T(8,128)} %get-tuple-element.139), channel_id=1, source_target_pairs={{0,5},{1,6},{2,7},{3,0},{4,1},{5,2},{6,3},{7,4},{8,13},{9,14},{10,... | collective-permute-start | bytes 835592 | tf_op jit(solution)/shard_map/ppermute | solution.py:20
  147.5 21.7 %collective-permute-start.19 = (f32[136,512]{1,0:T(8,128)}, f32[136,512]{1,0:T(8,128)}, u32[]{:S(2)}, u32[]{:S(2)}) collective-permute-start(f32[136,512]{1,0:T(8,128)} %get-tuple-element.140), channel_id=1, source_target_pairs={{0,6},{1,7},{2,0},{3,1},{4,2},{5,3},{6,4},{7,5},{8,14},{9,15},{10,... | collective-permute-start | bytes 835592 | tf_op jit(solution)/shard_map/ppermute | solution.py:20
  157.2 12.6 %collective-permute-start.20 = (f32[136,512]{1,0:T(8,128)}, f32[136,512]{1,0:T(8,128)}, u32[]{:S(2)}, u32[]{:S(2)}) collective-permute-start(f32[136,512]{1,0:T(8,128)} %get-tuple-element.141), channel_id=1, source_target_pairs={{0,7},{1,0},{2,1},{3,2},{4,3},{5,4},{6,5},{7,6},{8,15},{9,8},{10,9... | collective-permute-start | bytes 835592 | tf_op jit(solution)/shard_map/ppermute | solution.py:20
  (10 other events, 65.4 us)
Sparse Core Ops, SparseCore 0:
  58.7 36.1 all-gather.2
  173.5 30.4 all-gather.4

commit v4 on v3

--- a/solution.py
+++ b/solution.py
@@ -231,12 +231,12 @@
 
 
 def place_plan(ids, ins, outs):
-    core = ids[0] % 2
-    rows = ins[0].shape[0] // 4
-    for x in range(4):
-        for piece, owner in zip(ins, (core, 1 - core)):
-            start = pl.multiple_of((x * 2 + owner) * rows, rows)
-            yield piece.at[pl.ds(x * rows, rows), :], outs[0].at[pl.ds(start, rows), :]
+    chip, core = ids[0] // 2, ids[0] % 2
+    rows = ins[0].shape[0]
+    for j, piece in enumerate(ins):
+        owner = core if j < 4 else 1 - core
+        start = pl.multiple_of((lax.rem(chip - j % 4 + 4, 4) * 2 + owner) * rows, rows)
+        yield piece, outs[0].at[pl.ds(start, rows), :]
 
 
 def copying(plan, split_stores, n_small, n_in, n_out, *refs):
@@ -366,7 +366,7 @@
     moment_swap = lax.ppermute(moment_line, "rep", swap)
     returned = lax.all_to_all(spread.reshape(owners, rows, side), "fsdp", 0, 0, tiled=True)
     grams = [g if k == 0 else rep_shift(g, k, reps) for k, g in enumerate(grams)]
-    returned, *grams = barrier((returned, *grams))
+    returned, moment_swap, *grams = barrier((returned, moment_swap, *grams))
     tails = (2 * share, 8)
     (part,) = call(
         direction_kernel,
@@ -376,8 +376,8 @@
         [pltpu.VMEM((16, 128), F32)],
         [None] + [tails] * reps,
     )
-    line = lax.all_gather(part, "rep", axis=0, tiled=True, axis_index_groups=lines)
-    last_ids, part = barrier((ids, part))
+    found = [part] + [rep_shift(part, 2 * k, reps) for k in range(1, chips)]
+    last_ids, _ = barrier((ids, part))
     moment_new, left_new, right_new = call(
         stat_kernel,
         [(shard_rows, full_width), stats, stats],
@@ -385,12 +385,13 @@
         [moment_line, moment_swap, stat_left[0, 0], stat_right[0, 0], *grams],
         [],
     )
-    line, left_new = barrier((line, left_new))
+    found[2], left_new = barrier((found[2], left_new))
+    swapped = [lax.ppermute(x, "rep", swap) for x in found]
     (direction,) = shuffle(
         place_plan,
         [(shard_rows, full_width)],
         [ids],
-        [line, lax.ppermute(line, "rep", swap)],
+        found + swapped,
         2 * chips,
         True,
     )

time: 220 us -> 215 us (0.977)
  waiting for transfers between devices: 99.8 us -> 95.8 us
    ppermute x17 -> x20, waiting for transfers between devices: 52.2 us -> 73.5 us  [rep_shift(): lax.ppermute(value, 'rep', [(i, (i + step) % count) for i in range(count)])]
    all_gather x1 -> x0, waiting for transfers between devices: 18.8 us -> none  [shards(): lax.all_gather(part, 'rep', axis=0, tiled=True, axis_index_groups=lines)]
    ppermute x17 -> x20, starting transfers between devices: 23.1 us -> 18.3 us  [rep_shift(): lax.ppermute(value, 'rep', [(i, (i + step) % count) for i in range(count)])]
    ppermute x1, waiting for transfers between devices: 3.8 us -> 0.01 us  [shards(): moment_swap = lax.ppermute(moment_line, 'rep', swap)]
    ppermute x1 -> x4, starting transfers between devices: 0.67 us -> 4.07 us  [shards(): swapped = [lax.ppermute(x, 'rep', swap) for x in found]]
  transfers between devices with their start and end apart: 29 -> 34, of which waited for: 19 -> 22; matrix products, arithmetic and copies ran while one was open for 1% -> 1% of each run, Pallas kernels for 11% -> 12%
where the time goes in v4:
time: 215 us; the launch traced here: 214 us
  waiting for transfers between devices  95.8 us (45%)
  starting transfers between devices  60.3 us (28%)
  Pallas kernels  35.3 us (16%)
  between operations  14.3 us (7%)
  local copies, waits for them, and re-layouts  4.5 us (2%)
  other arithmetic  3.81 us (2%)
    ppermute x20, waiting for transfers between devices, rep_shift(): lax.ppermute(value, 'rep', [(i, (i + step) % count) for i in range(count)])  73.5 us
    pallas_call x6, Pallas kernels, call(): pl.pallas_call(functools.partial(staged, kernel, cuts, len(small), len(in...  27.9 us
    ppermute x20, starting transfers between devices, rep_shift(): lax.ppermute(value, 'rep', [(i, (i + step) % count) for i in range(count)])  18.3 us
    all_to_all x1, starting transfers between devices, shards(): arrived = lax.all_to_all(packed, 'fsdp', 0, 0, tiled=True)  11.3 us
    all_to_all x1, waiting for transfers between devices, shards(): lax.all_to_all(arrived.reshape(block_rows, quarters, rows, side), 'rep',...  10.7 us
    all_to_all x1, starting transfers between devices, shards(): lax.all_to_all(spread.reshape(owners, rows, side), 'fsdp', 0, 0, tiled=True)  9.39 us
    pallas_call x2, Pallas kernels, shuffle(): pl.pallas_call(functools.partial(copying, plan, split_stores, len(small),...  7.35 us
    all_to_all x1, starting transfers between devices, shards(): spread = lax.all_to_all(applied, 'rep', 0, 0, tiled=True)  4.99 us
  transfers between devices with their start and end apart: 34, of which 22 were waited for; matrix products, arithmetic and copies ran while one was open for 1% of the time, Pallas kernels for 12%

profile of v4, /device:TPU:1, one launch (start us, length us, event | category | flops | bytes accessed | tf_op | source)
XLA Modules:
  0.0 214.0 jit_solution(1069451058946622436)
XLA Ops:
  10.1 3.2 %collective-permute-start = (f32[4,16,6656]{2,1,0:T(8,128)}, f32[4,16,6656]{2,1,0:T(8,128)}, u32[]{:S(2)}, u32[]{:S(2)}) collective-permute-start(f32[4,16,6656]{2,1,0:T(8,128)} %dynamic-slice_bitcast_fusion), channel_id=1, source_target_pairs={{0,1},{1,0},{2,3},{3,2},{4,5},{5,4},{6,7},{7,6},{8,9},{9,8},{10,11... | collective-permute-start | bytes 5111816 | tf_op jit(solution)/shard_map/ppermute | solution.py:304
  13.4 3.6 %collective-permute-done = f32[4,16,6656]{2,1,0:T(8,128)} collective-permute-done((f32[4,16,6656]{2,1,0:T(8,128)}, f32[4,16,6656]{2,1,0:T(8,128)}, u32[]{:S(2)}, u32[]{:S(2)}) %collective-permute-start) | collective-permute-done | bytes 1703968 | tf_op jit(solution)/shard_map/ppermute | solution.py:304
  22.8 3.9 %shard_map.102 = (f32[2,64,384]{2,1,0:T(8,128)}, f32[2,64,384]{2,1,0:T(8,128)}, f32[2,64,384]{2,1,0:T(8,128)}, f32[2,64,384]{2,1,0:T(8,128)}, f32[2,64,384]{2,1,...) custom-call(s32[2]{0:T(128)S(1)} %pad_add_fusion.refs_0_, ...), custom_call_target="tpu_custom_call" | custom-call | tf_op jit(solution)/shard_map/pallas_call | solution.py:273
  26.7 4.7 %collective-permute-done.3.refs_5_ = f32[16,6656]{1,0:T(8,128)} collective-permute-done((f32[16,6656]{1,0:T(8,128)}, f32[16,6656]{1,0:T(8,128)}, u32[]{:S(2)}, u32[]{:S(2)}) %collective-permute-start.3) | collective-permute-done | bytes 426016 | tf_op jit(solution)/shard_map/ppermute | solution.py:20
  33.4 10.1 %collective-permute-done.1.refs_3_ = f32[16,6656]{1,0:T(8,128)} collective-permute-done((f32[16,6656]{1,0:T(8,128)}, f32[16,6656]{1,0:T(8,128)}, u32[]{:S(2)}, u32[]{:S(2)}) %collective-permute-start.1) | collective-permute-done | bytes 426016 | tf_op jit(solution)/shard_map/ppermute | solution.py:20
  43.5 3.7 %shard_map.103 = (f32[16,6656]{1,0:T(8,128)}, f32[8,512]{1,0:T(8,128)}, f32[32,16,512]{2,1,0:T(8,128)}) custom-call(s32[2]{0:T(128)S(1)} %pad_add_fusion.refs_0_, s32[8,32]{1,0:T(8,128)S(1)} %bitcast.30, f32[16,6656]{1,0:T(8,128)} %get-tuple-element.163.refs_2_, f32[16,6656]{1,0:T(8,128)} %collective-permute-done.1.refs_3_, ...), custom_call_target="tpu_custom_call" | custom-call | tf_op jit(solution)/shard_map/pallas_call | solution.py:210
  47.2 11.3 %all-to-all-start = ((f32[32,16,512]{2,1,0:T(8,128)}), f32[32,16,512]{2,1,0:T(8,128)}, u32[]{:S(2)}, u32[]{:S(2)}) async-start(f32[32,16,512]{2,1,0:T(8,128)} %get-tuple-element.101), calls=%async_computation | async-start | bytes 2097152 | tf_op jit(solution)/shard_map/all_to_all | solution.py:337
  67.0 11.7 %collective-permute-done.5.refs_3_ = f32[2,64,384]{2,1,0:T(8,128)} collective-permute-done((f32[2,64,384]{2,1,0:T(8,128)}, f32[2,64,384]{2,1,0:T(8,128)}, u32[]{:S(2)}, u32[]{:S(2)}) %collective-permute-start.5) | collective-permute-done | bytes 196640 | tf_op jit(solution)/shard_map/ppermute | solution.py:20
  78.8 3.5 %collective-permute-done.6.refs_4_ = f32[2,64,384]{2,1,0:T(8,128)} collective-permute-done((f32[2,64,384]{2,1,0:T(8,128)}, f32[2,64,384]{2,1,0:T(8,128)}, u32[]{:S(2)}, u32[]{:S(2)}) %collective-permute-start.6) | collective-permute-done | bytes 196640 | tf_op jit(solution)/shard_map/ppermute | solution.py:20
  83.3 4.6 %collective-permute-done.9.refs_7_ = f32[2,64,384]{2,1,0:T(8,128)} collective-permute-done((f32[2,64,384]{2,1,0:T(8,128)}, f32[2,64,384]{2,1,0:T(8,128)}, u32[]{:S(2)}, u32[]{:S(2)}) %collective-permute-start.9) | collective-permute-done | bytes 196640 | tf_op jit(solution)/shard_map/ppermute | solution.py:20
  89.7 4.2 %all-to-all-start.1 = ((f32[8,4,16,512]{3,2,1,0:T(8,128)}), f32[8,4,16,512]{3,2,1,0:T(8,128)}, u32[]{:S(2)}, u32[]{:S(2)}) async-start(f32[8,4,16,512]{3,2,1,0:T(8,128)} %bitcast.15), calls=%async_computation.1 | async-start | bytes 2097152 | tf_op jit(solution)/shard_map/all_to_all | solution.py:346
  93.9 3.9 %shard_map.104 = (bf16[512,512]{1,0:T(8,128)(2,1)}, bf16[512,512]{1,0:T(8,128)(2,1)}, bf16[512,512]{1,0:T(8,128)(2,1)}, bf16[512,512]{1,0:T(8,128)(2,1)}) custom-call(s32[2]{0:T(128)S(1)} %pad_add_fusion.refs_0_, f32[2,64,384]{2,1,0:T(8,128)} %get-tuple-element.112.refs_1_, f32[2,64,384]{2,1,0:T(8,128)} %collective-permute-done.4.refs_2_, ...), custom_call_target="tpu_custom_call" | custom-call | tf_op jit(solution)/shard_map/pallas_call | solution.py:210
  97.8 10.7 %all-to-all-done.1.refs_0_.refs_1_ = f32[8,4,16,512]{3,2,1,0:T(8,128)} async-done(((f32[8,4,16,512]{3,2,1,0:T(8,128)}), f32[8,4,16,512]{3,2,1,0:T(8,128)}, u32[]{:S(2)}, u32[]{:S(2)}) %all-to-all-start.1) | async-done | bytes 1048608 | tf_op jit(solution)/shard_map/all_to_all | solution.py:346
  108.5 5.0 %shard_map.105 = f32[8,4,16,512]{3,2,1,0:T(8,128)} custom-call(f32[8,4,16,512]{3,2,1,0:T(8,128)} %all-to-all-done.1.refs_0_.refs_1_, bf16[512,512]{1,0:T(8,128)(2,1)} %get-tuple-element.120.refs_1_, bf16[512,512]{1,0:T(8,128)(2,1)} %get-tuple-element.121.refs_2_, bf16[512,512]{1,0:T(8,128)(2,1)} %get-tuple-element.122.refs_3_, ...), custom_call_target="tpu_custom_call" | custom-call | tf_op jit(solution)/shard_map/pallas_call | solution.py:210
  113.6 5.0 %all-to-all-start.2 = ((f32[8,4,16,512]{3,2,1,0:T(8,128)}), f32[8,4,16,512]{3,2,1,0:T(8,128)}, u32[]{:S(2)}, u32[]{:S(2)}) async-start(f32[8,4,16,512]{3,2,1,0:T(8,128)} %shard_map.105), calls=%async_computation.2 | async-start | bytes 2097152 | tf_op jit(solution)/shard_map/all_to_all | solution.py:357
  126.0 5.0 %shard_map.106 = (f32[136,512]{1,0:T(8,128)}, f32[136,512]{1,0:T(8,128)}, f32[136,512]{1,0:T(8,128)}, f32[136,512]{1,0:T(8,128)}, f32[136,512]{1,0:T(8,128)}, /*...) custom-call(s32[2]{0:T(128)S(1)} %pad_add_fusion.refs_0_, ...), custom_call_target="tpu_custom_call" | custom-call | tf_op jit(solution)/shard_map/pallas_call | solution.py:210
  133.8 9.4 %all-to-all-start.3 = ((f32[32,16,512]{2,1,0:T(8,128)}), f32[32,16,512]{2,1,0:T(8,128)}, u32[]{:S(2)}, u32[]{:S(2)}) async-start(f32[32,16,512]{2,1,0:T(8,128)} %bitcast.16), calls=%async_computation.3 | async-start | bytes 2097152 | tf_op jit(solution)/shard_map/all_to_all | solution.py:367
  153.4 6.6 %collective-permute-done.16.refs_5_.refs_7_ = f32[136,512]{1,0:T(8,128)} collective-permute-done((f32[136,512]{1,0:T(8,128)}, f32[136,512]{1,0:T(8,128)}, u32[]{:S(2)}, u32[]{:S(2)}) %collective-permute-start.16) | collective-permute-done | bytes 278560 | tf_op jit(solution)/shard_map/ppermute | solution.py:20
  160.0 12.4 %collective-permute-done.17.refs_6_.refs_8_ = f32[136,512]{1,0:T(8,128)} collective-permute-done((f32[136,512]{1,0:T(8,128)}, f32[136,512]{1,0:T(8,128)}, u32[]{:S(2)}, u32[]{:S(2)}) %collective-permute-start.17) | collective-permute-done | bytes 278560 | tf_op jit(solution)/shard_map/ppermute | solution.py:20
  172.7 6.1 %collective-permute-done.21.refs_10_.refs_12_ = f32[136,512]{1,0:T(8,128)} collective-permute-done((f32[136,512]{1,0:T(8,128)}, f32[136,512]{1,0:T(8,128)}, u32[]{:S(2)}, u32[]{:S(2)}) %collective-permute-start.21) | collective-permute-done | bytes 278560 | tf_op jit(solution)/shard_map/ppermute | solution.py:20
  178.7 3.5 %shard_map.107.refs_1_ = f32[16,6656]{1,0:T(8,128)} custom-call(s32[2]{0:T(128)S(1)} %pad_add_fusion.refs_0_, s32[8,32]{1,0:T(8,128)S(1)} %bitcast.31, f32[32,16,512]{2,1,0:T(8,128)} %all-to-all-done.3.refs_2_, f32[136,512]{1,0:T(8,128)} %get-tuple-element.145.refs_3_.refs_5_, f32[136,512]{1,0:T(8,128)} %collective-permute-done.15.refs_4_.refs_6_, ...), custom_call_target="tpu_custom_call" | custom-call | tf_op jit(solution)/shard_map/pallas_call | solution.py:210
  185.2 6.7 %shard_map.108 = (f32[128,6656]{1,0:T(8,128)}, f32[8,64,512]{2,1,0:T(8,128)}, f32[8,64,512]{2,1,0:T(8,128)}) custom-call(s32[2]{0:T(128)S(1)} %pad_add_fusion.refs_0_, f32[64,6656]{1,0:T(8,128)} %all-gather.2.cloned.1.call-done.refs_1_, f32[64,6656]{1,0:T(8,128)} %collective-permute-done.14.refs_2_, f32[8,64,512]{2,1,0:T(8,128)} %bitcast.36, ...), custom_call_target="tpu_custom_call" | custom-call | tf_op jit(solution)/shard_map/pallas_call | solution.py:210
  192.0 3.6 %collective-permute-done.23.refs_3_ = f32[16,6656]{1,0:T(8,128)S(1)} collective-permute-done((f32[16,6656]{1,0:T(8,128)}, f32[16,6656]{1,0:T(8,128)S(1)}, u32[]{:S(2)}, u32[]{:S(2)}) %collective-permute-start.23) | collective-permute-done | bytes 426016 | tf_op jit(solution)/shard_map/ppermute | solution.py:20
  203.7 3.4 %shard_map.109 = f32[128,6656]{1,0:T(8,128)} custom-call(s32[2]{0:T(128)S(1)} %pad_add_fusion.refs_0_, f32[16,6656]{1,0:T(8,128)} %shard_map.107.refs_1_, f32[16,6656]{1,0:T(8,128)} %copy-done.4, f32[16,6656]{1,0:T(8,128)} %copy-done.2, f32[16,6656]{1,0:T(8,128)} %copy-done.3, f32[16,6656]{1,0:T(8,128)} %copy-done.5, f32[16,6656]{1,0:T(8,128)} %copy-done.8, ...), custom_call_target="tpu_custom_call" | custom-call | tf_op jit(solution)/shard_map/pallas_call | solution.py:273
  (78 shorter events, 53.8 us)
Async XLA Ops:
  20.1 11.3 %collective-permute-start.3 = (f32[16,6656]{1,0:T(8,128)}, f32[16,6656]{1,0:T(8,128)}, u32[]{:S(2)}, u32[]{:S(2)}) collective-permute-start(f32[16,6656]{1,0:T(8,128)} %get-tuple-element.160), channel_id=1, source_target_pairs={{0,6},{1,7},{2,0},{3,1},{4,2},{5,3},{6,4},{7,5},{8,14},{9,15},{10,... | collective-permute-start | bytes 1277960 | tf_op jit(solution)/shard_map/ppermute | solution.py:20
  20.8 12.6 %collective-permute-start.2 = (f32[16,6656]{1,0:T(8,128)}, f32[16,6656]{1,0:T(8,128)}, u32[]{:S(2)}, u32[]{:S(2)}) collective-permute-start(f32[16,6656]{1,0:T(8,128)} %get-tuple-element.161), channel_id=1, source_target_pairs={{0,4},{1,5},{2,6},{3,7},{4,0},{5,1},{6,2},{7,3},{8,12},{9,13},{10,... | collective-permute-start | bytes 1277960 | tf_op jit(solution)/shard_map/ppermute | solution.py:20
  21.3 22.2 %collective-permute-start.1 = (f32[16,6656]{1,0:T(8,128)}, f32[16,6656]{1,0:T(8,128)}, u32[]{:S(2)}, u32[]{:S(2)}) collective-permute-start(f32[16,6656]{1,0:T(8,128)} %get-tuple-element.162), channel_id=1, source_target_pairs={{0,2},{1,3},{2,4},{3,5},{4,6},{5,7},{6,0},{7,1},{8,10},{9,11},{10,... | collective-permute-start | bytes 1277960 | tf_op jit(solution)/shard_map/ppermute | solution.py:20
  47.2 42.5 %all-to-all-start = ((f32[32,16,512]{2,1,0:T(8,128)}), f32[32,16,512]{2,1,0:T(8,128)}, u32[]{:S(2)}, u32[]{:S(2)}) async-start(f32[32,16,512]{2,1,0:T(8,128)} %get-tuple-element.101), calls=%async_computation | async-start | bytes 2097152 | tf_op jit(solution)/shard_map/all_to_all | solution.py:337
  58.5 72.5 %all-gather.2.cloned.1.call-start = ((), (), s32[]{:S(2)}) async-start(), calls=%async_computation.4 | async-start | bytes 2129920 | tf_op jit(solution)/shard_map/all_gather | solution.py:335
  59.3 19.5 %collective-permute-start.5 = (f32[2,64,384]{2,1,0:T(8,128)}, f32[2,64,384]{2,1,0:T(8,128)}, u32[]{:S(2)}, u32[]{:S(2)}) collective-permute-start(f32[2,64,384]{2,1,0:T(8,128)} %get-tuple-element.105), channel_id=1, source_target_pairs={{0,2},{1,3},{2,4},{3,5},{4,6},{5,7},{6,0},{7,1},{8,10},{9,11},{10,... | collective-permute-start | bytes 589832 | tf_op jit(solution)/shard_map/ppermute | solution.py:20
  60.2 22.1 %collective-permute-start.6 = (f32[2,64,384]{2,1,0:T(8,128)}, f32[2,64,384]{2,1,0:T(8,128)}, u32[]{:S(2)}, u32[]{:S(2)}) collective-permute-start(f32[2,64,384]{2,1,0:T(8,128)} %get-tuple-element.106), channel_id=1, source_target_pairs={{0,3},{1,4},{2,5},{3,6},{4,7},{5,0},{6,1},{7,2},{8,11},{9,12},{10,... | collective-permute-start | bytes 589832 | tf_op jit(solution)/shard_map/ppermute | solution.py:20
  61.8 20.4 %collective-permute-start.7 = (f32[2,64,384]{2,1,0:T(8,128)}, f32[2,64,384]{2,1,0:T(8,128)}, u32[]{:S(2)}, u32[]{:S(2)}) collective-permute-start(f32[2,64,384]{2,1,0:T(8,128)} %get-tuple-element.107), channel_id=1, source_target_pairs={{0,4},{1,5},{2,6},{3,7},{4,0},{5,1},{6,2},{7,3},{8,12},{9,13},{10,... | collective-permute-start | bytes 589832 | tf_op jit(solution)/shard_map/ppermute | solution.py:20
  63.8 19.5 %collective-permute-start.8 = (f32[2,64,384]{2,1,0:T(8,128)}, f32[2,64,384]{2,1,0:T(8,128)}, u32[]{:S(2)}, u32[]{:S(2)}) collective-permute-start(f32[2,64,384]{2,1,0:T(8,128)} %get-tuple-element.108), channel_id=1, source_target_pairs={{0,5},{1,6},{2,7},{3,0},{4,1},{5,2},{6,3},{7,4},{8,13},{9,14},{10,... | collective-permute-start | bytes 589832 | tf_op jit(solution)/shard_map/ppermute | solution.py:20
  66.4 21.5 %collective-permute-start.9 = (f32[2,64,384]{2,1,0:T(8,128)}, f32[2,64,384]{2,1,0:T(8,128)}, u32[]{:S(2)}, u32[]{:S(2)}) collective-permute-start(f32[2,64,384]{2,1,0:T(8,128)} %get-tuple-element.109), channel_id=1, source_target_pairs={{0,6},{1,7},{2,0},{3,1},{4,2},{5,3},{6,4},{7,5},{8,14},{9,15},{10,... | collective-permute-start | bytes 589832 | tf_op jit(solution)/shard_map/ppermute | solution.py:20
  78.8 10.9 %collective-permute-start.10 = (f32[2,64,384]{2,1,0:T(8,128)}, f32[2,64,384]{2,1,0:T(8,128)}, u32[]{:S(2)}, u32[]{:S(2)}) collective-permute-start(f32[2,64,384]{2,1,0:T(8,128)} %get-tuple-element.110), channel_id=1, source_target_pairs={{0,7},{1,0},{2,1},{3,2},{4,3},{5,4},{6,5},{7,6},{8,15},{9,8},{10,9... | collective-permute-start | bytes 589832 | tf_op jit(solution)/shard_map/ppermute | solution.py:20
  89.7 18.8 %all-to-all-start.1 = ((f32[8,4,16,512]{3,2,1,0:T(8,128)}), f32[8,4,16,512]{3,2,1,0:T(8,128)}, u32[]{:S(2)}, u32[]{:S(2)}) async-start(f32[8,4,16,512]{3,2,1,0:T(8,128)} %bitcast.15), calls=%async_computation.1 | async-start | bytes 2097152 | tf_op jit(solution)/shard_map/all_to_all | solution.py:346
  113.6 20.2 %all-to-all-start.2 = ((f32[8,4,16,512]{3,2,1,0:T(8,128)}), f32[8,4,16,512]{3,2,1,0:T(8,128)}, u32[]{:S(2)}, u32[]{:S(2)}) async-start(f32[8,4,16,512]{3,2,1,0:T(8,128)} %shard_map.105), calls=%async_computation.2 | async-start | bytes 2097152 | tf_op jit(solution)/shard_map/all_to_all | solution.py:357
  133.8 45.0 %all-to-all-start.3 = ((f32[32,16,512]{2,1,0:T(8,128)}), f32[32,16,512]{2,1,0:T(8,128)}, u32[]{:S(2)}, u32[]{:S(2)}) async-start(f32[32,16,512]{2,1,0:T(8,128)} %bitcast.16), calls=%async_computation.3 | async-start | bytes 2097152 | tf_op jit(solution)/shard_map/all_to_all | solution.py:367
  143.2 35.6 %collective-permute-start.14 = (f32[64,6656]{1,0:T(8,128)}, f32[64,6656]{1,0:T(8,128)}, u32[]{:S(2)}, u32[]{:S(2)}) collective-permute-start(f32[64,6656]{1,0:T(8,128)} %all-gather.2.cloned.1.call-done.refs_1_), channel_id=1, source_target_pairs={{0,1},{1,0},{2,3},{3,2},{4,5},{5,4},{6,7},{7,6},{8,9},{9,8},{10,11... | collective-permute-start | bytes 5111816 | tf_op jit(solution)/shard_map/ppermute | solution.py:366
  144.6 15.4 %collective-permute-start.16 = (f32[136,512]{1,0:T(8,128)}, f32[136,512]{1,0:T(8,128)}, u32[]{:S(2)}, u32[]{:S(2)}) collective-permute-start(f32[136,512]{1,0:T(8,128)} %get-tuple-element.138), channel_id=1, source_target_pairs={{0,2},{1,3},{2,4},{3,5},{4,6},{5,7},{6,0},{7,1},{8,10},{9,11},{10,... | collective-permute-start | bytes 835592 | tf_op jit(solution)/shard_map/ppermute | solution.py:20
  144.7 27.7 %collective-permute-start.17 = (f32[136,512]{1,0:T(8,128)}, f32[136,512]{1,0:T(8,128)}, u32[]{:S(2)}, u32[]{:S(2)}) collective-permute-start(f32[136,512]{1,0:T(8,128)} %get-tuple-element.139), channel_id=1, source_target_pairs={{0,3},{1,4},{2,5},{3,6},{4,7},{5,0},{6,1},{7,2},{8,11},{9,12},{10,... | collective-permute-start | bytes 835592 | tf_op jit(solution)/shard_map/ppermute | solution.py:20
  147.1 25.3 %collective-permute-start.18 = (f32[136,512]{1,0:T(8,128)}, f32[136,512]{1,0:T(8,128)}, u32[]{:S(2)}, u32[]{:S(2)}) collective-permute-start(f32[136,512]{1,0:T(8,128)} %get-tuple-element.140), channel_id=1, source_target_pairs={{0,4},{1,5},{2,6},{3,7},{4,0},{5,1},{6,2},{7,3},{8,12},{9,13},{10,... | collective-permute-start | bytes 835592 | tf_op jit(solution)/shard_map/ppermute | solution.py:20
  150.3 22.1 %collective-permute-start.19 = (f32[136,512]{1,0:T(8,128)}, f32[136,512]{1,0:T(8,128)}, u32[]{:S(2)}, u32[]{:S(2)}) collective-permute-start(f32[136,512]{1,0:T(8,128)} %get-tuple-element.141), channel_id=1, source_target_pairs={{0,5},{1,6},{2,7},{3,0},{4,1},{5,2},{6,3},{7,4},{8,13},{9,14},{10,... | collective-permute-start | bytes 835592 | tf_op jit(solution)/shard_map/ppermute | solution.py:20
  160.0 12.6 %collective-permute-start.20 = (f32[136,512]{1,0:T(8,128)}, f32[136,512]{1,0:T(8,128)}, u32[]{:S(2)}, u32[]{:S(2)}) collective-permute-start(f32[136,512]{1,0:T(8,128)} %get-tuple-element.142), channel_id=1, source_target_pairs={{0,6},{1,7},{2,0},{3,1},{4,2},{5,3},{6,4},{7,5},{8,14},{9,15},{10,... | collective-permute-start | bytes 835592 | tf_op jit(solution)/shard_map/ppermute | solution.py:20
  182.2 13.3 %collective-permute-start.23 = (f32[16,6656]{1,0:T(8,128)}, f32[16,6656]{1,0:T(8,128)S(1)}, u32[]{:S(2)}, u32[]{:S(2)}) collective-permute-start(f32[16,6656]{1,0:T(8,128)} %shard_map.107.refs_1_), channel_id=1, source_target_pairs={{0,4},{1,5},{2,6},{3,7},{4,0},{5,1},{6,2},{7,3},{8,12},{9,13},{10,... | collective-permute-start | bytes 1277960 | tf_op jit(solution)/shard_map/ppermute | solution.py:20
  182.3 16.4 %collective-permute-start.24 = (f32[16,6656]{1,0:T(8,128)}, f32[16,6656]{1,0:T(8,128)S(1)}, u32[]{:S(2)}, u32[]{:S(2)}) collective-permute-start(f32[16,6656]{1,0:T(8,128)} %shard_map.107.refs_1_), channel_id=1, source_target_pairs={{0,6},{1,7},{2,0},{3,1},{4,2},{5,3},{6,4},{7,5},{8,14},{9,15},{10,... | collective-permute-start | bytes 1277960 | tf_op jit(solution)/shard_map/ppermute | solution.py:20
  182.4 17.8 %collective-permute-start.22 = (f32[16,6656]{1,0:T(8,128)}, f32[16,6656]{1,0:T(8,128)S(1)}, u32[]{:S(2)}, u32[]{:S(2)}) collective-permute-start(f32[16,6656]{1,0:T(8,128)} %shard_map.107.refs_1_), channel_id=1, source_target_pairs={{0,2},{1,3},{2,4},{3,5},{4,6},{5,7},{6,0},{7,1},{8,10},{9,11},{10,... | collective-permute-start | bytes 1277960 | tf_op jit(solution)/shard_map/ppermute | solution.py:20
  183.9 17.6 %collective-permute-start.25 = (f32[16,6656]{1,0:T(8,128)}, f32[16,6656]{1,0:T(8,128)S(1)}, u32[]{:S(2)}, u32[]{:S(2)}) collective-permute-start(f32[16,6656]{1,0:T(8,128)} %shard_map.107.refs_1_), channel_id=1, source_target_pairs={{0,1},{1,0},{2,3},{3,2},{4,5},{5,4},{6,7},{7,6},{8,9},{9,8},{10,11... | collective-permute-start | bytes 1277960 | tf_op jit(solution)/shard_map/ppermute | solution.py:389
  (20 other events, 134.3 us)
Sparse Core Ops, SparseCore 0:
  61.2 34.7 all-gather.1

commit v5 on v4

--- a/solution.py
+++ b/solution.py
@@ -281,6 +281,50 @@
     )(*small, *[pltpu.with_memory_space_constraint(x, pltpu.HBM) for x in ins])
 
 
+def give_plan(ids, ins, outs):
+    core = ids[0] % 2
+    for x in range(ins[0].shape[0]):
+        yield ins[0].at[x, 1 - core], outs[0].at[x]
+
+
+def sum_kernel(ids, grad, other, *refs):
+    outs, (mine, theirs, sems, out_sems) = refs[:4], refs[4:]
+    chip, core = ids[0] // 2, ids[0] % 2
+    order = (2, 1, 3, 0)
+    loads, stores = {}, []
+    for k in order:
+        x = lax.rem(chip + k, 4)
+        loads[k] = (
+            pltpu.make_async_copy(grad.at[x, core], mine.at[k], sems.at[k]),
+            pltpu.make_async_copy(other.at[x], theirs.at[k], sems.at[4 + k]),
+        )
+        for load in loads[k]:
+            load.start()
+    for k in order:
+        for load in loads[k]:
+            load.wait()
+        mine[k] = mine[k] + theirs[k]
+        stores.append(pltpu.make_async_copy(mine.at[k], outs[k], out_sems.at[k]))
+        stores[-1].start()
+    for store in stores:
+        store.wait()
+
+
+def pair_sums(ids, grad, other):
+    hbm = pl.BlockSpec(memory_space=pltpu.HBM)
+    chips, _, rows, width = grad.shape
+    held = pltpu.VMEM((chips, rows, width), F32)
+    return pl.pallas_call(
+        sum_kernel,
+        out_shape=[pltpu.HBM((rows, width), F32)] * chips,
+        in_specs=[pl.BlockSpec(memory_space=pltpu.SMEM), hbm, hbm],
+        out_specs=[hbm] * chips,
+        scratch_shapes=[held, held]
+        + [pltpu.SemaphoreType.DMA((2 * chips,)), pltpu.SemaphoreType.DMA((chips,))],
+        compiler_params=PARAMS,
+    )(ids, *[pltpu.with_memory_space_constraint(x, pltpu.HBM) for x in (grad, other)])
+
+
 def shards(gradient, second_moment, owner_cols, stat_left, stat_right, root_left, root_right):
     shard_rows, full_width = gradient.shape[1:]
     side = stat_left.shape[-1]
@@ -301,13 +345,10 @@
 
     grad = gradient[0].reshape(chips, 2, rows, full_width)
     swap = [(i, i ^ 1) for i in range(reps)]
-    other = lax.ppermute(pick(grad, 1 - core, 1), "rep", swap)
-    mine = pick(grad, core, 1)
-    parts = []
-    for k in range(chips):
-        to = (chip + k) % chips
-        piece = pick(mine, to) + pick(other, to)
-        parts.append(piece if k == 0 else rep_shift(piece, 2 * k, reps))
+    (given,) = shuffle(give_plan, [(chips, rows, full_width)], [ids], [grad], chips, True)
+    other = lax.ppermute(given, "rep", swap)
+    parts = pair_sums(ids, grad, other)
+    parts = [p if k == 0 else rep_shift(p, 2 * k, reps) for k, p in enumerate(parts)]
     second = lax.dynamic_slice_in_dim(second_moment, rep * rows, rows, 0)
     later_ids, _ = barrier((ids, parts[0]))
     stats = (block_rows, share, side)

time: 215 us -> 214 us (level)
  Pallas kernels: 35.3 us -> 41.9 us
  waiting for transfers between devices: 95.8 us -> 92.2 us
  other arithmetic: 3.81 us -> 0.68 us
    ppermute x20, waiting for transfers between devices: 73.5 us -> 70.1 us  [rep_shift(): lax.ppermute(value, 'rep', [(i, (i + step) % count) for i in range(count)])]
    pallas_call x0 -> x1, Pallas kernels: none -> 3.37 us  [pair_sums(): pl.pallas_call(sum_kernel, out_shape=[pltpu.HBM((rows, width), F32)] * ch...]
    add x1 -> x0, other arithmetic: 3.13 us -> none  [shards(): piece = pick(mine, to) + pick(other, to)]
    pallas_call x2 -> x3, Pallas kernels: 7.35 us -> 10.5 us  [shuffle(): pl.pallas_call(functools.partial(copying, plan, split_stores, len(small),...]
    squeeze x1 -> x0, local copies, waits for them, and re-layouts: 2.92 us -> none  [pick(): return lax.dynamic_index_in_dim(array, index, axis, keepdims=False)]
  transfers between devices with their start and end apart: 34 -> 34, of which waited for: 22 -> 23; matrix products, arithmetic and copies ran while one was open for 1% -> 1% of each run, Pallas kernels for 12% -> 12%
where the time goes in v5:
time: 214 us; the launch traced here: 213 us
  waiting for transfers between devices  92.2 us (43%)
  starting transfers between devices  61.5 us (29%)
  Pallas kernels  41.9 us (20%)
  between operations  14.3 us (7%)
  local copies, waits for them, and re-layouts  2.36 us (1%)
    ppermute x20, waiting for transfers between devices, rep_shift(): lax.ppermute(value, 'rep', [(i, (i + step) % count) for i in range(count)])  70.1 us
    pallas_call x6, Pallas kernels, call(): pl.pallas_call(functools.partial(staged, kernel, cuts, len(small), len(in...  28 us
    ppermute x20, starting transfers between devices, rep_shift(): lax.ppermute(value, 'rep', [(i, (i + step) % count) for i in range(count)])  20.3 us
    all_to_all x1, waiting for transfers between devices, shards(): lax.all_to_all(arrived.reshape(block_rows, quarters, rows, side), 'rep',...  10.5 us
    pallas_call x3, Pallas kernels, shuffle(): pl.pallas_call(functools.partial(copying, plan, split_stores, len(small),...  10.5 us
    all_to_all x1, starting transfers between devices, shards(): arrived = lax.all_to_all(packed, 'fsdp', 0, 0, tiled=True)  10.4 us
    all_to_all x1, starting transfers between devices, shards(): lax.all_to_all(spread.reshape(owners, rows, side), 'fsdp', 0, 0, tiled=True)  9.41 us
    all_to_all x1, starting transfers between devices, shards(): spread = lax.all_to_all(applied, 'rep', 0, 0, tiled=True)  4.99 us
  transfers between devices with their start and end apart: 34, of which 23 were waited for; matrix products, arithmetic and copies ran while one was open for 1% of the time, Pallas kernels for 12%

profile of v5, /device:TPU:1, one launch (start us, length us, event | category | flops | bytes accessed | tf_op | source)
XLA Modules:
  0.0 212.9 jit_solution(14754587862912922842)
XLA Ops:
  10.4 3.3 %collective-permute-start = (f32[4,16,6656]{2,1,0:T(8,128)}, f32[4,16,6656]{2,1,0:T(8,128)}, u32[]{:S(2)}, u32[]{:S(2)}) collective-permute-start(f32[4,16,6656]{2,1,0:T(8,128)} %shard_map.102), channel_id=1, source_target_pairs={{0,1},{1,0},{2,3},{3,2},{4,5},{5,4},{6,7},{7,6},{8,9},{9,8},{10,11... | collective-permute-start | bytes 5111816 | tf_op jit(solution)/shard_map/ppermute | solution.py:349
  13.7 3.6 %collective-permute-done.other = f32[4,16,6656]{2,1,0:T(8,128)} collective-permute-done((f32[4,16,6656]{2,1,0:T(8,128)}, f32[4,16,6656]{2,1,0:T(8,128)}, u32[]{:S(2)}, u32[]{:S(2)}) %collective-permute-start) | collective-permute-done | bytes 1703968 | tf_op jit(solution)/shard_map/ppermute | solution.py:349
  17.3 3.4 %shard_map.103 = (f32[16,6656]{1,0:T(8,128)}, f32[16,6656]{1,0:T(8,128)}, f32[16,6656]{1,0:T(8,128)}, f32[16,6656]{1,0:T(8,128)}) custom-call(s32[2]{0:T(128)S(1)} %pad_add_fusion.refs_0_.ids, f32[4,2,16,6656]{3,2,1,0:T(8,128)} %bitcast.15, f32[4,16,6656]{2,1,0:T(8,128)} %collective-permute-done.other), custom_call_target="tpu_custom_call" | custom-call | tf_op jit(solution)/shard_map/pallas_call | solution.py:317
  24.6 3.9 %shard_map.104 = (f32[2,64,384]{2,1,0:T(8,128)}, f32[2,64,384]{2,1,0:T(8,128)}, f32[2,64,384]{2,1,0:T(8,128)}, f32[2,64,384]{2,1,0:T(8,128)}, f32[2,64,384]{2,1,...) custom-call(s32[2]{0:T(128)S(1)} %pad_add_fusion.refs_0_.ids, ...), custom_call_target="tpu_custom_call" | custom-call | tf_op jit(solution)/shard_map/pallas_call | solution.py:273
  28.5 5.4 %collective-permute-done.1.refs_3_ = f32[16,6656]{1,0:T(8,128)S(1)} collective-permute-done((f32[16,6656]{1,0:T(8,128)}, f32[16,6656]{1,0:T(8,128)S(1)}, u32[]{:S(2)}, u32[]{:S(2)}) %collective-permute-start.1) | collective-permute-done | bytes 426016 | tf_op jit(solution)/shard_map/ppermute | solution.py:20
  33.9 7.7 %collective-permute-done.2.refs_4_ = f32[16,6656]{1,0:T(8,128)S(1)} collective-permute-done((f32[16,6656]{1,0:T(8,128)}, f32[16,6656]{1,0:T(8,128)S(1)}, u32[]{:S(2)}, u32[]{:S(2)}) %collective-permute-start.2) | collective-permute-done | bytes 426016 | tf_op jit(solution)/shard_map/ppermute | solution.py:20
  43.5 3.7 %shard_map.105 = (f32[16,6656]{1,0:T(8,128)}, f32[8,512]{1,0:T(8,128)}, f32[32,16,512]{2,1,0:T(8,128)}) custom-call(s32[2]{0:T(128)S(1)} %pad_add_fusion.refs_0_.ids, s32[8,32]{1,0:T(8,128)S(1)} %bitcast.12, f32[16,6656]{1,0:T(8,128)} %get-tuple-element.86.refs_2_, f32[16,6656]{1,0:T(8,128)} %copy-done.2, f32[16,6656]{1,0:T(8,128)} %copy-done.3, ...), custom_call_target="tpu_custom_call" | custom-call | tf_op jit(solution)/shard_map/pallas_call | solution.py:210
  47.2 10.4 %all-to-all-start = ((f32[32,16,512]{2,1,0:T(8,128)}), f32[32,16,512]{2,1,0:T(8,128)}, u32[]{:S(2)}, u32[]{:S(2)}) async-start(f32[32,16,512]{2,1,0:T(8,128)} %get-tuple-element.109), calls=%async_computation | async-start | bytes 2097152 | tf_op jit(solution)/shard_map/all_to_all | solution.py:378
  66.7 4.8 %collective-permute-done.5.refs_3_ = f32[2,64,384]{2,1,0:T(8,128)} collective-permute-done((f32[2,64,384]{2,1,0:T(8,128)}, f32[2,64,384]{2,1,0:T(8,128)}, u32[]{:S(2)}, u32[]{:S(2)}) %collective-permute-start.5) | collective-permute-done | bytes 196640 | tf_op jit(solution)/shard_map/ppermute | solution.py:20
  73.4 9.0 %collective-permute-done.7.refs_5_ = f32[2,64,384]{2,1,0:T(8,128)} collective-permute-done((f32[2,64,384]{2,1,0:T(8,128)}, f32[2,64,384]{2,1,0:T(8,128)}, u32[]{:S(2)}, u32[]{:S(2)}) %collective-permute-start.7) | collective-permute-done | bytes 196640 | tf_op jit(solution)/shard_map/ppermute | solution.py:20
  88.7 4.2 %all-to-all-start.1 = ((f32[8,4,16,512]{3,2,1,0:T(8,128)}), f32[8,4,16,512]{3,2,1,0:T(8,128)}, u32[]{:S(2)}, u32[]{:S(2)}) async-start(f32[8,4,16,512]{3,2,1,0:T(8,128)} %bitcast.6), calls=%async_computation.1 | async-start | bytes 2097152 | tf_op jit(solution)/shard_map/all_to_all | solution.py:387
  92.9 3.9 %shard_map.106 = (bf16[512,512]{1,0:T(8,128)(2,1)}, bf16[512,512]{1,0:T(8,128)(2,1)}, bf16[512,512]{1,0:T(8,128)(2,1)}, bf16[512,512]{1,0:T(8,128)(2,1)}) custom-call(s32[2]{0:T(128)S(1)} %pad_add_fusion.refs_0_.ids, f32[2,64,384]{2,1,0:T(8,128)} %get-tuple-element.120.refs_1_, f32[2,64,384]{2,1,0:T(8,128)} %collective-permute-done.4.refs_2_, ...), custom_call_target="tpu_custom_call" | custom-call | tf_op jit(solution)/shard_map/pallas_call | solution.py:210
  96.8 10.5 %all-to-all-done.1.refs_0_.refs_1_ = f32[8,4,16,512]{3,2,1,0:T(8,128)} async-done(((f32[8,4,16,512]{3,2,1,0:T(8,128)}), f32[8,4,16,512]{3,2,1,0:T(8,128)}, u32[]{:S(2)}, u32[]{:S(2)}) %all-to-all-start.1) | async-done | bytes 1048608 | tf_op jit(solution)/shard_map/all_to_all | solution.py:387
  107.3 5.0 %shard_map.107 = f32[8,4,16,512]{3,2,1,0:T(8,128)} custom-call(f32[8,4,16,512]{3,2,1,0:T(8,128)} %all-to-all-done.1.refs_0_.refs_1_, bf16[512,512]{1,0:T(8,128)(2,1)} %get-tuple-element.128.refs_1_, bf16[512,512]{1,0:T(8,128)(2,1)} %get-tuple-element.129.refs_2_, bf16[512,512]{1,0:T(8,128)(2,1)} %get-tuple-element.130.refs_3_, ...), custom_call_target="tpu_custom_call" | custom-call | tf_op jit(solution)/shard_map/pallas_call | solution.py:210
  112.4 5.0 %all-to-all-start.2 = ((f32[8,4,16,512]{3,2,1,0:T(8,128)}), f32[8,4,16,512]{3,2,1,0:T(8,128)}, u32[]{:S(2)}, u32[]{:S(2)}) async-start(f32[8,4,16,512]{3,2,1,0:T(8,128)} %shard_map.107), calls=%async_computation.2 | async-start | bytes 2097152 | tf_op jit(solution)/shard_map/all_to_all | solution.py:398
  124.8 5.0 %shard_map.108 = (f32[136,512]{1,0:T(8,128)}, f32[136,512]{1,0:T(8,128)}, f32[136,512]{1,0:T(8,128)}, f32[136,512]{1,0:T(8,128)}, f32[136,512]{1,0:T(8,128)}, /*...) custom-call(s32[2]{0:T(128)S(1)} %pad_add_fusion.refs_0_.ids, ...), custom_call_target="tpu_custom_call" | custom-call | tf_op jit(solution)/shard_map/pallas_call | solution.py:210
  132.6 9.4 %all-to-all-start.3 = ((f32[32,16,512]{2,1,0:T(8,128)}), f32[32,16,512]{2,1,0:T(8,128)}, u32[]{:S(2)}, u32[]{:S(2)}) async-start(f32[32,16,512]{2,1,0:T(8,128)} %bitcast.7), calls=%async_computation.3 | async-start | bytes 2097152 | tf_op jit(solution)/shard_map/all_to_all | solution.py:408
  152.2 6.6 %collective-permute-done.16.refs_5_.refs_7_ = f32[136,512]{1,0:T(8,128)} collective-permute-done((f32[136,512]{1,0:T(8,128)}, f32[136,512]{1,0:T(8,128)}, u32[]{:S(2)}, u32[]{:S(2)}) %collective-permute-start.16) | collective-permute-done | bytes 278560 | tf_op jit(solution)/shard_map/ppermute | solution.py:20
  158.9 12.4 %collective-permute-done.17.refs_6_.refs_8_ = f32[136,512]{1,0:T(8,128)} collective-permute-done((f32[136,512]{1,0:T(8,128)}, f32[136,512]{1,0:T(8,128)}, u32[]{:S(2)}, u32[]{:S(2)}) %collective-permute-start.17) | collective-permute-done | bytes 278560 | tf_op jit(solution)/shard_map/ppermute | solution.py:20
  171.5 6.1 %collective-permute-done.21.refs_10_.refs_12_ = f32[136,512]{1,0:T(8,128)} collective-permute-done((f32[136,512]{1,0:T(8,128)}, f32[136,512]{1,0:T(8,128)}, u32[]{:S(2)}, u32[]{:S(2)}) %collective-permute-start.21) | collective-permute-done | bytes 278560 | tf_op jit(solution)/shard_map/ppermute | solution.py:20
  177.6 3.5 %shard_map.109.refs_1_ = f32[16,6656]{1,0:T(8,128)} custom-call(s32[2]{0:T(128)S(1)} %pad_add_fusion.refs_0_.ids, s32[8,32]{1,0:T(8,128)S(1)} %bitcast.13, f32[32,16,512]{2,1,0:T(8,128)} %all-to-all-done.3.refs_2_, f32[136,512]{1,0:T(8,128)} %get-tuple-element.153.refs_3_.refs_5_, f32[136,512]{1,0:T(8,128)} %collective-permute-done.15.refs_4_.refs_6_, ...), custom_call_target="tpu_custom_call" | custom-call | tf_op jit(solution)/shard_map/pallas_call | solution.py:210
  184.1 6.8 %shard_map.110 = (f32[128,6656]{1,0:T(8,128)}, f32[8,64,512]{2,1,0:T(8,128)}, f32[8,64,512]{2,1,0:T(8,128)}) custom-call(s32[2]{0:T(128)S(1)} %pad_add_fusion.refs_0_.ids, f32[64,6656]{1,0:T(8,128)} %all-gather.2.cloned.1.call-done.refs_1_, f32[64,6656]{1,0:T(8,128)} %collective-permute-done.14.refs_2_, f32[8,64,512]{2,1,0:T(8,128)} %bitcast.18, ...), custom_call_target="tpu_custom_call" | custom-call | tf_op jit(solution)/shard_map/pallas_call | solution.py:210
  190.9 3.5 %collective-permute-done.23.refs_3_ = f32[16,6656]{1,0:T(8,128)S(1)} collective-permute-done((f32[16,6656]{1,0:T(8,128)}, f32[16,6656]{1,0:T(8,128)S(1)}, u32[]{:S(2)}, u32[]{:S(2)}) %collective-permute-start.23) | collective-permute-done | bytes 426016 | tf_op jit(solution)/shard_map/ppermute | solution.py:20
  202.6 3.4 %shard_map.111 = f32[128,6656]{1,0:T(8,128)} custom-call(s32[2]{0:T(128)S(1)} %pad_add_fusion.refs_0_.ids, f32[16,6656]{1,0:T(8,128)} %shard_map.109.refs_1_, f32[16,6656]{1,0:T(8,128)} %copy-done.7, f32[16,6656]{1,0:T(8,128)} %copy-done.5, f32[16,6656]{1,0:T(8,128)} %copy-done.6, f32[16,6656]{1,0:T(8,128)} %copy-done.8, f32[16,6656]{1,0:T(8,128)} %copy-done.11, ...), custom_call_target="tpu_custom_call" | custom-call | tf_op jit(solution)/shard_map/pallas_call | solution.py:273
  (84 shorter events, 58.1 us)
Async XLA Ops:
  20.7 13.3 %collective-permute-start.1 = (f32[16,6656]{1,0:T(8,128)}, f32[16,6656]{1,0:T(8,128)S(1)}, u32[]{:S(2)}, u32[]{:S(2)}) collective-permute-start(f32[16,6656]{1,0:T(8,128)} %get-tuple-element.97), channel_id=1, source_target_pairs={{0,2},{1,3},{2,4},{3,5},{4,6},{5,7},{6,0},{7,1},{8,10},{9,11},{10,... | collective-permute-start | bytes 1277960 | tf_op jit(solution)/shard_map/ppermute | solution.py:20
  20.8 20.9 %collective-permute-start.2 = (f32[16,6656]{1,0:T(8,128)}, f32[16,6656]{1,0:T(8,128)S(1)}, u32[]{:S(2)}, u32[]{:S(2)}) collective-permute-start(f32[16,6656]{1,0:T(8,128)} %get-tuple-element.98), channel_id=1, source_target_pairs={{0,4},{1,5},{2,6},{3,7},{4,0},{5,1},{6,2},{7,3},{8,12},{9,13},{10,... | collective-permute-start | bytes 1277960 | tf_op jit(solution)/shard_map/ppermute | solution.py:20
  22.7 20.0 %collective-permute-start.3 = (f32[16,6656]{1,0:T(8,128)}, f32[16,6656]{1,0:T(8,128)S(1)}, u32[]{:S(2)}, u32[]{:S(2)}) collective-permute-start(f32[16,6656]{1,0:T(8,128)} %get-tuple-element.99), channel_id=1, source_target_pairs={{0,6},{1,7},{2,0},{3,1},{4,2},{5,3},{6,4},{7,5},{8,14},{9,15},{10,... | collective-permute-start | bytes 1277960 | tf_op jit(solution)/shard_map/ppermute | solution.py:20
  47.2 41.5 %all-to-all-start = ((f32[32,16,512]{2,1,0:T(8,128)}), f32[32,16,512]{2,1,0:T(8,128)}, u32[]{:S(2)}, u32[]{:S(2)}) async-start(f32[32,16,512]{2,1,0:T(8,128)} %get-tuple-element.109), calls=%async_computation | async-start | bytes 2097152 | tf_op jit(solution)/shard_map/all_to_all | solution.py:378
  57.5 72.3 %all-gather.2.cloned.1.call-start = ((), (), s32[]{:S(2)}) async-start(), calls=%async_computation.4 | async-start | bytes 2129920 | tf_op jit(solution)/shard_map/all_gather | solution.py:376
  60.6 11.0 %collective-permute-start.5 = (f32[2,64,384]{2,1,0:T(8,128)}, f32[2,64,384]{2,1,0:T(8,128)}, u32[]{:S(2)}, u32[]{:S(2)}) collective-permute-start(f32[2,64,384]{2,1,0:T(8,128)} %get-tuple-element.113), channel_id=1, source_target_pairs={{0,2},{1,3},{2,4},{3,5},{4,6},{5,7},{6,0},{7,1},{8,10},{9,11},{10,... | collective-permute-start | bytes 589832 | tf_op jit(solution)/shard_map/ppermute | solution.py:20
  61.6 11.8 %collective-permute-start.6 = (f32[2,64,384]{2,1,0:T(8,128)}, f32[2,64,384]{2,1,0:T(8,128)}, u32[]{:S(2)}, u32[]{:S(2)}) collective-permute-start(f32[2,64,384]{2,1,0:T(8,128)} %get-tuple-element.114), channel_id=1, source_target_pairs={{0,3},{1,4},{2,5},{3,6},{4,7},{5,0},{6,1},{7,2},{8,11},{9,12},{10,... | collective-permute-start | bytes 589832 | tf_op jit(solution)/shard_map/ppermute | solution.py:20
  63.0 19.3 %collective-permute-start.7 = (f32[2,64,384]{2,1,0:T(8,128)}, f32[2,64,384]{2,1,0:T(8,128)}, u32[]{:S(2)}, u32[]{:S(2)}) collective-permute-start(f32[2,64,384]{2,1,0:T(8,128)} %get-tuple-element.115), channel_id=1, source_target_pairs={{0,4},{1,5},{2,6},{3,7},{4,0},{5,1},{6,2},{7,3},{8,12},{9,13},{10,... | collective-permute-start | bytes 589832 | tf_op jit(solution)/shard_map/ppermute | solution.py:20
  63.9 20.3 %collective-permute-start.8 = (f32[2,64,384]{2,1,0:T(8,128)}, f32[2,64,384]{2,1,0:T(8,128)}, u32[]{:S(2)}, u32[]{:S(2)}) collective-permute-start(f32[2,64,384]{2,1,0:T(8,128)} %get-tuple-element.116), channel_id=1, source_target_pairs={{0,5},{1,6},{2,7},{3,0},{4,1},{5,2},{6,3},{7,4},{8,13},{9,14},{10,... | collective-permute-start | bytes 589832 | tf_op jit(solution)/shard_map/ppermute | solution.py:20
  66.1 19.7 %collective-permute-start.9 = (f32[2,64,384]{2,1,0:T(8,128)}, f32[2,64,384]{2,1,0:T(8,128)}, u32[]{:S(2)}, u32[]{:S(2)}) collective-permute-start(f32[2,64,384]{2,1,0:T(8,128)} %get-tuple-element.117), channel_id=1, source_target_pairs={{0,6},{1,7},{2,0},{3,1},{4,2},{5,3},{6,4},{7,5},{8,14},{9,15},{10,... | collective-permute-start | bytes 589832 | tf_op jit(solution)/shard_map/ppermute | solution.py:20
  71.5 17.1 %collective-permute-start.10 = (f32[2,64,384]{2,1,0:T(8,128)}, f32[2,64,384]{2,1,0:T(8,128)}, u32[]{:S(2)}, u32[]{:S(2)}) collective-permute-start(f32[2,64,384]{2,1,0:T(8,128)} %get-tuple-element.118), channel_id=1, source_target_pairs={{0,7},{1,0},{2,1},{3,2},{4,3},{5,4},{6,5},{7,6},{8,15},{9,8},{10,9... | collective-permute-start | bytes 589832 | tf_op jit(solution)/shard_map/ppermute | solution.py:20
  88.7 18.6 %all-to-all-start.1 = ((f32[8,4,16,512]{3,2,1,0:T(8,128)}), f32[8,4,16,512]{3,2,1,0:T(8,128)}, u32[]{:S(2)}, u32[]{:S(2)}) async-start(f32[8,4,16,512]{3,2,1,0:T(8,128)} %bitcast.6), calls=%async_computation.1 | async-start | bytes 2097152 | tf_op jit(solution)/shard_map/all_to_all | solution.py:387
  112.4 20.2 %all-to-all-start.2 = ((f32[8,4,16,512]{3,2,1,0:T(8,128)}), f32[8,4,16,512]{3,2,1,0:T(8,128)}, u32[]{:S(2)}, u32[]{:S(2)}) async-start(f32[8,4,16,512]{3,2,1,0:T(8,128)} %shard_map.107), calls=%async_computation.2 | async-start | bytes 2097152 | tf_op jit(solution)/shard_map/all_to_all | solution.py:398
  132.6 45.0 %all-to-all-start.3 = ((f32[32,16,512]{2,1,0:T(8,128)}), f32[32,16,512]{2,1,0:T(8,128)}, u32[]{:S(2)}, u32[]{:S(2)}) async-start(f32[32,16,512]{2,1,0:T(8,128)} %bitcast.7), calls=%async_computation.3 | async-start | bytes 2097152 | tf_op jit(solution)/shard_map/all_to_all | solution.py:408
  142.0 35.6 %collective-permute-start.14 = (f32[64,6656]{1,0:T(8,128)}, f32[64,6656]{1,0:T(8,128)}, u32[]{:S(2)}, u32[]{:S(2)}) collective-permute-start(f32[64,6656]{1,0:T(8,128)} %all-gather.2.cloned.1.call-done.refs_1_), channel_id=1, source_target_pairs={{0,1},{1,0},{2,3},{3,2},{4,5},{5,4},{6,7},{7,6},{8,9},{9,8},{10,11... | collective-permute-start | bytes 5111816 | tf_op jit(solution)/shard_map/ppermute | solution.py:407
  143.5 15.4 %collective-permute-start.16 = (f32[136,512]{1,0:T(8,128)}, f32[136,512]{1,0:T(8,128)}, u32[]{:S(2)}, u32[]{:S(2)}) collective-permute-start(f32[136,512]{1,0:T(8,128)} %get-tuple-element.146), channel_id=1, source_target_pairs={{0,2},{1,3},{2,4},{3,5},{4,6},{5,7},{6,0},{7,1},{8,10},{9,11},{10,... | collective-permute-start | bytes 835592 | tf_op jit(solution)/shard_map/ppermute | solution.py:20
  143.5 27.7 %collective-permute-start.17 = (f32[136,512]{1,0:T(8,128)}, f32[136,512]{1,0:T(8,128)}, u32[]{:S(2)}, u32[]{:S(2)}) collective-permute-start(f32[136,512]{1,0:T(8,128)} %get-tuple-element.147), channel_id=1, source_target_pairs={{0,3},{1,4},{2,5},{3,6},{4,7},{5,0},{6,1},{7,2},{8,11},{9,12},{10,... | collective-permute-start | bytes 835592 | tf_op jit(solution)/shard_map/ppermute | solution.py:20
  146.0 25.3 %collective-permute-start.18 = (f32[136,512]{1,0:T(8,128)}, f32[136,512]{1,0:T(8,128)}, u32[]{:S(2)}, u32[]{:S(2)}) collective-permute-start(f32[136,512]{1,0:T(8,128)} %get-tuple-element.148), channel_id=1, source_target_pairs={{0,4},{1,5},{2,6},{3,7},{4,0},{5,1},{6,2},{7,3},{8,12},{9,13},{10,... | collective-permute-start | bytes 835592 | tf_op jit(solution)/shard_map/ppermute | solution.py:20
  149.2 22.1 %collective-permute-start.19 = (f32[136,512]{1,0:T(8,128)}, f32[136,512]{1,0:T(8,128)}, u32[]{:S(2)}, u32[]{:S(2)}) collective-permute-start(f32[136,512]{1,0:T(8,128)} %get-tuple-element.149), channel_id=1, source_target_pairs={{0,5},{1,6},{2,7},{3,0},{4,1},{5,2},{6,3},{7,4},{8,13},{9,14},{10,... | collective-permute-start | bytes 835592 | tf_op jit(solution)/shard_map/ppermute | solution.py:20
  158.9 12.6 %collective-permute-start.20 = (f32[136,512]{1,0:T(8,128)}, f32[136,512]{1,0:T(8,128)}, u32[]{:S(2)}, u32[]{:S(2)}) collective-permute-start(f32[136,512]{1,0:T(8,128)} %get-tuple-element.150), channel_id=1, source_target_pairs={{0,6},{1,7},{2,0},{3,1},{4,2},{5,3},{6,4},{7,5},{8,14},{9,15},{10,... | collective-permute-start | bytes 835592 | tf_op jit(solution)/shard_map/ppermute | solution.py:20
  181.1 13.3 %collective-permute-start.23 = (f32[16,6656]{1,0:T(8,128)}, f32[16,6656]{1,0:T(8,128)S(1)}, u32[]{:S(2)}, u32[]{:S(2)}) collective-permute-start(f32[16,6656]{1,0:T(8,128)} %shard_map.109.refs_1_), channel_id=1, source_target_pairs={{0,4},{1,5},{2,6},{3,7},{4,0},{5,1},{6,2},{7,3},{8,12},{9,13},{10,... | collective-permute-start | bytes 1277960 | tf_op jit(solution)/shard_map/ppermute | solution.py:20
  181.2 16.4 %collective-permute-start.24 = (f32[16,6656]{1,0:T(8,128)}, f32[16,6656]{1,0:T(8,128)S(1)}, u32[]{:S(2)}, u32[]{:S(2)}) collective-permute-start(f32[16,6656]{1,0:T(8,128)} %shard_map.109.refs_1_), channel_id=1, source_target_pairs={{0,6},{1,7},{2,0},{3,1},{4,2},{5,3},{6,4},{7,5},{8,14},{9,15},{10,... | collective-permute-start | bytes 1277960 | tf_op jit(solution)/shard_map/ppermute | solution.py:20
  181.3 17.8 %collective-permute-start.22 = (f32[16,6656]{1,0:T(8,128)}, f32[16,6656]{1,0:T(8,128)S(1)}, u32[]{:S(2)}, u32[]{:S(2)}) collective-permute-start(f32[16,6656]{1,0:T(8,128)} %shard_map.109.refs_1_), channel_id=1, source_target_pairs={{0,2},{1,3},{2,4},{3,5},{4,6},{5,7},{6,0},{7,1},{8,10},{9,11},{10,... | collective-permute-start | bytes 1277960 | tf_op jit(solution)/shard_map/ppermute | solution.py:20
  182.7 17.6 %collective-permute-start.25 = (f32[16,6656]{1,0:T(8,128)}, f32[16,6656]{1,0:T(8,128)S(1)}, u32[]{:S(2)}, u32[]{:S(2)}) collective-permute-start(f32[16,6656]{1,0:T(8,128)} %shard_map.109.refs_1_), channel_id=1, source_target_pairs={{0,1},{1,0},{2,3},{3,2},{4,5},{5,4},{6,7},{7,6},{8,9},{9,8},{10,11... | collective-permute-start | bytes 1277960 | tf_op jit(solution)/shard_map/ppermute | solution.py:430
  (23 other events, 147.0 us)
Sparse Core Ops, SparseCore 0:
  60.2 35.3 all-gather.1

commit v6 on v4

--- a/solution.py
+++ b/solution.py
@@ -144,27 +144,77 @@
         )
 
 
-def direction_kernel(ids, owner_cols, returned, *refs):
-    grams = refs[:8]
-    direction, norms = refs[8:]
+def direction_kernel(ids, owner_cols, returned, direction):
     row = ids[1]
     width = returned.shape[-1]
-    total = grams[0][...]
-    for k in range(1, 8):
-        total = total + grams[k][...]
+    for o in range(returned.shape[0]):
+        col = owner_cols[row, o]
+
+        @pl.when(col >= 0)
+        def _():
+            start = pl.multiple_of(col * width, width)
+            direction[:, pl.ds(start, width)] = returned[o]
+
+
+def place_kernel(ids, *refs):
+    pieces, grams, direction = refs[:8], refs[8:16], refs[16]
+    held, tails, sems, out_sems = refs[17:]
+    chip, core = ids[0] // 2, ids[0] % 2
+    rows = pieces[0].shape[0]
+    first, count = grams[0].shape[0] - 8, 8
+    width = tails.shape[-1]
+    loads = [
+        pltpu.make_async_copy(gram.at[pl.ds(first, 8), :], tails.at[j], sems.at[j])
+        for j, gram in enumerate(grams)
+    ]
+    loads = loads + [
+        pltpu.make_async_copy(piece, held.at[j], sems.at[count + j])
+        for j, piece in enumerate(pieces)
+    ]
+    for load in loads:
+        load.start()
+    for load in loads[:count]:
+        load.wait()
+    total = tails[0]
+    for j in range(1, count):
+        total = total + tails[j]
+    norms = []
     for c in range(direction.shape[-1] // width):
         lane = (c // 8) * 128
         lanes = total[c % 8 : c % 8 + 1, lane : lane + 128]
-        norm = jnp.sqrt(jnp.sum(lanes, axis=1, keepdims=True))
-        norms[c : c + 1, :] = jnp.broadcast_to(norm, (1, 128))
-    for o in range(returned.shape[0]):
-        col = owner_cols[row, o]
-
-        @pl.when(col >= 0)
-        def _():
-            norm = norms[pl.ds(col, 1), :][:, 0:1]
-            start = pl.multiple_of(col * width, width)
-            direction[:, pl.ds(start, width)] = returned[o] * norm
+        norms.append(jnp.sqrt(jnp.sum(lanes, axis=1, keepdims=True)))
+    stores = []
+    for j in range(count):
+        loads[count + j].wait()
+        for c, norm in enumerate(norms):
+            here = slice(c * width, (c + 1) * width)
+            held[j, :, here] = held[j, :, here] * norm
+        owner = core if j < 4 else 1 - core
+        start = pl.multiple_of((lax.rem(chip - j % 4 + 4, 4) * 2 + owner) * rows, rows)
+        stores.append(
+            pltpu.make_async_copy(held.at[j], direction.at[pl.ds(start, rows), :], out_sems.at[j])
+        )
+        stores[-1].start()
+    for store in stores:
+        store.wait()
+
+
+def place(ids, pieces, grams, shape):
+    hbm = pl.BlockSpec(memory_space=pltpu.HBM)
+    ins = [*pieces, *grams]
+    return pl.pallas_call(
+        place_kernel,
+        out_shape=pltpu.HBM(shape, F32),
+        in_specs=[pl.BlockSpec(memory_space=pltpu.SMEM)] + [hbm] * len(ins),
+        out_specs=hbm,
+        scratch_shapes=[
+            pltpu.VMEM((8, *pieces[0].shape), F32),
+            pltpu.VMEM((8, 8, grams[0].shape[1]), F32),
+            pltpu.SemaphoreType.DMA((16,)),
+            pltpu.SemaphoreType.DMA((8,)),
+        ],
+        compiler_params=PARAMS,
+    )(ids, *[pltpu.with_memory_space_constraint(x, pltpu.HBM) for x in ins])
 
 
 def staged(kernel, cuts, n_small, n_in, n_out, *refs):
@@ -228,15 +278,6 @@
                     ins[side].at[to, :, pl.ds(lane, 128)],
                     out.at[side, :, slice(j * 128, (j + 1) * 128)],
                 )
-
-
-def place_plan(ids, ins, outs):
-    chip, core = ids[0] // 2, ids[0] % 2
-    rows = ins[0].shape[0]
-    for j, piece in enumerate(ins):
-        owner = core if j < 4 else 1 - core
-        start = pl.multiple_of((lax.rem(chip - j % 4 + 4, 4) * 2 + owner) * rows, rows)
-        yield piece, outs[0].at[pl.ds(start, rows), :]
 
 
 def copying(plan, split_stores, n_small, n_in, n_out, *refs):
@@ -366,16 +407,8 @@
     moment_swap = lax.ppermute(moment_line, "rep", swap)
     returned = lax.all_to_all(spread.reshape(owners, rows, side), "fsdp", 0, 0, tiled=True)
     grams = [g if k == 0 else rep_shift(g, k, reps) for k, g in enumerate(grams)]
-    returned, moment_swap, *grams = barrier((returned, moment_swap, *grams))
-    tails = (2 * share, 8)
-    (part,) = call(
-        direction_kernel,
-        [strip],
-        [ids, oc],
-        [returned, *grams],
-        [pltpu.VMEM((16, 128), F32)],
-        [None] + [tails] * reps,
-    )
+    returned, moment_swap = barrier((returned, moment_swap))
+    (part,) = call(direction_kernel, [strip], [ids, oc], [returned], [])
     found = [part] + [rep_shift(part, 2 * k, reps) for k in range(1, chips)]
     last_ids, _ = barrier((ids, part))
     moment_new, left_new, right_new = call(
@@ -387,14 +420,7 @@
     )
     found[2], left_new = barrier((found[2], left_new))
     swapped = [lax.ppermute(x, "rep", swap) for x in found]
-    (direction,) = shuffle(
-        place_plan,
-        [(shard_rows, full_width)],
-        [ids],
-        found + swapped,
-        2 * chips,
-        True,
-    )
+    direction = place(ids, found + swapped, grams, (shard_rows, full_width))
     return (direction, moment_new, left_new[None, None], right_new[None, None])
 
 

time: 215 us -> 225 us (1.047)
  starting transfers between devices: 60.3 us -> 69.6 us
    ppermute x20, waiting for transfers between devices: 73.5 us -> 54.5 us  [rep_shift(): lax.ppermute(value, 'rep', [(i, (i + step) % count) for i in range(count)])]
    all_to_all x1, waiting for transfers between devices: 0.01 us -> 17 us  [shards(): lax.all_to_all(spread.reshape(owners, rows, side), 'fsdp', 0, 0, tiled=True)]
    ppermute x20, starting transfers between devices: 18.3 us -> 27.6 us  [rep_shift(): lax.ppermute(value, 'rep', [(i, (i + step) % count) for i in range(count)])]
    pallas_call x0 -> x1, Pallas kernels: none -> 3.66 us  [place(): pl.pallas_call(place_kernel, out_shape=pltpu.HBM(shape, F32), in_specs=[p...]
    pallas_call x2 -> x1, Pallas kernels: 7.35 us -> 3.96 us  [shuffle(): pl.pallas_call(functools.partial(copying, plan, split_stores, len(small),...]
  transfers between devices with their start and end apart: 34 -> 34, of which waited for: 22 -> 19; matrix products, arithmetic and copies ran while one was open for 1% -> 1% of each run, Pallas kernels for 12% -> 12%
where the time goes in v6:
time: 225 us; the launch traced here: 223 us
  waiting for transfers between devices  94.7 us (42%)
  starting transfers between devices  69.6 us (31%)
  Pallas kernels  34.9 us (16%)
  between operations  14.3 us (6%)
  local copies, waits for them, and re-layouts  5.37 us (2%)
  other arithmetic  3.81 us (2%)
    ppermute x20, waiting for transfers between devices, rep_shift(): lax.ppermute(value, 'rep', [(i, (i + step) % count) for i in range(count)])  54.5 us
    ppermute x20, starting transfers between devices, rep_shift(): lax.ppermute(value, 'rep', [(i, (i + step) % count) for i in range(count)])  27.6 us
    pallas_call x6, Pallas kernels, call(): pl.pallas_call(functools.partial(staged, kernel, cuts, len(small), len(in...  27.3 us
    all_to_all x1, waiting for transfers between devices, shards(): lax.all_to_all(spread.reshape(owners, rows, side), 'fsdp', 0, 0, tiled=True)  17 us
    all_to_all x1, starting transfers between devices, shards(): arrived = lax.all_to_all(packed, 'fsdp', 0, 0, tiled=True)  11.3 us
    all_to_all x1, waiting for transfers between devices, shards(): lax.all_to_all(arrived.reshape(block_rows, quarters, rows, side), 'rep',...  10.7 us
    all_to_all x1, starting transfers between devices, shards(): lax.all_to_all(spread.reshape(owners, rows, side), 'fsdp', 0, 0, tiled=True)  9.39 us
    all_to_all x1, starting transfers between devices, shards(): spread = lax.all_to_all(applied, 'rep', 0, 0, tiled=True)  5.01 us
  transfers between devices with their start and end apart: 34, of which 19 were waited for; matrix products, arithmetic and copies ran while one was open for 1% of the time, Pallas kernels for 12%

profile of v6, /device:TPU:1, one launch (start us, length us, event | category | flops | bytes accessed | tf_op | source)
XLA Modules:
  0.0 222.7 jit_solution(5506020114201720091)
XLA Ops:
  10.1 3.2 %collective-permute-start = (f32[4,16,6656]{2,1,0:T(8,128)}, f32[4,16,6656]{2,1,0:T(8,128)}, u32[]{:S(2)}, u32[]{:S(2)}) collective-permute-start(f32[4,16,6656]{2,1,0:T(8,128)} %dynamic-slice_bitcast_fusion), channel_id=1, source_target_pairs={{0,1},{1,0},{2,3},{3,2},{4,5},{5,4},{6,7},{7,6},{8,9},{9,8},{10,11... | collective-permute-start | bytes 5111816 | tf_op jit(solution)/shard_map/ppermute | solution.py:345
  13.4 3.6 %collective-permute-done = f32[4,16,6656]{2,1,0:T(8,128)} collective-permute-done((f32[4,16,6656]{2,1,0:T(8,128)}, f32[4,16,6656]{2,1,0:T(8,128)}, u32[]{:S(2)}, u32[]{:S(2)}) %collective-permute-start) | collective-permute-done | bytes 1703968 | tf_op jit(solution)/shard_map/ppermute | solution.py:345
  22.8 4.0 %shard_map.102 = (f32[2,64,384]{2,1,0:T(8,128)}, f32[2,64,384]{2,1,0:T(8,128)}, f32[2,64,384]{2,1,0:T(8,128)}, f32[2,64,384]{2,1,0:T(8,128)}, f32[2,64,384]{2,1,...) custom-call(s32[2]{0:T(128)S(1)} %pad_add_fusion.refs_0_.ids, ...), custom_call_target="tpu_custom_call" | custom-call | tf_op jit(solution)/shard_map/pallas_call | solution.py:314
  26.8 4.6 %collective-permute-done.3.refs_5_ = f32[16,6656]{1,0:T(8,128)} collective-permute-done((f32[16,6656]{1,0:T(8,128)}, f32[16,6656]{1,0:T(8,128)}, u32[]{:S(2)}, u32[]{:S(2)}) %collective-permute-start.3) | collective-permute-done | bytes 426016 | tf_op jit(solution)/shard_map/ppermute | solution.py:20
  33.4 10.1 %collective-permute-done.1.refs_3_ = f32[16,6656]{1,0:T(8,128)} collective-permute-done((f32[16,6656]{1,0:T(8,128)}, f32[16,6656]{1,0:T(8,128)}, u32[]{:S(2)}, u32[]{:S(2)}) %collective-permute-start.1) | collective-permute-done | bytes 426016 | tf_op jit(solution)/shard_map/ppermute | solution.py:20
  43.5 3.7 %shard_map.103 = (f32[16,6656]{1,0:T(8,128)}, f32[8,512]{1,0:T(8,128)}, f32[32,16,512]{2,1,0:T(8,128)}) custom-call(s32[2]{0:T(128)S(1)} %pad_add_fusion.refs_0_.ids, s32[8,32]{1,0:T(8,128)S(1)} %bitcast.30, f32[16,6656]{1,0:T(8,128)} %get-tuple-element.147.refs_2_, f32[16,6656]{1,0:T(8,128)} %collective-permute-done.1.refs_3_, ...), custom_call_target="tpu_custom_call" | custom-call | tf_op jit(solution)/shard_map/pallas_call | solution.py:260
  47.2 11.3 %all-to-all-start = ((f32[32,16,512]{2,1,0:T(8,128)}), f32[32,16,512]{2,1,0:T(8,128)}, u32[]{:S(2)}, u32[]{:S(2)}) async-start(f32[32,16,512]{2,1,0:T(8,128)} %get-tuple-element.93), calls=%async_computation | async-start | bytes 2097152 | tf_op jit(solution)/shard_map/all_to_all | solution.py:378
  67.0 11.7 %collective-permute-done.5.refs_3_ = f32[2,64,384]{2,1,0:T(8,128)} collective-permute-done((f32[2,64,384]{2,1,0:T(8,128)}, f32[2,64,384]{2,1,0:T(8,128)}, u32[]{:S(2)}, u32[]{:S(2)}) %collective-permute-start.5) | collective-permute-done | bytes 196640 | tf_op jit(solution)/shard_map/ppermute | solution.py:20
  78.8 3.5 %collective-permute-done.6.refs_4_ = f32[2,64,384]{2,1,0:T(8,128)} collective-permute-done((f32[2,64,384]{2,1,0:T(8,128)}, f32[2,64,384]{2,1,0:T(8,128)}, u32[]{:S(2)}, u32[]{:S(2)}) %collective-permute-start.6) | collective-permute-done | bytes 196640 | tf_op jit(solution)/shard_map/ppermute | solution.py:20
  83.3 4.6 %collective-permute-done.9.refs_7_ = f32[2,64,384]{2,1,0:T(8,128)} collective-permute-done((f32[2,64,384]{2,1,0:T(8,128)}, f32[2,64,384]{2,1,0:T(8,128)}, u32[]{:S(2)}, u32[]{:S(2)}) %collective-permute-start.9) | collective-permute-done | bytes 196640 | tf_op jit(solution)/shard_map/ppermute | solution.py:20
  89.7 4.2 %all-to-all-start.1 = ((f32[8,4,16,512]{3,2,1,0:T(8,128)}), f32[8,4,16,512]{3,2,1,0:T(8,128)}, u32[]{:S(2)}, u32[]{:S(2)}) async-start(f32[8,4,16,512]{3,2,1,0:T(8,128)} %bitcast.15), calls=%async_computation.1 | async-start | bytes 2097152 | tf_op jit(solution)/shard_map/all_to_all | solution.py:387
  93.9 3.9 %shard_map.104 = (bf16[512,512]{1,0:T(8,128)(2,1)}, bf16[512,512]{1,0:T(8,128)(2,1)}, bf16[512,512]{1,0:T(8,128)(2,1)}, bf16[512,512]{1,0:T(8,128)(2,1)}) custom-call(s32[2]{0:T(128)S(1)} %pad_add_fusion.refs_0_.ids, f32[2,64,384]{2,1,0:T(8,128)} %get-tuple-element.104.refs_1_, f32[2,64,384]{2,1,0:T(8,128)} %collective-permute-done.4.refs_2_, ...), custom_call_target="tpu_custom_call" | custom-call | tf_op jit(solution)/shard_map/pallas_call | solution.py:260
  97.8 10.7 %all-to-all-done.1.refs_0_.refs_1_ = f32[8,4,16,512]{3,2,1,0:T(8,128)} async-done(((f32[8,4,16,512]{3,2,1,0:T(8,128)}), f32[8,4,16,512]{3,2,1,0:T(8,128)}, u32[]{:S(2)}, u32[]{:S(2)}) %all-to-all-start.1) | async-done | bytes 1048608 | tf_op jit(solution)/shard_map/all_to_all | solution.py:387
  108.5 5.0 %shard_map.105 = f32[8,4,16,512]{3,2,1,0:T(8,128)} custom-call(f32[8,4,16,512]{3,2,1,0:T(8,128)} %all-to-all-done.1.refs_0_.refs_1_, bf16[512,512]{1,0:T(8,128)(2,1)} %get-tuple-element.112.refs_1_, bf16[512,512]{1,0:T(8,128)(2,1)} %get-tuple-element.113.refs_2_, bf16[512,512]{1,0:T(8,128)(2,1)} %get-tuple-element.114.refs_3_, ...), custom_call_target="tpu_custom_call" | custom-call | tf_op jit(solution)/shard_map/pallas_call | solution.py:260
  113.6 5.0 %all-to-all-start.2 = ((f32[8,4,16,512]{3,2,1,0:T(8,128)}), f32[8,4,16,512]{3,2,1,0:T(8,128)}, u32[]{:S(2)}, u32[]{:S(2)}) async-start(f32[8,4,16,512]{3,2,1,0:T(8,128)} %shard_map.105), calls=%async_computation.2 | async-start | bytes 2097152 | tf_op jit(solution)/shard_map/all_to_all | solution.py:398
  118.6 3.2 %collective-permute-start.13 = (f32[8,512]{1,0:T(8,128)S(1)}, f32[8,512]{1,0:T(8,128)S(1)}, u32[]{:S(2)}, u32[]{:S(2)}) collective-permute-start(f32[8,512]{1,0:T(8,128)S(1)} %copy-done.11), channel_id=1, source_target_pairs={{0,24},{8,16},{16,8},{24,0},{32,56},{40,48},{48,40},{56,32},{64,88... | collective-permute-start | bytes 49160 | tf_op jit(solution)/shard_map/ppermute | solution.py:384
  126.0 5.1 %shard_map.106 = (f32[136,512]{1,0:T(8,128)}, f32[136,512]{1,0:T(8,128)}, f32[136,512]{1,0:T(8,128)}, f32[136,512]{1,0:T(8,128)}, f32[136,512]{1,0:T(8,128)}, /*...) custom-call(s32[2]{0:T(128)S(1)} %pad_add_fusion.refs_0_.ids, ...), custom_call_target="tpu_custom_call" | custom-call | tf_op jit(solution)/shard_map/pallas_call | solution.py:260
  133.8 9.4 %all-to-all-start.3 = ((f32[32,16,512]{2,1,0:T(8,128)}), f32[32,16,512]{2,1,0:T(8,128)}, u32[]{:S(2)}, u32[]{:S(2)}) async-start(f32[32,16,512]{2,1,0:T(8,128)} %bitcast.16), calls=%async_computation.3 | async-start | bytes 2097152 | tf_op jit(solution)/shard_map/all_to_all | solution.py:408
  150.8 17.0 %all-to-all-done.3.refs_2_ = f32[32,16,512]{2,1,0:T(8,128)} async-done(((f32[32,16,512]{2,1,0:T(8,128)}), f32[32,16,512]{2,1,0:T(8,128)}, u32[]{:S(2)}, u32[]{:S(2)}) %all-to-all-start.3) | async-done | bytes 1048608 | tf_op jit(solution)/shard_map/all_to_all | solution.py:408
  176.2 6.1 %collective-permute-start.23 = (f32[136,512]{1,0:T(8,128)}, f32[136,512]{1,0:T(8,128)S(1)}, u32[]{:S(2)}, u32[]{:S(2)}) collective-permute-start(f32[136,512]{1,0:T(8,128)} %get-tuple-element.138), channel_id=1, source_target_pairs={{0,7},{1,0},{2,1},{3,2},{4,3},{5,4},{6,5},{7,6},{8,15},{9,8},{10,9... | collective-permute-start | bytes 835592 | tf_op jit(solution)/shard_map/ppermute | solution.py:20
  182.3 12.8 %collective-permute-done.22.refs_11_.refs_14_ = f32[136,512]{1,0:T(8,128)S(1)} collective-permute-done((f32[136,512]{1,0:T(8,128)}, f32[136,512]{1,0:T(8,128)S(1)}, u32[]{:S(2)}, u32[]{:S(2)}) %collective-permute-start.22) | collective-permute-done | bytes 278560 | tf_op jit(solution)/shard_map/ppermute | solution.py:20
  195.1 3.3 %collective-permute-start.25 = (f32[16,6656]{1,0:T(8,128)}, f32[16,6656]{1,0:T(8,128)S(1)}, u32[]{:S(2)}, u32[]{:S(2)}) collective-permute-start(f32[16,6656]{1,0:T(8,128)} %shard_map.107.refs_0_), channel_id=1, source_target_pairs={{0,1},{1,0},{2,3},{3,2},{4,5},{5,4},{6,7},{7,6},{8,9},{9,8},{10,11... | collective-permute-start | bytes 1277960 | tf_op jit(solution)/shard_map/ppermute | solution.py:422
  201.4 6.7 %shard_map.108 = (f32[128,6656]{1,0:T(8,128)}, f32[8,64,512]{2,1,0:T(8,128)}, f32[8,64,512]{2,1,0:T(8,128)}) custom-call(s32[2]{0:T(128)S(1)} %pad_add_fusion.refs_0_.ids, f32[64,6656]{1,0:T(8,128)} %all-gather.2.cloned.1.call-done.refs_1_, f32[64,6656]{1,0:T(8,128)} %collective-permute-done.14.refs_2_, f32[8,64,512]{2,1,0:T(8,128)} %bitcast.36, ...), custom_call_target="tpu_custom_call" | custom-call | tf_op jit(solution)/shard_map/pallas_call | solution.py:260
  212.2 3.7 %shard_map.109 = f32[128,6656]{1,0:T(8,128)} custom-call(s32[2]{0:T(128)S(1)} %pad_add_fusion.refs_0_.ids, f32[16,6656]{1,0:T(8,128)} %shard_map.107.refs_0_, f32[16,6656]{1,0:T(8,128)} %copy-done.6, f32[16,6656]{1,0:T(8,128)} %copy-done.4, f32[16,6656]{1,0:T(8,128)} %copy-done.5, f32[16,6656]{1,0:T(8,128)} %copy-done.7, f32[16,6656]{1,0:T(8,128)} %copy-done.9, ...), custom_call_target="tpu_custom_call" | custom-call | tf_op jit(solution)/shard_map/pallas_call | solution.py:205
  (82 shorter events, 52.0 us)
Async XLA Ops:
  20.1 11.3 %collective-permute-start.3 = (f32[16,6656]{1,0:T(8,128)}, f32[16,6656]{1,0:T(8,128)}, u32[]{:S(2)}, u32[]{:S(2)}) collective-permute-start(f32[16,6656]{1,0:T(8,128)} %get-tuple-element.144), channel_id=1, source_target_pairs={{0,6},{1,7},{2,0},{3,1},{4,2},{5,3},{6,4},{7,5},{8,14},{9,15},{10,... | collective-permute-start | bytes 1277960 | tf_op jit(solution)/shard_map/ppermute | solution.py:20
  20.8 12.6 %collective-permute-start.2 = (f32[16,6656]{1,0:T(8,128)}, f32[16,6656]{1,0:T(8,128)}, u32[]{:S(2)}, u32[]{:S(2)}) collective-permute-start(f32[16,6656]{1,0:T(8,128)} %get-tuple-element.145), channel_id=1, source_target_pairs={{0,4},{1,5},{2,6},{3,7},{4,0},{5,1},{6,2},{7,3},{8,12},{9,13},{10,... | collective-permute-start | bytes 1277960 | tf_op jit(solution)/shard_map/ppermute | solution.py:20
  21.3 22.2 %collective-permute-start.1 = (f32[16,6656]{1,0:T(8,128)}, f32[16,6656]{1,0:T(8,128)}, u32[]{:S(2)}, u32[]{:S(2)}) collective-permute-start(f32[16,6656]{1,0:T(8,128)} %get-tuple-element.146), channel_id=1, source_target_pairs={{0,2},{1,3},{2,4},{3,5},{4,6},{5,7},{6,0},{7,1},{8,10},{9,11},{10,... | collective-permute-start | bytes 1277960 | tf_op jit(solution)/shard_map/ppermute | solution.py:20
  47.2 42.5 %all-to-all-start = ((f32[32,16,512]{2,1,0:T(8,128)}), f32[32,16,512]{2,1,0:T(8,128)}, u32[]{:S(2)}, u32[]{:S(2)}) async-start(f32[32,16,512]{2,1,0:T(8,128)} %get-tuple-element.93), calls=%async_computation | async-start | bytes 2097152 | tf_op jit(solution)/shard_map/all_to_all | solution.py:378
  58.5 72.5 %all-gather.2.cloned.1.call-start = ((), (), s32[]{:S(2)}) async-start(), calls=%async_computation.4 | async-start | bytes 2129920 | tf_op jit(solution)/shard_map/all_gather | solution.py:376
  59.3 19.5 %collective-permute-start.5 = (f32[2,64,384]{2,1,0:T(8,128)}, f32[2,64,384]{2,1,0:T(8,128)}, u32[]{:S(2)}, u32[]{:S(2)}) collective-permute-start(f32[2,64,384]{2,1,0:T(8,128)} %get-tuple-element.97), channel_id=1, source_target_pairs={{0,2},{1,3},{2,4},{3,5},{4,6},{5,7},{6,0},{7,1},{8,10},{9,11},{10,... | collective-permute-start | bytes 589832 | tf_op jit(solution)/shard_map/ppermute | solution.py:20
  60.2 22.1 %collective-permute-start.6 = (f32[2,64,384]{2,1,0:T(8,128)}, f32[2,64,384]{2,1,0:T(8,128)}, u32[]{:S(2)}, u32[]{:S(2)}) collective-permute-start(f32[2,64,384]{2,1,0:T(8,128)} %get-tuple-element.98), channel_id=1, source_target_pairs={{0,3},{1,4},{2,5},{3,6},{4,7},{5,0},{6,1},{7,2},{8,11},{9,12},{10,... | collective-permute-start | bytes 589832 | tf_op jit(solution)/shard_map/ppermute | solution.py:20
  61.8 20.4 %collective-permute-start.7 = (f32[2,64,384]{2,1,0:T(8,128)}, f32[2,64,384]{2,1,0:T(8,128)}, u32[]{:S(2)}, u32[]{:S(2)}) collective-permute-start(f32[2,64,384]{2,1,0:T(8,128)} %get-tuple-element.99), channel_id=1, source_target_pairs={{0,4},{1,5},{2,6},{3,7},{4,0},{5,1},{6,2},{7,3},{8,12},{9,13},{10,... | collective-permute-start | bytes 589832 | tf_op jit(solution)/shard_map/ppermute | solution.py:20
  63.8 19.5 %collective-permute-start.8 = (f32[2,64,384]{2,1,0:T(8,128)}, f32[2,64,384]{2,1,0:T(8,128)}, u32[]{:S(2)}, u32[]{:S(2)}) collective-permute-start(f32[2,64,384]{2,1,0:T(8,128)} %get-tuple-element.100), channel_id=1, source_target_pairs={{0,5},{1,6},{2,7},{3,0},{4,1},{5,2},{6,3},{7,4},{8,13},{9,14},{10,... | collective-permute-start | bytes 589832 | tf_op jit(solution)/shard_map/ppermute | solution.py:20
  66.4 21.5 %collective-permute-start.9 = (f32[2,64,384]{2,1,0:T(8,128)}, f32[2,64,384]{2,1,0:T(8,128)}, u32[]{:S(2)}, u32[]{:S(2)}) collective-permute-start(f32[2,64,384]{2,1,0:T(8,128)} %get-tuple-element.101), channel_id=1, source_target_pairs={{0,6},{1,7},{2,0},{3,1},{4,2},{5,3},{6,4},{7,5},{8,14},{9,15},{10,... | collective-permute-start | bytes 589832 | tf_op jit(solution)/shard_map/ppermute | solution.py:20
  89.7 18.8 %all-to-all-start.1 = ((f32[8,4,16,512]{3,2,1,0:T(8,128)}), f32[8,4,16,512]{3,2,1,0:T(8,128)}, u32[]{:S(2)}, u32[]{:S(2)}) async-start(f32[8,4,16,512]{3,2,1,0:T(8,128)} %bitcast.15), calls=%async_computation.1 | async-start | bytes 2097152 | tf_op jit(solution)/shard_map/all_to_all | solution.py:387
  113.6 20.2 %all-to-all-start.2 = ((f32[8,4,16,512]{3,2,1,0:T(8,128)}), f32[8,4,16,512]{3,2,1,0:T(8,128)}, u32[]{:S(2)}, u32[]{:S(2)}) async-start(f32[8,4,16,512]{3,2,1,0:T(8,128)} %shard_map.105), calls=%async_computation.2 | async-start | bytes 2097152 | tf_op jit(solution)/shard_map/all_to_all | solution.py:398
  133.8 34.1 %all-to-all-start.3 = ((f32[32,16,512]{2,1,0:T(8,128)}), f32[32,16,512]{2,1,0:T(8,128)}, u32[]{:S(2)}, u32[]{:S(2)}) async-start(f32[32,16,512]{2,1,0:T(8,128)} %bitcast.16), calls=%async_computation.3 | async-start | bytes 2097152 | tf_op jit(solution)/shard_map/all_to_all | solution.py:408
  144.4 26.3 %collective-permute-start.17 = (f32[136,512]{1,0:T(8,128)}, f32[136,512]{1,0:T(8,128)}, u32[]{:S(2)}, u32[]{:S(2)}) collective-permute-start(f32[136,512]{1,0:T(8,128)} %get-tuple-element.132), channel_id=1, source_target_pairs={{0,1},{1,2},{2,3},{3,4},{4,5},{5,6},{6,7},{7,0},{8,9},{9,10},{10,1... | collective-permute-start | bytes 835592 | tf_op jit(solution)/shard_map/ppermute | solution.py:20
  144.6 26.4 %collective-permute-start.18 = (f32[136,512]{1,0:T(8,128)}, f32[136,512]{1,0:T(8,128)}, u32[]{:S(2)}, u32[]{:S(2)}) collective-permute-start(f32[136,512]{1,0:T(8,128)} %get-tuple-element.133), channel_id=1, source_target_pairs={{0,2},{1,3},{2,4},{3,5},{4,6},{5,7},{6,0},{7,1},{8,10},{9,11},{10,... | collective-permute-start | bytes 835592 | tf_op jit(solution)/shard_map/ppermute | solution.py:20
  144.7 28.8 %collective-permute-start.19 = (f32[136,512]{1,0:T(8,128)}, f32[136,512]{1,0:T(8,128)}, u32[]{:S(2)}, u32[]{:S(2)}) collective-permute-start(f32[136,512]{1,0:T(8,128)} %get-tuple-element.134), channel_id=1, source_target_pairs={{0,3},{1,4},{2,5},{3,6},{4,7},{5,0},{6,1},{7,2},{8,11},{9,12},{10,... | collective-permute-start | bytes 835592 | tf_op jit(solution)/shard_map/ppermute | solution.py:20
  147.2 26.3 %collective-permute-start.20 = (f32[136,512]{1,0:T(8,128)}, f32[136,512]{1,0:T(8,128)}, u32[]{:S(2)}, u32[]{:S(2)}) collective-permute-start(f32[136,512]{1,0:T(8,128)} %get-tuple-element.135), channel_id=1, source_target_pairs={{0,4},{1,5},{2,6},{3,7},{4,0},{5,1},{6,2},{7,3},{8,12},{9,13},{10,... | collective-permute-start | bytes 835592 | tf_op jit(solution)/shard_map/ppermute | solution.py:20
  148.4 27.8 %collective-permute-start.21 = (f32[136,512]{1,0:T(8,128)}, f32[136,512]{1,0:T(8,128)}, u32[]{:S(2)}, u32[]{:S(2)}) collective-permute-start(f32[136,512]{1,0:T(8,128)} %get-tuple-element.136), channel_id=1, source_target_pairs={{0,5},{1,6},{2,7},{3,0},{4,1},{5,2},{6,3},{7,4},{8,13},{9,14},{10,... | collective-permute-start | bytes 835592 | tf_op jit(solution)/shard_map/ppermute | solution.py:20
  170.7 37.4 %collective-permute-start.16 = (f32[16,6656]{1,0:T(8,128)}, f32[16,6656]{1,0:T(8,128)S(1)}, u32[]{:S(2)}, u32[]{:S(2)}) collective-permute-start(f32[16,6656]{1,0:T(8,128)} %shard_map.107.refs_0_), channel_id=1, source_target_pairs={{0,4},{1,5},{2,6},{3,7},{4,0},{5,1},{6,2},{7,3},{8,12},{9,13},{10,... | collective-permute-start | bytes 1277960 | tf_op jit(solution)/shard_map/ppermute | solution.py:20
  171.1 37.1 %collective-permute-start.24 = (f32[16,6656]{1,0:T(8,128)}, f32[16,6656]{1,0:T(8,128)S(1)}, u32[]{:S(2)}, u32[]{:S(2)}) collective-permute-start(f32[16,6656]{1,0:T(8,128)} %shard_map.107.refs_0_), channel_id=1, source_target_pairs={{0,6},{1,7},{2,0},{3,1},{4,2},{5,3},{6,4},{7,5},{8,14},{9,15},{10,... | collective-permute-start | bytes 1277960 | tf_op jit(solution)/shard_map/ppermute | solution.py:20
  173.5 34.8 %collective-permute-start.15 = (f32[16,6656]{1,0:T(8,128)}, f32[16,6656]{1,0:T(8,128)S(1)}, u32[]{:S(2)}, u32[]{:S(2)}) collective-permute-start(f32[16,6656]{1,0:T(8,128)} %shard_map.107.refs_0_), channel_id=1, source_target_pairs={{0,2},{1,3},{2,4},{3,5},{4,6},{5,7},{6,0},{7,1},{8,10},{9,11},{10,... | collective-permute-start | bytes 1277960 | tf_op jit(solution)/shard_map/ppermute | solution.py:20
  173.5 21.6 %collective-permute-start.22 = (f32[136,512]{1,0:T(8,128)}, f32[136,512]{1,0:T(8,128)S(1)}, u32[]{:S(2)}, u32[]{:S(2)}) collective-permute-start(f32[136,512]{1,0:T(8,128)} %get-tuple-element.137), channel_id=1, source_target_pairs={{0,6},{1,7},{2,0},{3,1},{4,2},{5,3},{6,4},{7,5},{8,14},{9,15},{10,... | collective-permute-start | bytes 835592 | tf_op jit(solution)/shard_map/ppermute | solution.py:20
  176.2 24.5 %collective-permute-start.23 = (f32[136,512]{1,0:T(8,128)}, f32[136,512]{1,0:T(8,128)S(1)}, u32[]{:S(2)}, u32[]{:S(2)}) collective-permute-start(f32[136,512]{1,0:T(8,128)} %get-tuple-element.138), channel_id=1, source_target_pairs={{0,7},{1,0},{2,1},{3,2},{4,3},{5,4},{6,5},{7,6},{8,15},{9,8},{10,9... | collective-permute-start | bytes 835592 | tf_op jit(solution)/shard_map/ppermute | solution.py:20
  195.1 13.8 %collective-permute-start.25 = (f32[16,6656]{1,0:T(8,128)}, f32[16,6656]{1,0:T(8,128)S(1)}, u32[]{:S(2)}, u32[]{:S(2)}) collective-permute-start(f32[16,6656]{1,0:T(8,128)} %shard_map.107.refs_0_), channel_id=1, source_target_pairs={{0,1},{1,0},{2,3},{3,2},{4,5},{5,4},{6,7},{7,6},{8,9},{9,8},{10,11... | collective-permute-start | bytes 1277960 | tf_op jit(solution)/shard_map/ppermute | solution.py:422
  (22 other events, 135.0 us)
Sparse Core Ops, SparseCore 0:
  61.2 34.7 all-gather.1

commit v7 on v4

--- a/solution.py
+++ b/solution.py
@@ -366,7 +366,7 @@
     moment_swap = lax.ppermute(moment_line, "rep", swap)
     returned = lax.all_to_all(spread.reshape(owners, rows, side), "fsdp", 0, 0, tiled=True)
     grams = [g if k == 0 else rep_shift(g, k, reps) for k, g in enumerate(grams)]
-    returned, moment_swap, *grams = barrier((returned, moment_swap, *grams))
+    returned, *grams = barrier((returned, *grams))
     tails = (2 * share, 8)
     (part,) = call(
         direction_kernel,

time: 215 us -> 212 us (0.986)
  waiting for transfers between devices: 95.8 us -> 92.1 us
    ppermute x20, waiting for transfers between devices: 73.5 us -> 68.6 us  [rep_shift(): lax.ppermute(value, 'rep', [(i, (i + step) % count) for i in range(count)])]
    ppermute x20, starting transfers between devices: 18.3 us -> 23.1 us  [rep_shift(): lax.ppermute(value, 'rep', [(i, (i + step) % count) for i in range(count)])]
    ppermute x4, starting transfers between devices: 4.07 us -> 0.66 us  [shards(): swapped = [lax.ppermute(x, 'rep', swap) for x in found]]
  transfers between devices with their start and end apart: 34 -> 34, of which waited for: 22 -> 21; matrix products, arithmetic and copies ran while one was open for 1% -> 1% of each run, Pallas kernels for 12% -> 13%
where the time goes in v7:
time: 212 us; the launch traced here: 211 us
  waiting for transfers between devices  92.1 us (43%)
  starting transfers between devices  61.4 us (29%)
  Pallas kernels  35.3 us (17%)
  between operations  14.2 us (7%)
  local copies, waits for them, and re-layouts  4.64 us (2%)
  other arithmetic  3.81 us (2%)
    ppermute x20, waiting for transfers between devices, rep_shift(): lax.ppermute(value, 'rep', [(i, (i + step) % count) for i in range(count)])  68.6 us
    pallas_call x6, Pallas kernels, call(): pl.pallas_call(functools.partial(staged, kernel, cuts, len(small), len(in...  27.9 us
    ppermute x20, starting transfers between devices, rep_shift(): lax.ppermute(value, 'rep', [(i, (i + step) % count) for i in range(count)])  23.1 us
    all_to_all x1, waiting for transfers between devices, shards(): lax.all_to_all(arrived.reshape(block_rows, quarters, rows, side), 'rep',...  11.3 us
    all_to_all x1, starting transfers between devices, shards(): arrived = lax.all_to_all(packed, 'fsdp', 0, 0, tiled=True)  10.3 us
    all_to_all x1, starting transfers between devices, shards(): lax.all_to_all(spread.reshape(owners, rows, side), 'fsdp', 0, 0, tiled=True)  9.24 us
    pallas_call x2, Pallas kernels, shuffle(): pl.pallas_call(functools.partial(copying, plan, split_stores, len(small),...  7.37 us
    all_to_all x1, starting transfers between devices, shards(): lax.all_to_all(arrived.reshape(block_rows, quarters, rows, side), 'rep',...  5.08 us
  transfers between devices with their start and end apart: 34, of which 21 were waited for; matrix products, arithmetic and copies ran while one was open for 1% of the time, Pallas kernels for 13%

profile of v7, /device:TPU:1, one launch (start us, length us, event | category | flops | bytes accessed | tf_op | source)
XLA Modules:
  0.0 211.4 jit_solution(16762676083123863748)
XLA Ops:
  10.1 3.2 %collective-permute-start = (f32[4,16,6656]{2,1,0:T(8,128)}, f32[4,16,6656]{2,1,0:T(8,128)}, u32[]{:S(2)}, u32[]{:S(2)}) collective-permute-start(f32[4,16,6656]{2,1,0:T(8,128)} %dynamic-slice_bitcast_fusion), channel_id=1, source_target_pairs={{0,1},{1,0},{2,3},{3,2},{4,5},{5,4},{6,7},{7,6},{8,9},{9,8},{10,11... | collective-permute-start | bytes 5111816 | tf_op jit(solution)/shard_map/ppermute | solution.py:304
  13.4 3.6 %collective-permute-done = f32[4,16,6656]{2,1,0:T(8,128)} collective-permute-done((f32[4,16,6656]{2,1,0:T(8,128)}, f32[4,16,6656]{2,1,0:T(8,128)}, u32[]{:S(2)}, u32[]{:S(2)}) %collective-permute-start) | collective-permute-done | bytes 1703968 | tf_op jit(solution)/shard_map/ppermute | solution.py:304
  16.9 3.1 %bitcast_add_fusion = (f32[16,6656]{1,0:T(8,128)}, f32[16,6656]{1,0:T(8,128)}, f32[16,6656]{1,0:T(8,128)}, f32[16,6656]{1,0:T(8,128)}) fusion(f32[4,16,6656]{2,1,0:T(8,128)} %collective-permute-done, s32[]{:T(128)S(6)} %select_n.83, f32[4,2,16,6656]{3,2,1,0:T(8,128)} %bitcast.33, s32[]{:T(128)S(6)} %select_n.84, s32[]{:T(128)S(6)} %select_n.74, ...), kind=kLoop, calls=%fused_computation.1 | loop fusion | flops 425984 | bytes 5111844 | tf_op jit(solution)/shard_map/add | solution.py:309
  24.0 3.9 %shard_map.102 = (f32[2,64,384]{2,1,0:T(8,128)}, f32[2,64,384]{2,1,0:T(8,128)}, f32[2,64,384]{2,1,0:T(8,128)}, f32[2,64,384]{2,1,0:T(8,128)}, f32[2,64,384]{2,1,...) custom-call(s32[2]{0:T(128)S(1)} %pad_add_fusion.refs_0_, ...), custom_call_target="tpu_custom_call" | custom-call | tf_op jit(solution)/shard_map/pallas_call | solution.py:273
  27.9 5.4 %collective-permute-done.1.refs_3_ = f32[16,6656]{1,0:T(8,128)} collective-permute-done((f32[16,6656]{1,0:T(8,128)}, f32[16,6656]{1,0:T(8,128)}, u32[]{:S(2)}, u32[]{:S(2)}) %collective-permute-start.1) | collective-permute-done | bytes 426016 | tf_op jit(solution)/shard_map/ppermute | solution.py:20
  33.4 7.7 %collective-permute-done.2.refs_4_ = f32[16,6656]{1,0:T(8,128)} collective-permute-done((f32[16,6656]{1,0:T(8,128)}, f32[16,6656]{1,0:T(8,128)}, u32[]{:S(2)}, u32[]{:S(2)}) %collective-permute-start.2) | collective-permute-done | bytes 426016 | tf_op jit(solution)/shard_map/ppermute | solution.py:20
  42.0 3.7 %shard_map.103 = (f32[16,6656]{1,0:T(8,128)}, f32[8,512]{1,0:T(8,128)}, f32[32,16,512]{2,1,0:T(8,128)}) custom-call(s32[2]{0:T(128)S(1)} %pad_add_fusion.refs_0_, s32[8,32]{1,0:T(8,128)S(1)} %bitcast.30, f32[16,6656]{1,0:T(8,128)} %get-tuple-element.161.refs_2_, f32[16,6656]{1,0:T(8,128)} %collective-permute-done.1.refs_3_, ...), custom_call_target="tpu_custom_call" | custom-call | tf_op jit(solution)/shard_map/pallas_call | solution.py:210
  45.7 10.3 %all-to-all-start = ((f32[32,16,512]{2,1,0:T(8,128)}), f32[32,16,512]{2,1,0:T(8,128)}, u32[]{:S(2)}, u32[]{:S(2)}) async-start(f32[32,16,512]{2,1,0:T(8,128)} %get-tuple-element.100), calls=%async_computation | async-start | bytes 2097152 | tf_op jit(solution)/shard_map/all_to_all | solution.py:337
  66.9 11.9 %collective-permute-done.5.refs_3_ = f32[2,64,384]{2,1,0:T(8,128)} collective-permute-done((f32[2,64,384]{2,1,0:T(8,128)}, f32[2,64,384]{2,1,0:T(8,128)}, u32[]{:S(2)}, u32[]{:S(2)}) %collective-permute-start.5) | collective-permute-done | bytes 196640 | tf_op jit(solution)/shard_map/ppermute | solution.py:20
  85.1 5.1 %all-to-all-start.1 = ((f32[8,4,16,512]{3,2,1,0:T(8,128)}), f32[8,4,16,512]{3,2,1,0:T(8,128)}, u32[]{:S(2)}, u32[]{:S(2)}) async-start(f32[8,4,16,512]{3,2,1,0:T(8,128)} %bitcast.15), calls=%async_computation.1 | async-start | bytes 2097152 | tf_op jit(solution)/shard_map/all_to_all | solution.py:346
  90.2 3.9 %shard_map.104 = (bf16[512,512]{1,0:T(8,128)(2,1)}, bf16[512,512]{1,0:T(8,128)(2,1)}, bf16[512,512]{1,0:T(8,128)(2,1)}, bf16[512,512]{1,0:T(8,128)(2,1)}) custom-call(s32[2]{0:T(128)S(1)} %pad_add_fusion.refs_0_, f32[2,64,384]{2,1,0:T(8,128)} %get-tuple-element.111.refs_1_, f32[2,64,384]{2,1,0:T(8,128)} %collective-permute-done.4.refs_2_, ...), custom_call_target="tpu_custom_call" | custom-call | tf_op jit(solution)/shard_map/pallas_call | solution.py:210
  94.1 11.3 %all-to-all-done.1.refs_0_.refs_1_ = f32[8,4,16,512]{3,2,1,0:T(8,128)} async-done(((f32[8,4,16,512]{3,2,1,0:T(8,128)}), f32[8,4,16,512]{3,2,1,0:T(8,128)}, u32[]{:S(2)}, u32[]{:S(2)}) %all-to-all-start.1) | async-done | bytes 1048608 | tf_op jit(solution)/shard_map/all_to_all | solution.py:346
  105.4 5.1 %shard_map.105 = f32[8,4,16,512]{3,2,1,0:T(8,128)} custom-call(f32[8,4,16,512]{3,2,1,0:T(8,128)} %all-to-all-done.1.refs_0_.refs_1_, bf16[512,512]{1,0:T(8,128)(2,1)} %get-tuple-element.119.refs_1_, bf16[512,512]{1,0:T(8,128)(2,1)} %get-tuple-element.120.refs_2_, bf16[512,512]{1,0:T(8,128)(2,1)} %get-tuple-element.121.refs_3_, ...), custom_call_target="tpu_custom_call" | custom-call | tf_op jit(solution)/shard_map/pallas_call | solution.py:210
  110.4 5.0 %all-to-all-start.2 = ((f32[8,4,16,512]{3,2,1,0:T(8,128)}), f32[8,4,16,512]{3,2,1,0:T(8,128)}, u32[]{:S(2)}, u32[]{:S(2)}) async-start(f32[8,4,16,512]{3,2,1,0:T(8,128)} %shard_map.105), calls=%async_computation.2 | async-start | bytes 2097152 | tf_op jit(solution)/shard_map/all_to_all | solution.py:357
  123.6 5.0 %shard_map.106 = (f32[136,512]{1,0:T(8,128)}, f32[136,512]{1,0:T(8,128)}, f32[136,512]{1,0:T(8,128)}, f32[136,512]{1,0:T(8,128)}, f32[136,512]{1,0:T(8,128)}, /*...) custom-call(s32[2]{0:T(128)S(1)} %pad_add_fusion.refs_0_, ...), custom_call_target="tpu_custom_call" | custom-call | tf_op jit(solution)/shard_map/pallas_call | solution.py:210
  130.6 9.2 %all-to-all-start.3 = ((f32[32,16,512]{2,1,0:T(8,128)}), f32[32,16,512]{2,1,0:T(8,128)}, u32[]{:S(2)}, u32[]{:S(2)}) async-start(f32[32,16,512]{2,1,0:T(8,128)} %bitcast.16), calls=%async_computation.3 | async-start | bytes 2097152 | tf_op jit(solution)/shard_map/all_to_all | solution.py:367
  150.1 6.6 %collective-permute-done.15.refs_5_.refs_7_ = f32[136,512]{1,0:T(8,128)} collective-permute-done((f32[136,512]{1,0:T(8,128)}, f32[136,512]{1,0:T(8,128)}, u32[]{:S(2)}, u32[]{:S(2)}) %collective-permute-start.15) | collective-permute-done | bytes 278560 | tf_op jit(solution)/shard_map/ppermute | solution.py:20
  156.7 12.4 %collective-permute-done.16.refs_6_.refs_8_ = f32[136,512]{1,0:T(8,128)} collective-permute-done((f32[136,512]{1,0:T(8,128)}, f32[136,512]{1,0:T(8,128)}, u32[]{:S(2)}, u32[]{:S(2)}) %collective-permute-start.16) | collective-permute-done | bytes 278560 | tf_op jit(solution)/shard_map/ppermute | solution.py:20
  169.4 6.1 %collective-permute-done.20.refs_10_.refs_12_ = f32[136,512]{1,0:T(8,128)} collective-permute-done((f32[136,512]{1,0:T(8,128)}, f32[136,512]{1,0:T(8,128)}, u32[]{:S(2)}, u32[]{:S(2)}) %collective-permute-start.20) | collective-permute-done | bytes 278560 | tf_op jit(solution)/shard_map/ppermute | solution.py:20
  175.4 3.5 %shard_map.107.refs_1_ = f32[16,6656]{1,0:T(8,128)} custom-call(s32[2]{0:T(128)S(1)} %pad_add_fusion.refs_0_, s32[8,32]{1,0:T(8,128)S(1)} %bitcast.31, f32[32,16,512]{2,1,0:T(8,128)} %all-to-all-done.3.refs_2_, f32[136,512]{1,0:T(8,128)} %get-tuple-element.143.refs_3_.refs_5_, f32[136,512]{1,0:T(8,128)} %collective-permute-done.14.refs_4_.refs_6_, ...), custom_call_target="tpu_custom_call" | custom-call | tf_op jit(solution)/shard_map/pallas_call | solution.py:210
  182.0 6.7 %shard_map.108 = (f32[128,6656]{1,0:T(8,128)}, f32[8,64,512]{2,1,0:T(8,128)}, f32[8,64,512]{2,1,0:T(8,128)}) custom-call(s32[2]{0:T(128)S(1)} %pad_add_fusion.refs_0_, f32[64,6656]{1,0:T(8,128)} %all-gather.2.cloned.1.call-done.refs_1_, f32[64,6656]{1,0:T(8,128)} %collective-permute-done.23.refs_2_, f32[8,64,512]{2,1,0:T(8,128)} %bitcast.36, ...), custom_call_target="tpu_custom_call" | custom-call | tf_op jit(solution)/shard_map/pallas_call | solution.py:210
  188.7 3.6 %collective-permute-done.22.refs_3_ = f32[16,6656]{1,0:T(8,128)S(1)} collective-permute-done((f32[16,6656]{1,0:T(8,128)}, f32[16,6656]{1,0:T(8,128)S(1)}, u32[]{:S(2)}, u32[]{:S(2)}) %collective-permute-start.22) | collective-permute-done | bytes 426016 | tf_op jit(solution)/shard_map/ppermute | solution.py:20
  192.2 5.5 %collective-permute-done.21.refs_2_ = f32[16,6656]{1,0:T(8,128)S(1)} collective-permute-done((f32[16,6656]{1,0:T(8,128)}, f32[16,6656]{1,0:T(8,128)S(1)}, u32[]{:S(2)}, u32[]{:S(2)}) %collective-permute-start.21) | collective-permute-done | bytes 426016 | tf_op jit(solution)/shard_map/ppermute | solution.py:20
  201.1 3.4 %shard_map.109 = f32[128,6656]{1,0:T(8,128)} custom-call(s32[2]{0:T(128)S(1)} %pad_add_fusion.refs_0_, f32[16,6656]{1,0:T(8,128)} %shard_map.107.refs_1_, f32[16,6656]{1,0:T(8,128)} %copy-done.3, f32[16,6656]{1,0:T(8,128)} %copy-done.2, f32[16,6656]{1,0:T(8,128)} %copy-done.4, f32[16,6656]{1,0:T(8,128)} %copy-done.5, f32[16,6656]{1,0:T(8,128)} %copy-done.7, ...), custom_call_target="tpu_custom_call" | custom-call | tf_op jit(solution)/shard_map/pallas_call | solution.py:273
  (78 shorter events, 51.9 us)
Async XLA Ops:
  20.1 13.3 %collective-permute-start.1 = (f32[16,6656]{1,0:T(8,128)}, f32[16,6656]{1,0:T(8,128)}, u32[]{:S(2)}, u32[]{:S(2)}) collective-permute-start(f32[16,6656]{1,0:T(8,128)} %get-tuple-element.160), channel_id=1, source_target_pairs={{0,2},{1,3},{2,4},{3,5},{4,6},{5,7},{6,0},{7,1},{8,10},{9,11},{10,... | collective-permute-start | bytes 1277960 | tf_op jit(solution)/shard_map/ppermute | solution.py:20
  20.1 21.0 %collective-permute-start.2 = (f32[16,6656]{1,0:T(8,128)}, f32[16,6656]{1,0:T(8,128)}, u32[]{:S(2)}, u32[]{:S(2)}) collective-permute-start(f32[16,6656]{1,0:T(8,128)} %get-tuple-element.159), channel_id=1, source_target_pairs={{0,4},{1,5},{2,6},{3,7},{4,0},{5,1},{6,2},{7,3},{8,12},{9,13},{10,... | collective-permute-start | bytes 1277960 | tf_op jit(solution)/shard_map/ppermute | solution.py:20
  22.0 20.1 %collective-permute-start.3 = (f32[16,6656]{1,0:T(8,128)}, f32[16,6656]{1,0:T(8,128)}, u32[]{:S(2)}, u32[]{:S(2)}) collective-permute-start(f32[16,6656]{1,0:T(8,128)} %get-tuple-element.158), channel_id=1, source_target_pairs={{0,6},{1,7},{2,0},{3,1},{4,2},{5,3},{6,4},{7,5},{8,14},{9,15},{10,... | collective-permute-start | bytes 1277960 | tf_op jit(solution)/shard_map/ppermute | solution.py:20
  45.7 39.3 %all-to-all-start = ((f32[32,16,512]{2,1,0:T(8,128)}), f32[32,16,512]{2,1,0:T(8,128)}, u32[]{:S(2)}, u32[]{:S(2)}) async-start(f32[32,16,512]{2,1,0:T(8,128)} %get-tuple-element.100), calls=%async_computation | async-start | bytes 2097152 | tf_op jit(solution)/shard_map/all_to_all | solution.py:337
  56.1 72.6 %all-gather.2.cloned.1.call-start = ((), (), s32[]{:S(2)}) async-start(), calls=%async_computation.4 | async-start | bytes 2129920 | tf_op jit(solution)/shard_map/all_gather | solution.py:335
  58.3 8.0 %collective-permute-start.4 = (f32[2,64,384]{2,1,0:T(8,128)}, f32[2,64,384]{2,1,0:T(8,128)}, u32[]{:S(2)}, u32[]{:S(2)}) collective-permute-start(f32[2,64,384]{2,1,0:T(8,128)} %get-tuple-element.103), channel_id=1, source_target_pairs={{0,1},{1,2},{2,3},{3,4},{4,5},{5,6},{6,7},{7,0},{8,9},{9,10},{10,1... | collective-permute-start | bytes 589832 | tf_op jit(solution)/shard_map/ppermute | solution.py:20
  59.3 19.5 %collective-permute-start.5 = (f32[2,64,384]{2,1,0:T(8,128)}, f32[2,64,384]{2,1,0:T(8,128)}, u32[]{:S(2)}, u32[]{:S(2)}) collective-permute-start(f32[2,64,384]{2,1,0:T(8,128)} %get-tuple-element.104), channel_id=1, source_target_pairs={{0,2},{1,3},{2,4},{3,5},{4,6},{5,7},{6,0},{7,1},{8,10},{9,11},{10,... | collective-permute-start | bytes 589832 | tf_op jit(solution)/shard_map/ppermute | solution.py:20
  60.3 21.4 %collective-permute-start.6 = (f32[2,64,384]{2,1,0:T(8,128)}, f32[2,64,384]{2,1,0:T(8,128)}, u32[]{:S(2)}, u32[]{:S(2)}) collective-permute-start(f32[2,64,384]{2,1,0:T(8,128)} %get-tuple-element.105), channel_id=1, source_target_pairs={{0,3},{1,4},{2,5},{3,6},{4,7},{5,0},{6,1},{7,2},{8,11},{9,12},{10,... | collective-permute-start | bytes 589832 | tf_op jit(solution)/shard_map/ppermute | solution.py:20
  62.1 19.5 %collective-permute-start.7 = (f32[2,64,384]{2,1,0:T(8,128)}, f32[2,64,384]{2,1,0:T(8,128)}, u32[]{:S(2)}, u32[]{:S(2)}) collective-permute-start(f32[2,64,384]{2,1,0:T(8,128)} %get-tuple-element.106), channel_id=1, source_target_pairs={{0,4},{1,5},{2,6},{3,7},{4,0},{5,1},{6,2},{7,3},{8,12},{9,13},{10,... | collective-permute-start | bytes 589832 | tf_op jit(solution)/shard_map/ppermute | solution.py:20
  63.6 19.6 %collective-permute-start.8 = (f32[2,64,384]{2,1,0:T(8,128)}, f32[2,64,384]{2,1,0:T(8,128)}, u32[]{:S(2)}, u32[]{:S(2)}) collective-permute-start(f32[2,64,384]{2,1,0:T(8,128)} %get-tuple-element.107), channel_id=1, source_target_pairs={{0,5},{1,6},{2,7},{3,0},{4,1},{5,2},{6,3},{7,4},{8,13},{9,14},{10,... | collective-permute-start | bytes 589832 | tf_op jit(solution)/shard_map/ppermute | solution.py:20
  66.3 18.8 %collective-permute-start.9 = (f32[2,64,384]{2,1,0:T(8,128)}, f32[2,64,384]{2,1,0:T(8,128)}, u32[]{:S(2)}, u32[]{:S(2)}) collective-permute-start(f32[2,64,384]{2,1,0:T(8,128)} %get-tuple-element.108), channel_id=1, source_target_pairs={{0,6},{1,7},{2,0},{3,1},{4,2},{5,3},{6,4},{7,5},{8,14},{9,15},{10,... | collective-permute-start | bytes 589832 | tf_op jit(solution)/shard_map/ppermute | solution.py:20
  85.1 20.3 %all-to-all-start.1 = ((f32[8,4,16,512]{3,2,1,0:T(8,128)}), f32[8,4,16,512]{3,2,1,0:T(8,128)}, u32[]{:S(2)}, u32[]{:S(2)}) async-start(f32[8,4,16,512]{3,2,1,0:T(8,128)} %bitcast.15), calls=%async_computation.1 | async-start | bytes 2097152 | tf_op jit(solution)/shard_map/all_to_all | solution.py:346
  110.4 20.2 %all-to-all-start.2 = ((f32[8,4,16,512]{3,2,1,0:T(8,128)}), f32[8,4,16,512]{3,2,1,0:T(8,128)}, u32[]{:S(2)}, u32[]{:S(2)}) async-start(f32[8,4,16,512]{3,2,1,0:T(8,128)} %shard_map.105), calls=%async_computation.2 | async-start | bytes 2097152 | tf_op jit(solution)/shard_map/all_to_all | solution.py:357
  130.6 44.8 %all-to-all-start.3 = ((f32[32,16,512]{2,1,0:T(8,128)}), f32[32,16,512]{2,1,0:T(8,128)}, u32[]{:S(2)}, u32[]{:S(2)}) async-start(f32[32,16,512]{2,1,0:T(8,128)} %bitcast.16), calls=%async_computation.3 | async-start | bytes 2097152 | tf_op jit(solution)/shard_map/all_to_all | solution.py:367
  139.9 42.1 %collective-permute-start.23 = (f32[64,6656]{1,0:T(8,128)}, f32[64,6656]{1,0:T(8,128)}, u32[]{:S(2)}, u32[]{:S(2)}) collective-permute-start(f32[64,6656]{1,0:T(8,128)} %all-gather.2.cloned.1.call-done.refs_1_), channel_id=1, source_target_pairs={{0,1},{1,0},{2,3},{3,2},{4,5},{5,4},{6,7},{7,6},{8,9},{9,8},{10,11... | collective-permute-start | bytes 5111816 | tf_op jit(solution)/shard_map/ppermute | solution.py:366
  141.3 15.4 %collective-permute-start.15 = (f32[136,512]{1,0:T(8,128)}, f32[136,512]{1,0:T(8,128)}, u32[]{:S(2)}, u32[]{:S(2)}) collective-permute-start(f32[136,512]{1,0:T(8,128)} %get-tuple-element.136), channel_id=1, source_target_pairs={{0,2},{1,3},{2,4},{3,5},{4,6},{5,7},{6,0},{7,1},{8,10},{9,11},{10,... | collective-permute-start | bytes 835592 | tf_op jit(solution)/shard_map/ppermute | solution.py:20
  141.4 27.7 %collective-permute-start.16 = (f32[136,512]{1,0:T(8,128)}, f32[136,512]{1,0:T(8,128)}, u32[]{:S(2)}, u32[]{:S(2)}) collective-permute-start(f32[136,512]{1,0:T(8,128)} %get-tuple-element.137), channel_id=1, source_target_pairs={{0,3},{1,4},{2,5},{3,6},{4,7},{5,0},{6,1},{7,2},{8,11},{9,12},{10,... | collective-permute-start | bytes 835592 | tf_op jit(solution)/shard_map/ppermute | solution.py:20
  143.9 25.3 %collective-permute-start.17 = (f32[136,512]{1,0:T(8,128)}, f32[136,512]{1,0:T(8,128)}, u32[]{:S(2)}, u32[]{:S(2)}) collective-permute-start(f32[136,512]{1,0:T(8,128)} %get-tuple-element.138), channel_id=1, source_target_pairs={{0,4},{1,5},{2,6},{3,7},{4,0},{5,1},{6,2},{7,3},{8,12},{9,13},{10,... | collective-permute-start | bytes 835592 | tf_op jit(solution)/shard_map/ppermute | solution.py:20
  147.1 22.1 %collective-permute-start.18 = (f32[136,512]{1,0:T(8,128)}, f32[136,512]{1,0:T(8,128)}, u32[]{:S(2)}, u32[]{:S(2)}) collective-permute-start(f32[136,512]{1,0:T(8,128)} %get-tuple-element.139), channel_id=1, source_target_pairs={{0,5},{1,6},{2,7},{3,0},{4,1},{5,2},{6,3},{7,4},{8,13},{9,14},{10,... | collective-permute-start | bytes 835592 | tf_op jit(solution)/shard_map/ppermute | solution.py:20
  156.7 12.6 %collective-permute-start.19 = (f32[136,512]{1,0:T(8,128)}, f32[136,512]{1,0:T(8,128)}, u32[]{:S(2)}, u32[]{:S(2)}) collective-permute-start(f32[136,512]{1,0:T(8,128)} %get-tuple-element.140), channel_id=1, source_target_pairs={{0,6},{1,7},{2,0},{3,1},{4,2},{5,3},{6,4},{7,5},{8,14},{9,15},{10,... | collective-permute-start | bytes 835592 | tf_op jit(solution)/shard_map/ppermute | solution.py:20
  178.9 13.3 %collective-permute-start.22 = (f32[16,6656]{1,0:T(8,128)}, f32[16,6656]{1,0:T(8,128)S(1)}, u32[]{:S(2)}, u32[]{:S(2)}) collective-permute-start(f32[16,6656]{1,0:T(8,128)} %shard_map.107.refs_1_), channel_id=1, source_target_pairs={{0,4},{1,5},{2,6},{3,7},{4,0},{5,1},{6,2},{7,3},{8,12},{9,13},{10,... | collective-permute-start | bytes 1277960 | tf_op jit(solution)/shard_map/ppermute | solution.py:20
  179.1 18.7 %collective-permute-start.21 = (f32[16,6656]{1,0:T(8,128)}, f32[16,6656]{1,0:T(8,128)S(1)}, u32[]{:S(2)}, u32[]{:S(2)}) collective-permute-start(f32[16,6656]{1,0:T(8,128)} %shard_map.107.refs_1_), channel_id=1, source_target_pairs={{0,2},{1,3},{2,4},{3,5},{4,6},{5,7},{6,0},{7,1},{8,10},{9,11},{10,... | collective-permute-start | bytes 1277960 | tf_op jit(solution)/shard_map/ppermute | solution.py:20
  179.1 19.1 %collective-permute-start.24 = (f32[16,6656]{1,0:T(8,128)}, f32[16,6656]{1,0:T(8,128)S(1)}, u32[]{:S(2)}, u32[]{:S(2)}) collective-permute-start(f32[16,6656]{1,0:T(8,128)} %shard_map.107.refs_1_), channel_id=1, source_target_pairs={{0,6},{1,7},{2,0},{3,1},{4,2},{5,3},{6,4},{7,5},{8,14},{9,15},{10,... | collective-permute-start | bytes 1277960 | tf_op jit(solution)/shard_map/ppermute | solution.py:20
  181.8 16.5 %collective-permute-start.25 = (f32[16,6656]{1,0:T(8,128)}, f32[16,6656]{1,0:T(8,128)S(1)}, u32[]{:S(2)}, u32[]{:S(2)}) collective-permute-start(f32[16,6656]{1,0:T(8,128)} %shard_map.107.refs_1_), channel_id=1, source_target_pairs={{0,1},{1,0},{2,3},{3,2},{4,5},{5,4},{6,7},{7,6},{8,9},{9,8},{10,11... | collective-permute-start | bytes 1277960 | tf_op jit(solution)/shard_map/ppermute | solution.py:389
  (20 other events, 131.5 us)
Sparse Core Ops, SparseCore 0:
  58.7 36.1 all-gather.1
